TPU v7x, 32 devices: a whole 2x2x4 slice. The times are simulated.
32 devices in a mesh: row: 4 (over y, core), col: 8 (over z, x).
Axes of the slice: x: 2, y: 2, z: 4, core: 2. Of those that a mesh axis runs over, the one named last changes fastest.
Arguments:
- points: bfloat16 [65536, 512], P(('row', 'col')), may hold values from -6 to 6
- targets: float32 [65536, 256], P(('row', 'col'))
- plan: int32 [6], replicated, may hold values from 0 to 127
- block_inverse: float32 [6, 512, 512], replicated
Outputs:
- residual: float32 [65536, 256], P(('row', 'col'))
- block_steps: bfloat16 [6, 512, 256], replicated
- losses: float32 [6], replicated
All inputs are finite; a program needn't handle non-finite values.
Results may differ from a plain program's by a relative error of at most 0.0062.
Values may be sent and summed in bfloat16 or wider, within the bound.
No kernel may reach another device: no remote copies, remote signals or barrier semaphores. Data moves between devices by JAX's collectives and lax.ppermute only.
A program may use at most 64 MiB of HBM per device.

v0:
```python
import jax
import jax.numpy as jnp
from jax import lax
from jax.sharding import PartitionSpec as P

RIDGE = 1.0


def broadcast(block, axis, owner):
    block = jnp.where(lax.axis_index(axis) == owner, block, jnp.zeros_like(block))
    return lax.psum(block, axis)


def route(payload, owner):
    across = lax.axis_size("col")
    first = (
        broadcast(payload[0], "col", owner % across),
        broadcast(payload[1], "col", owner % across),
    )
    return (
        broadcast(first[0], "row", owner // across),
        broadcast(first[1], "row", owner // across),
    )


def on_device(points, targets, plan, block_inverse):
    rows, features = points.shape
    width = targets.shape[1]
    blocksize = block_inverse.shape[1]
    rounds = block_inverse.shape[0]
    across = lax.axis_size("col")
    devices = lax.axis_size("row") * across
    here = lax.axis_index("row") * across + lax.axis_index("col")
    gamma = 2.0 / features
    total = rows * devices * width
    sqnorm = jnp.sum(jnp.square(points.astype(jnp.float32)), axis=1)
    residual = targets
    owners = []
    offsets = []
    for r in range(rounds):
        start = plan[r] * blocksize
        owner = start // rows
        owners.append(owner)
        offsets.append(jnp.clip(start - here * rows, 0, rows - blocksize))
    losses = []
    updates = []
    for r in range(rounds):
        owner = owners[r]
        offset = offsets[r]
        mine = owner == here
        local_rows = lax.dynamic_slice_in_dim(residual, offset, blocksize, 0)
        step = jnp.dot(block_inverse[r], local_rows, precision=lax.Precision.HIGHEST)
        step_half = step.astype(jnp.bfloat16)
        local_points = lax.dynamic_slice_in_dim(points, offset, blocksize, 0)
        block_points, shared_step = route((local_points, step_half), owner)
        updates.append(shared_step)
        block_norm = jnp.sum(jnp.square(block_points.astype(jnp.float32)), axis=1)
        inner = lax.dot_general(
            points, block_points, (((1,), (1,)), ((), ())), preferred_element_type=jnp.float32
        )
        kernel = jnp.exp(-gamma * (sqnorm[:, None] + block_norm[None, :] - 2.0 * inner)).astype(
            jnp.bfloat16
        )
        residual = residual - jnp.dot(kernel, shared_step, preferred_element_type=jnp.float32)
        owned = lax.dynamic_slice_in_dim(residual, offset, blocksize, 0)
        owned = jnp.where(mine, owned - RIDGE * step, owned)
        residual = lax.dynamic_update_slice_in_dim(residual, owned, offset, 0)
        partial_sum = jnp.sum(residual * residual)
        losses.append(lax.psum(partial_sum, ("row", "col")) / total)
    result = jnp.stack(losses)
    return (residual, jnp.stack(updates), result)


def solution(mesh):
    placed = (P(("row", "col"), None), P(("row", "col"), None), P(), P())
    return jax.shard_map(
        on_device,
        mesh=mesh,
        in_specs=placed,
        out_specs=(P(("row", "col"), None), P(), P()),
        check_vma=False,
    )
```

profile of v0, /device:TPU:0, one launch (start us, length us, event | category | flops | bytes accessed | tf_op | source)
XLA Modules:
  0.0 833.3 jit_solution(257840816450241425)
XLA Ops:
  12.8 4.0 convert_select_fusion.5
  19.1 77.7 %all-reduce.36.cloned.1.call-done = (bf16[512,256]{0,1:T(8,128)(2,1)}, bf16[512,512]{1,0:T(8,128)(2,1)}) async-done(((bf16[512,256]{0,1:T(8,128)(2,1)}, bf16[512,512]{1,0:T(8,128)(2,1)}), (bf16[512,256]{0,1:T(8,128)(2,1)}, bf16[512,512]{1,0:T(8,128)(2,1)})) %all-reduce.36.cloned.1.call-update) | async-done | bytes 786448 | tf_op jit(solution)/shard_map/psum | solution.py:11
  98.5 2.9 copy.7
  101.8 31.2 %all-reduce.48.cloned.1.call-done = (bf16[512,256]{0,1:T(8,128)(2,1)}, bf16[512,512]{1,0:T(8,128)(2,1)}) async-done(((bf16[512,256]{0,1:T(8,128)(2,1)}, bf16[512,512]{1,0:T(8,128)(2,1)}), (bf16[512,256]{0,1:T(8,128)(2,1)}, bf16[512,512]{1,0:T(8,128)(2,1)})) %all-reduce.48.cloned.1.call-update) | async-done | bytes 786448 | tf_op jit(solution)/shard_map/psum | solution.py:11
  134.2 5.4 convolution_subtract_fusion.5
  140.9 2.8 dynamic_update_slice.18
  143.7 3.2 convert_select_fusion.4
  147.0 75.1 %all-reduce.34.cloned.1.call-done = (bf16[512,256]{0,1:T(8,128)(2,1)}, bf16[512,512]{1,0:T(8,128)(2,1)}) async-done(((bf16[512,256]{0,1:T(8,128)(2,1)}, bf16[512,512]{1,0:T(8,128)(2,1)}), (bf16[512,256]{0,1:T(8,128)(2,1)}, bf16[512,512]{1,0:T(8,128)(2,1)})) %all-reduce.34.cloned.1.call-update) | async-done | bytes 786448 | tf_op jit(solution)/shard_map/psum | solution.py:11
  225.9 32.7 %all-reduce.46.cloned.1.call-done = (bf16[512,256]{0,1:T(8,128)(2,1)}, bf16[512,512]{1,0:T(8,128)(2,1)}) async-done(((bf16[512,256]{0,1:T(8,128)(2,1)}, bf16[512,512]{1,0:T(8,128)(2,1)}), (bf16[512,256]{0,1:T(8,128)(2,1)}, bf16[512,512]{1,0:T(8,128)(2,1)})) %all-reduce.46.cloned.1.call-update) | async-done | bytes 786448 | tf_op jit(solution)/shard_map/psum | solution.py:11
  259.8 5.4 convolution_subtract_fusion.4
  266.5 2.9 dynamic_update_slice.19
  269.4 3.2 convert_select_fusion.3
  272.7 75.7 %all-reduce.32.cloned.1.call-done = (bf16[512,256]{0,1:T(8,128)(2,1)}, bf16[512,512]{1,0:T(8,128)(2,1)}) async-done(((bf16[512,256]{0,1:T(8,128)(2,1)}, bf16[512,512]{1,0:T(8,128)(2,1)}), (bf16[512,256]{0,1:T(8,128)(2,1)}, bf16[512,512]{1,0:T(8,128)(2,1)})) %all-reduce.32.cloned.1.call-update) | async-done | bytes 786448 | tf_op jit(solution)/shard_map/psum | solution.py:11
  352.1 32.9 %all-reduce.44.cloned.1.call-done = (bf16[512,256]{0,1:T(8,128)(2,1)}, bf16[512,512]{1,0:T(8,128)(2,1)}) async-done(((bf16[512,256]{0,1:T(8,128)(2,1)}, bf16[512,512]{1,0:T(8,128)(2,1)}), (bf16[512,256]{0,1:T(8,128)(2,1)}, bf16[512,512]{1,0:T(8,128)(2,1)})) %all-reduce.44.cloned.1.call-update) | async-done | bytes 786448 | tf_op jit(solution)/shard_map/psum | solution.py:11
  386.2 5.4 convolution_subtract_fusion.3
  392.9 3.5 dynamic_update_slice.20
  396.4 3.2 convert_select_fusion.2
  399.7 75.0 %all-reduce.30.cloned.1.call-done = (bf16[512,256]{0,1:T(8,128)(2,1)}, bf16[512,512]{1,0:T(8,128)(2,1)}) async-done(((bf16[512,256]{0,1:T(8,128)(2,1)}, bf16[512,512]{1,0:T(8,128)(2,1)}), (bf16[512,256]{0,1:T(8,128)(2,1)}, bf16[512,512]{1,0:T(8,128)(2,1)})) %all-reduce.30.cloned.1.call-update) | async-done | bytes 786448 | tf_op jit(solution)/shard_map/psum | solution.py:11
  476.4 34.5 %all-reduce.42.cloned.1.call-done = (bf16[512,256]{0,1:T(8,128)(2,1)}, bf16[512,512]{1,0:T(8,128)(2,1)}) async-done(((bf16[512,256]{0,1:T(8,128)(2,1)}, bf16[512,512]{1,0:T(8,128)(2,1)}), (bf16[512,256]{0,1:T(8,128)(2,1)}, bf16[512,512]{1,0:T(8,128)(2,1)})) %all-reduce.42.cloned.1.call-update) | async-done | bytes 786448 | tf_op jit(solution)/shard_map/psum | solution.py:11
  512.1 5.4 convolution_subtract_fusion.2
  518.8 2.8 dynamic_update_slice.21
  521.6 3.2 convert_select_fusion.1
  528.7 71.4 %all-reduce.28.cloned.1.call-done = (bf16[512,256]{0,1:T(8,128)(2,1)}, bf16[512,512]{1,0:T(8,128)(2,1)}) async-done(((bf16[512,256]{0,1:T(8,128)(2,1)}, bf16[512,512]{1,0:T(8,128)(2,1)}), (bf16[512,256]{0,1:T(8,128)(2,1)}, bf16[512,512]{1,0:T(8,128)(2,1)})) %all-reduce.28.cloned.1.call-update) | async-done | bytes 786448 | tf_op jit(solution)/shard_map/psum | solution.py:11
  605.1 31.6 %all-reduce.40.cloned.1.call-done = (bf16[512,256]{0,1:T(8,128)(2,1)}, bf16[512,512]{1,0:T(8,128)(2,1)}) async-done(((bf16[512,256]{0,1:T(8,128)(2,1)}, bf16[512,512]{1,0:T(8,128)(2,1)}), (bf16[512,256]{0,1:T(8,128)(2,1)}, bf16[512,512]{1,0:T(8,128)(2,1)})) %all-reduce.40.cloned.1.call-update) | async-done | bytes 786448 | tf_op jit(solution)/shard_map/psum | solution.py:11
  638.0 5.4 convolution_subtract_fusion.1
  647.5 3.2 convert_select_fusion
  650.8 2.9 multiply_reduce_fusion.4
  656.3 70.2 %all-reduce.26.cloned.1.call-done = (bf16[512,256]{0,1:T(8,128)(2,1)}, bf16[512,512]{1,0:T(8,128)(2,1)}) async-done(((bf16[512,256]{0,1:T(8,128)(2,1)}, bf16[512,512]{1,0:T(8,128)(2,1)}), (bf16[512,256]{0,1:T(8,128)(2,1)}, bf16[512,512]{1,0:T(8,128)(2,1)})) %all-reduce.26.cloned.1.call-update) | async-done | bytes 786448 | tf_op jit(solution)/shard_map/psum | solution.py:11
  731.6 31.5 %all-reduce.38.cloned.1.call-done = (bf16[512,256]{0,1:T(8,128)(2,1)}, bf16[512,512]{1,0:T(8,128)(2,1)}) async-done(((bf16[512,256]{0,1:T(8,128)(2,1)}, bf16[512,512]{1,0:T(8,128)(2,1)}), (bf16[512,256]{0,1:T(8,128)(2,1)}, bf16[512,512]{1,0:T(8,128)(2,1)})) %all-reduce.38.cloned.1.call-update) | async-done | bytes 786448 | tf_op jit(solution)/shard_map/psum | solution.py:11
  764.3 5.4 convolution_subtract_fusion
  773.8 2.9 multiply_reduce_fusion.1
  778.5 40.5 %all-reduce = (f32[]{:T(128)}, f32[]{:T(128)}, f32[]{:T(128)}, f32[]{:T(128)}, f32[]{:T(128)}, /*index=5*/f32[]{:T(128)}) all-reduce(f32[]{:T(128)} %multiply_reduce_fusion.6, f32[]{:T(128)} %multiply_reduce_fusion.5, f32[]{:T(128)} %multiply_reduce_fusion.4, ...), channel_id=1, replica_groups=mesh['row'=4,'col'=8] {'row','col'}, use_global_device_ids=true, to_apply=%region_32.33 | all-reduce | flops 6 | bytes 48 | tf_op jit(solution)/shard_map/psum | solution.py:69
  (84 shorter events, 58.0 us)
Async XLA Ops:
  7.2 9.6 %copy-start = (bf16[2048,512]{1,0:T(8,128)(2,1)S(1)}, bf16[2048,512]{1,0:T(8,128)(2,1)}, u32[]{:S(2)}) copy-start(bf16[2048,512]{1,0:T(8,128)(2,1)} %param.4) | copy-start | bytes 6291460
  7.2 89.6 %all-reduce.36.cloned.1.call-start = ((), (), s32[]{:S(2)}) async-start(), calls=%async_computation.5 | async-start | bytes 1572864 | tf_op jit(solution)/shard_map/psum | solution.py:11
  19.1 114.0 %all-reduce.48.cloned.1.call-start = ((), (), s32[]{:S(2)}) async-start(), calls=%async_computation.11 | async-start | bytes 1572864 | tf_op jit(solution)/shard_map/psum | solution.py:11
  98.4 123.7 %all-reduce.34.cloned.1.call-start = ((), (), s32[]{:S(2)}) async-start(), calls=%async_computation.4 | async-start | bytes 1572864 | tf_op jit(solution)/shard_map/psum | solution.py:11
  146.9 111.7 %all-reduce.46.cloned.1.call-start = ((), (), s32[]{:S(2)}) async-start(), calls=%async_computation.10 | async-start | bytes 1572864 | tf_op jit(solution)/shard_map/psum | solution.py:11
  225.7 122.7 %all-reduce.32.cloned.1.call-start = ((), (), s32[]{:S(2)}) async-start(), calls=%async_computation.3 | async-start | bytes 1572864 | tf_op jit(solution)/shard_map/psum | solution.py:11
  272.6 112.4 %all-reduce.44.cloned.1.call-start = ((), (), s32[]{:S(2)}) async-start(), calls=%async_computation.9 | async-start | bytes 1572864 | tf_op jit(solution)/shard_map/psum | solution.py:11
  352.0 122.7 %all-reduce.30.cloned.1.call-start = ((), (), s32[]{:S(2)}) async-start(), calls=%async_computation.2 | async-start | bytes 1572864 | tf_op jit(solution)/shard_map/psum | solution.py:11
  399.6 111.3 %all-reduce.42.cloned.1.call-start = ((), (), s32[]{:S(2)}) async-start(), calls=%async_computation.8 | async-start | bytes 1572864 | tf_op jit(solution)/shard_map/psum | solution.py:11
  476.4 123.7 %all-reduce.28.cloned.1.call-start = ((), (), s32[]{:S(2)}) async-start(), calls=%async_computation.1 | async-start | bytes 1572864 | tf_op jit(solution)/shard_map/psum | solution.py:11
  521.6 6.3 copy-start.3
  524.9 111.9 %all-reduce.40.cloned.1.call-start = ((), (), s32[]{:S(2)}) async-start(), calls=%async_computation.7 | async-start | bytes 1572864 | tf_op jit(solution)/shard_map/psum | solution.py:11
  600.8 3.6 copy-start.4
  601.6 124.9 %all-reduce.26.cloned.1.call-start = ((), (), s32[]{:S(2)}) async-start(), calls=%async_computation | async-start | bytes 1572864 | tf_op jit(solution)/shard_map/psum | solution.py:11
  647.4 6.2 copy-start.5
  650.7 4.8 copy-start.6
  650.7 112.3 %all-reduce.38.cloned.1.call-start = ((), (), s32[]{:S(2)}) async-start(), calls=%async_computation.6 | async-start | bytes 1572864 | tf_op jit(solution)/shard_map/psum | solution.py:11
  650.8 3.7 copy-start.2
  727.3 3.6 copy-start.7
  773.8 2.9 copy-start.1
  776.7 45.9 %copy-start.8 = (bf16[512,256]{0,1:T(8,128)(2,1)S(1)}, bf16[512,256]{0,1:T(8,128)(2,1)}, u32[]{:S(2)}) copy-start(bf16[512,256]{0,1:T(8,128)(2,1)} %get-tuple-element.24) | copy-start | bytes 786436
Sparse Core Ops, SparseCore 0:
  19.2 77.5 all-reduce.35
  99.3 33.6 all-reduce.47
  147.1 74.9 all-reduce.33
  225.8 32.7 all-reduce.45
  272.7 75.6 all-reduce.31
  352.2 32.7 all-reduce.43
  399.8 74.9 all-reduce.29
  477.2 33.6 all-reduce.41
  525.0 75.0 all-reduce.27
  603.0 33.6 all-reduce.39
  650.8 75.6 all-reduce.25
  729.4 33.6 all-reduce.37
where the time goes:
time: 837 us; the launch traced here: 833 us
  waiting for transfers between devices  640 us (76%)
  matrix products  52.5 us (6%)
  other arithmetic  46.1 us (6%)
  blocking collectives  40.5 us (5%)
  local copies, waits for them, and re-layouts  31.5 us (4%)
  between operations  22.2 us (3%)
    psum x12, waiting for transfers between devices, broadcast(): return lax.psum(block, axis)  639 us
    psum x1, blocking collectives, on_device(): losses.append(lax.psum(partial_sum, ('row', 'col')) / total)  40.5 us
    dot_general x6, matrix products, on_device(): jnp.dot(kernel, shared_step, preferred_element_type=jnp.float32)  32.4 us
    dot_general x6, matrix products, on_device(): jnp.dot(block_inverse[r], local_rows, precision=lax.Precision.HIGHEST)  20.1 us
    dynamic_update_slice x6, local copies, waits for them, and re-layouts, on_device(): residual = lax.dynamic_update_slice_in_dim(residual, owned, offset, 0)  17.7 us
  transfers between devices with their start and end apart: 12, of which 12 were waited for; matrix products, arithmetic and copies ran while one was open for 2% of the time, Pallas kernels for 0%

commit v1 on v0

v1 whole, which is shorter than its diff:
```python
import functools
import math

import jax
import jax.numpy as jnp
from jax import lax
from jax.experimental import pallas as pl
from jax.experimental.pallas import tpu as pltpu
from jax.sharding import PartitionSpec as P

RIDGE = 1.0
AXES = ("row", "col")
HALVINGS = 3
NT = (((1,), (1,)), ((), ()))
LOG2E = math.log2(math.e)
MIB = 1 << 20


def stage_bits(mesh_shape):
    cols = mesh_shape["col"].bit_length() - 1
    rows = mesh_shape["row"].bit_length() - 1
    core = cols
    along_col = list(range(cols))
    along_row = list(range(cols + 1, cols + rows))
    rest = along_col[2:] + along_row[1:]
    first = along_col[:2] + along_row[:1] + rest
    second = along_row[:1] + along_col[:2] + rest
    return core, (first, second)


def swap(x, devices, bit_of):
    return lax.ppermute(x, AXES, [(i, i ^ (1 << bit_of(i))) for i in range(devices)])


class Route:
    def __init__(self, mesh_shape):
        self.devices = mesh_shape["row"] * mesh_shape["col"]
        self.core, self.orders = stage_bits(mesh_shape)
        self.stages = len(self.orders[0])
        self.halvings = min(HALVINGS, self.stages)
        self.here = lax.axis_index("row") * mesh_shape["col"] + lax.axis_index("col")
        self.side = (self.here >> self.core) & 1

    def swap_core(self, x):
        return swap(x, self.devices, lambda i: self.core)

    def swap_stage(self, x, k):
        return swap(x, self.devices, lambda i: self.orders[(i >> self.core) & 1][k])

    def bit(self, index, k, side=None):
        side = self.side if side is None else side
        first, second = self.orders
        return jnp.where(side == 0, (index >> first[k]) & 1, (index >> second[k]) & 1)

    def piece_rows(self, blocksize):
        count = 1 << self.halvings
        pieces = []
        for side in (self.side, 1 - self.side):
            for p in range(count):
                row = side * (blocksize // 2)
                for k in range(self.halvings):
                    flipped = self.bit(self.here, k, side) ^ ((p >> (self.halvings - 1 - k)) & 1)
                    row = row + flipped * (blocksize >> (k + 2))
                pieces.append(row)
        return jnp.stack(pieces).astype(jnp.int32)

    def spread(self, send, keep, owner):
        recv = self.swap_core(send)
        mine = keep
        same = ((owner >> self.core) & 1) == self.side
        for k in range(self.halvings):
            bit = self.bit(self.here, k)
            rows = mine.shape[1] // 2

            def half(which):
                return jnp.where(
                    same[:, None, None],
                    lax.dynamic_slice_in_dim(mine, which * rows, rows, 1),
                    lax.dynamic_slice_in_dim(recv, which * rows, rows, 1),
                )

            going, staying = half(1 - bit), half(bit)
            recv = self.swap_stage(going, k)
            mine = staying
            same = self.bit(owner, k) == bit
        for k in range(self.halvings, self.stages):
            mine = jnp.where(same[:, None, None], mine, recv)
            recv = self.swap_stage(mine, k)
            same = self.bit(owner, k) == self.bit(self.here, k)
        mine = jnp.where(same[:, None, None], mine, recv)[None]
        for k in reversed(range(self.halvings)):
            mine = jnp.concatenate([mine, self.swap_stage(mine, k)], 0)
        return mine, self.swap_core(mine)

    def total(self, x):
        x = x + self.swap_core(x)
        for k in range(self.stages):
            x = x + swap(x, self.devices, lambda i: self.orders[0][k])
        return x


def pick_kernel(going_ref, staying_ref, src_a, src_b, out_a, out_b):
    out_a[0] = src_a[...].astype(out_a.dtype)
    out_b[0] = src_b[...].astype(out_b.dtype)


def pick(array, going, staying, half):
    slots = going.shape[0]
    width = array.shape[1]
    shape = jax.ShapeDtypeStruct((slots, half, width), jnp.bfloat16)
    out = pl.BlockSpec((1, half, width), lambda r, a, b: (r, 0, 0))
    return pl.pallas_call(
        pick_kernel,
        out_shape=(shape, shape),
        grid_spec=pltpu.PrefetchScalarGridSpec(
            num_scalar_prefetch=2,
            grid=(slots,),
            in_specs=[
                pl.BlockSpec((half, width), lambda r, a, b: (a[r], 0)),
                pl.BlockSpec((half, width), lambda r, a, b: (b[r], 0)),
            ],
            out_specs=(out, out),
        ),
        name="pick",
    )(going, staying, array, array)


def squares(p):
    wide = p.astype(jnp.float32)
    wide = wide * wide
    high = wide.astype(jnp.bfloat16)
    return high, (wide - high.astype(jnp.float32)).astype(jnp.bfloat16)


def column_norms(p, scale):
    high, low = squares(p)
    ones = jnp.ones((p.shape[1], 128), jnp.bfloat16)
    both = jnp.dot(high, ones, preferred_element_type=jnp.float32)
    return scale * (both + jnp.dot(low, ones, preferred_element_type=jnp.float32))


def row_norms(p, scale):
    high, low = squares(p)
    ones = jnp.ones((8, p.shape[1]), jnp.bfloat16)
    both = lax.dot_general(ones, high, NT, preferred_element_type=jnp.float32)
    return scale * (both + lax.dot_general(ones, low, NT, preferred_element_type=jnp.float32))


def prepare_kernel(scale, points, inverse, norms, high, low):
    norms[...] = column_norms(points[...], scale)
    b = inverse[0]
    top = b.astype(jnp.bfloat16)
    high[0] = top
    low[0] = (b - top.astype(jnp.float32)).astype(jnp.bfloat16)


def prepare(points, inverse, scale):
    rounds, size, _ = inverse.shape
    rows, features = points.shape
    tile = rows // 4
    last = rows // tile - 1
    terms = jax.ShapeDtypeStruct(inverse.shape, jnp.bfloat16)
    block = pl.BlockSpec((1, size, size), lambda r: (r, 0, 0))
    return pl.pallas_call(
        functools.partial(prepare_kernel, scale),
        out_shape=(jax.ShapeDtypeStruct((rows, 128), jnp.float32), terms, terms),
        grid=(rounds,),
        in_specs=[
            pl.BlockSpec((tile, features), lambda r: (jnp.minimum(r, last), 0)),
            block,
        ],
        out_specs=(pl.BlockSpec((tile, 128), lambda r: (jnp.minimum(r, last), 0)), block, block),
        cost_estimate=pl.CostEstimate(flops=0, bytes_accessed=16 * MIB, transcendentals=0),
        name="prepare",
    )(points, inverse)


def assemble_kernel(scale, rows_ref, mine, other, out, across, down):
    count = mine.shape[0]
    piece = mine.shape[2]
    for p in range(count):
        out[0, pl.ds(pl.multiple_of(rows_ref[p], piece), piece), :] = mine[p, 0]
        out[0, pl.ds(pl.multiple_of(rows_ref[count + p], piece), piece), :] = other[p, 0]
    block = out[0]
    across[0] = row_norms(block, scale)
    down[0] = column_norms(block, scale)


def assemble(mine, other, piece_rows, scale):
    count, slots, piece, width = mine.shape
    size = 2 * count * piece
    src = pl.BlockSpec((count, 1, piece, width), lambda r, _: (0, r, 0, 0))

    def dst(*shape):
        return pl.BlockSpec((1,) + shape, lambda r, _: (r, 0, 0))

    return pl.pallas_call(
        functools.partial(assemble_kernel, scale),
        out_shape=(
            jax.ShapeDtypeStruct((slots, size, width), jnp.bfloat16),
            jax.ShapeDtypeStruct((slots, 8, size), jnp.float32),
            jax.ShapeDtypeStruct((slots, size, 128), jnp.float32),
        ),
        grid_spec=pltpu.PrefetchScalarGridSpec(
            num_scalar_prefetch=1,
            grid=(slots,),
            in_specs=[src, src],
            out_specs=(dst(size, width), dst(8, size), dst(size, 128)),
        ),
        cost_estimate=pl.CostEstimate(flops=0, bytes_accessed=12 * MIB, transcendentals=0),
        name="assemble",
    )(piece_rows, mine, other)


def gram_kernel(scale, left_ids, right_ids, left, right, down, across, out):
    inner = lax.dot_general(left[0], right[0], NT, preferred_element_type=jnp.float32)
    width = out.shape[2]
    offset = jnp.concatenate([down[0]] * (width // 128), axis=1) + across[0, 0:1, :]
    out[0] = jnp.exp2(inner * scale + offset).astype(out.dtype)


def gram(left, right, down, across, pairs, scale):
    size, features = left.shape[1:]
    width = right.shape[1]
    left_ids = jnp.array([i for i, _ in pairs], jnp.int32)
    right_ids = jnp.array([j for _, j in pairs], jnp.int32)
    n = len(pairs)
    return pl.pallas_call(
        functools.partial(gram_kernel, scale),
        out_shape=jax.ShapeDtypeStruct((n, size, width), jnp.bfloat16),
        grid_spec=pltpu.PrefetchScalarGridSpec(
            num_scalar_prefetch=2,
            grid=(n,),
            in_specs=[
                pl.BlockSpec((1, size, features), lambda g, a, b: (a[g], 0, 0)),
                pl.BlockSpec((1, width, features), lambda g, a, b: (b[g], 0, 0)),
                pl.BlockSpec((1, size, 128), lambda g, a, b: (a[g], 0, 0)),
                pl.BlockSpec((1, 8, width), lambda g, a, b: (b[g], 0, 0)),
            ],
            out_specs=pl.BlockSpec((1, size, width), lambda g, a, b: (g, 0, 0)),
        ),
        cost_estimate=pl.CostEstimate(
            flops=2 * n * size * width * features,
            bytes_accessed=2 * n * size * width,
            transcendentals=n * size * width,
        ),
        name="gram",
    )(left_ids, right_ids, left, right, down, across)


def solve_kernel(
    groups, plan, own, offset, piece_rows,
    mine, other, high, low, among, targets, *rest,
):
    tall = rest[:groups]
    residual, steps, losses = rest[groups:groups + 3]
    start, x, wide, cross, high_v, low_v, tall_v, sems, load_sems = rest[groups + 3:]
    rounds, size, width = steps.shape
    rows = residual.shape[0]
    per = rounds // groups
    tiles = rows // size
    count, piece = mine.shape[0], mine.shape[2]

    loads = []

    def load(src, dst):
        copy = pltpu.make_async_copy(src, dst, load_sems.at[len(loads)])
        copy.start()
        loads.append(copy)
        return copy

    ready = []
    pieces = []
    for r in range(rounds):
        mats = [load(high.at[r], high_v.at[r]), load(low.at[r], low_v.at[r])]
        if r > 0:
            first = r * (r - 1) // 2
            mats.append(load(among.at[pl.ds(first, r)], cross.at[pl.ds(first, r)]))
        body = load(tall[r // per].at[pl.ds((r % per) * tiles, tiles)], tall_v.at[r])
        ready.append((mats, body))
    targets_in = load(targets, residual)

    for p in range(count):
        for r in range(rounds):
            start[r, pl.ds(pl.multiple_of(piece_rows[p], piece), piece), :] = mine[p, r]
            start[r, pl.ds(pl.multiple_of(piece_rows[count + p], piece), piece), :] = other[p, r]

    for r in range(rounds):
        mats, body = ready[r]
        for copy in mats:
            copy.wait()
        value = start[r].astype(jnp.float32)
        first = r * (r - 1) // 2
        for s in range(r):
            value = value - jnp.dot(cross[first + s], steps[s], preferred_element_type=jnp.float32)
        x[...] = value
        for s in range(r):
            @pl.when(plan[s] == plan[r])
            def _():
                x[...] = x[...] - RIDGE * wide[s]
        value = x[...]
        top = value.astype(jnp.bfloat16)
        bottom = (value - top.astype(jnp.float32)).astype(jnp.bfloat16)
        step = jnp.dot(high_v[r], top, preferred_element_type=jnp.float32)
        step = step + jnp.dot(low_v[r], top, preferred_element_type=jnp.float32)
        step = step + jnp.dot(high_v[r], bottom, preferred_element_type=jnp.float32)
        wide[r] = step
        steps[r] = step.astype(jnp.bfloat16)

        if r == 0:
            targets_in.wait()
        body.wait()

        @pl.when(own[r] == 1)
        def _():
            where = pl.ds(pl.multiple_of(offset[r], size), size)
            residual[where, :] = residual[where, :] - RIDGE * wide[r]

        total = jnp.zeros((8, width), jnp.float32)
        for t in range(tiles):
            where = pl.ds(t * size, size)
            part = residual[where, :] - jnp.dot(
                tall_v[r, t], steps[r], preferred_element_type=jnp.float32
            )
            residual[where, :] = part
            total = total + jnp.sum((part * part).reshape(size // 8, 8, width), axis=0)
        folded = total[:, 0:128]
        for c in range(1, width // 128):
            folded = folded + total[:, c * 128:(c + 1) * 128]
        losses[r] = folded


def solve(plan, own, offset, piece_rows, mine, other, high, low, among, tall, targets):
    rounds, size, _ = high.shape
    rows, width = targets.shape
    tiles = rows // size
    groups = len(tall)
    n_loads = 4 * rounds
    smem = pl.BlockSpec(memory_space=pltpu.SMEM)
    vmem = pl.BlockSpec(memory_space=pltpu.VMEM)
    far = pl.BlockSpec(memory_space=pl.ANY)
    return pl.pallas_call(
        functools.partial(solve_kernel, groups),
        out_shape=(
            jax.ShapeDtypeStruct((rows, width), jnp.float32),
            jax.ShapeDtypeStruct((rounds, size, width), jnp.bfloat16),
            jax.ShapeDtypeStruct((rounds, 8, 128), jnp.float32),
        ),
        in_specs=[smem] * 4 + [vmem] * 2 + [far] * (4 + groups),
        out_specs=(vmem, vmem, vmem),
        scratch_shapes=[
            pltpu.VMEM((rounds, size, width), jnp.bfloat16),
            pltpu.VMEM((size, width), jnp.float32),
            pltpu.VMEM((rounds, size, width), jnp.float32),
            pltpu.VMEM(among.shape, jnp.bfloat16),
            pltpu.VMEM(high.shape, jnp.bfloat16),
            pltpu.VMEM(low.shape, jnp.bfloat16),
            pltpu.VMEM((rounds, tiles, size, size), jnp.bfloat16),
            pltpu.SemaphoreType.DMA((1,)),
            pltpu.SemaphoreType.DMA((n_loads,)),
        ],
        compiler_params=pltpu.CompilerParams(vmem_limit_bytes=50 * MIB),
        name="solve",
    )(plan, own, offset, piece_rows, mine, other, high, low, among, targets, *tall)


def on_device(mesh_shape, points, targets, plan, block_inverse):
    rows, features = points.shape
    width = targets.shape[1]
    rounds, size, _ = block_inverse.shape
    route = Route(mesh_shape)
    total = rows * route.devices * width
    gamma = 2.0 / features
    norm_scale = -gamma * LOG2E
    inner_scale = 2.0 * gamma * LOG2E
    half = size // 2

    begin = plan * size
    owner = begin // rows
    own = (owner == route.here).astype(jnp.int32)
    offset = jnp.clip(begin - route.here * rows, 0, rows - size)
    staying = offset // half + route.side
    going = offset // half + (1 - route.side)
    piece_rows = route.piece_rows(size)

    points_mine, points_other = route.spread(*pick(points, going, staying, half), owner)
    targets_mine, targets_other = route.spread(*pick(targets, going, staying, half), owner)

    norms, high, low = prepare(points, block_inverse, norm_scale)
    blocks, across, down = assemble(points_mine, points_other, piece_rows, norm_scale)
    tiles = rows // size
    left = points.reshape(tiles, size, features)
    left_norms = norms.reshape(tiles, size, 128)
    tall = []
    per = 2
    for r in range(0, rounds, per):
        pairs = [(t, s) for s in range(r, r + per) for t in range(tiles)]
        tall.append(gram(left, blocks, left_norms, across, pairs, inner_scale))
    among = gram(
        blocks, blocks, down, across, [(r, s) for r in range(rounds) for s in range(r)], inner_scale
    )
    residual, steps, partial = solve(
        plan, own, offset, piece_rows, targets_mine, targets_other, high, low, among, tall, targets
    )
    losses = jnp.sum(route.total(partial), axis=(1, 2)) / total
    return residual, steps, losses


def solution(mesh):
    placed = (P(AXES, None), P(AXES, None), P(), P())
    return jax.shard_map(
        functools.partial(on_device, dict(mesh.shape)),
        mesh=mesh,
        in_specs=placed,
        out_specs=(P(AXES, None), P(), P()),
        check_vma=False,
    )
```

time: 837 us -> 205 us (0.24)
  waiting for transfers between devices: 640 us -> 76.5 us
  Pallas kernels: 0 us -> 90.9 us
  matrix products: 52.5 us -> 0 us
  blocking collectives: 40.5 us -> 0 us
  other arithmetic: 46.1 us -> 8.43 us
  local copies, waits for them, and re-layouts: 31.5 us -> 0.72 us
  starting transfers between devices: 0.9 us -> 26.4 us
  between operations: 22.2 us -> 0.82 us
    psum x12 -> x0, waiting for transfers between devices: 639 us -> none  [broadcast(): return lax.psum(block, axis)]
    pallas_call x0 -> x9, Pallas kernels: none -> 90.9 us  [the longest x4 44.7 us: gram(): pl.pallas_call(functools.partial(gram_kernel, scale), out_shape=jax.Shape...]
    ppermute x0 -> x23, waiting for transfers between devices: none -> 76.5 us  [swap(): lax.ppermute(x, AXES, [(i, i ^ 1 << bit_of(i)) for i in range(devices)])]
    dot_general x12 -> x0, matrix products: 52.5 us -> none  [the longest x6 32.4 us: on_device(): jnp.dot(kernel, shared_step, preferred_element_type=jnp.float32)]
    psum x1 -> x0, blocking collectives: 40.5 us -> none  [on_device(): losses.append(lax.psum(partial_sum, ('row', 'col')) / total)]
    ppermute x0 -> x23, starting transfers between devices: none -> 26.4 us  [swap(): lax.ppermute(x, AXES, [(i, i ^ 1 << bit_of(i)) for i in range(devices)])]
    reduce_sum x13 -> x1, other arithmetic: 22.9 us -> 0.13 us  [on_device(): losses = jnp.sum(route.total(partial), axis=(1, 2)) / total]
    select_n x19 -> x8, other arithmetic: 23.2 us -> 5.4 us  [the longest x6 5.11 us: half(): jnp.where(same[:, None, None], lax.dynamic_slice_in_dim(mine, which * row...]
  transfers between devices with their start and end apart: 12 -> 23, of which waited for: 12 -> 17; matrix products, arithmetic and copies ran while one was open for 2% -> 2% of each run, Pallas kernels for 0% -> 33%
where the time goes in v1:
time: 205 us; the launch traced here: 204 us
  Pallas kernels  90.9 us (44%)
  waiting for transfers between devices  76.5 us (37%)
  starting transfers between devices  26.4 us (13%)
  other arithmetic  8.43 us (4%)
    ppermute x23, waiting for transfers between devices, swap(): lax.ppermute(x, AXES, [(i, i ^ 1 << bit_of(i)) for i in range(devices)])  76.5 us
    pallas_call x4, Pallas kernels, gram(): pl.pallas_call(functools.partial(gram_kernel, scale), out_shape=jax.Shape...  44.7 us
    ppermute x23, starting transfers between devices, swap(): lax.ppermute(x, AXES, [(i, i ^ 1 << bit_of(i)) for i in range(devices)])  26.4 us
    pallas_call x1, Pallas kernels, solve(): pl.pallas_call(functools.partial(solve_kernel, groups), out_shape=(jax.Sh...  19.1 us
    pallas_call x2, Pallas kernels, pick(): pl.pallas_call(pick_kernel, out_shape=(shape, shape), grid_spec=pltpu.Pre...  10.3 us
    pallas_call x1, Pallas kernels, prepare(): pl.pallas_call(functools.partial(prepare_kernel, scale), out_shape=(jax.S...  8.81 us
    pallas_call x1, Pallas kernels, assemble(): pl.pallas_call(functools.partial(assemble_kernel, scale), out_shape=(jax....  7.95 us
    select_n x6, other arithmetic, half(): jnp.where(same[:, None, None], lax.dynamic_slice_in_dim(mine, which * row...  5.11 us
  transfers between devices with their start and end apart: 23, of which 17 were waited for; matrix products, arithmetic and copies ran while one was open for 2% of the time, Pallas kernels for 33%

profile of v1, /device:TPU:0, one launch (start us, length us, event | category | flops | bytes accessed | tf_op | source)
XLA Modules:
  0.0 203.8 jit_solution(7159713727998107929)
XLA Ops:
  2.4 5.4 %pick.3 = (bf16[6,256,512]{2,1,0:T(8,128)(2,1)}, bf16[6,256,512]{2,1,0:T(8,128)(2,1)}) custom-call(s32[6]{0:T(128)} %broadcast_add_fusion.going_ref, s32[6]{0:T(128)} %get-tuple-element.31.staying_ref, bf16[2048,512]{1,0:T(8,128)(2,1)} %src_b.3, bf16[2048,512]{1,0:T(8,128)(2,1)} %src_b.3), custom_call_target="tpu_custom_call" | custom-call | tf_op jit(solution)/shard_map/pick/pallas_call | solution.py:112
  8.3 3.2 %collective-permute-done.9 = bf16[6,256,512]{2,1,0:T(8,128)(2,1)S(1)} collective-permute-done((bf16[6,256,512]{2,1,0:T(8,128)(2,1)}, bf16[6,256,512]{2,1,0:T(8,128)(2,1)S(1)}, u32[]{:S(2)}, u32[]{:S(2)}) %collective-permute-start.9) | collective-permute-done | bytes 1572896 | tf_op jit(solution)/shard_map/ppermute | solution.py:32
  11.5 2.9 %dynamic-slice_select_fusion.1 = (bf16[6,128,512]{2,1,0:T(8,128)(2,1)S(1)}, bf16[6,128,512]{2,1,0:T(8,128)(2,1)}) fusion(bf16[6,256,512]{2,1,0:T(8,128)(2,1)S(1)} %collective-permute-done.9, s32[]{:T(128)S(6)} %select_n.206, bf16[6,256,512]{2,1,0:T(8,128)(2,1)} %get-tuple-element.20, pred[6]{0:T(512)(128)(4,1)S(1)} %get-tuple-element.43, s32[]{:T(128)S(6)} %select_n.209), kind=kLoop, calls=%fused_computation.4 | loop fusion | flops 786432 | bytes 4718606 | tf_op jit(solution)/shard_map/jit(_where)/select_n | solution.py:76
  14.4 2.9 %collective-permute-start.10 = (bf16[6,128,512]{2,1,0:T(8,128)(2,1)}, bf16[6,128,512]{2,1,0:T(8,128)(2,1)S(1)}, u32[]{:S(2)}, u32[]{:S(2)}) collective-permute-start(bf16[6,128,512]{2,1,0:T(8,128)(2,1)} %get-tuple-element.35), channel_id=1, source_target_pairs={{0,1},{1,0},{2,3},{3,2},{4,5},{5,4},{6,7},{7,6},{8,24},{9,25},{10,... | collective-permute-start | bytes 2359304 | tf_op jit(solution)/shard_map/ppermute | solution.py:32
  17.3 10.2 %collective-permute-done.10 = bf16[6,128,512]{2,1,0:T(8,128)(2,1)S(1)} collective-permute-done((bf16[6,128,512]{2,1,0:T(8,128)(2,1)}, bf16[6,128,512]{2,1,0:T(8,128)(2,1)S(1)}, u32[]{:S(2)}, u32[]{:S(2)}) %collective-permute-start.10) | collective-permute-done | bytes 786464 | tf_op jit(solution)/shard_map/ppermute | solution.py:32
  27.8 2.2 %collective-permute-start.11 = (bf16[6,64,512]{2,1,0:T(8,128)(2,1)S(1)}, bf16[6,64,512]{2,1,0:T(8,128)(2,1)S(1)}, u32[]{:S(2)}, u32[]{:S(2)}) collective-permute-start(bf16[6,64,512]{2,1,0:T(8,128)(2,1)S(1)} %get-tuple-element.37), channel_id=1, source_target_pairs={{0,2},{1,3},{2,0},{3,1},{4,6},{5,7},{6,4},{7,5},{8,9},{9,8},{10,11... | collective-permute-start | bytes 1179656 | tf_op jit(solution)/shard_map/ppermute | solution.py:32
  30.0 5.8 %collective-permute-done.11 = bf16[6,64,512]{2,1,0:T(8,128)(2,1)S(1)} collective-permute-done((bf16[6,64,512]{2,1,0:T(8,128)(2,1)S(1)}, bf16[6,64,512]{2,1,0:T(8,128)(2,1)S(1)}, u32[]{:S(2)}, u32[]{:S(2)}) %collective-permute-start.11) | collective-permute-done | bytes 393248 | tf_op jit(solution)/shard_map/ppermute | solution.py:32
  35.9 2.7 %collective-permute-start.12 = (bf16[6,32,512]{2,1,0:T(8,128)(2,1)S(1)}, bf16[6,32,512]{2,1,0:T(8,128)(2,1)S(1)}, u32[]{:S(2)}, u32[]{:S(2)}) collective-permute-start(bf16[6,32,512]{2,1,0:T(8,128)(2,1)S(1)} %dynamic-slice_select_fusion.6), channel_id=1, source_target_pairs={{0,16},{1,17},{2,18},{3,19},{4,20},{5,21},{6,22},{7,23},{8,10},{9,... | collective-permute-start | bytes 589832 | tf_op jit(solution)/shard_map/ppermute | solution.py:32
  38.5 5.0 %pick.2 = (bf16[6,256,256]{2,1,0:T(8,128)(2,1)}, bf16[6,256,256]{2,1,0:T(8,128)(2,1)}) custom-call(s32[6]{0:T(128)} %broadcast_add_fusion.going_ref, s32[6]{0:T(128)} %get-tuple-element.31.staying_ref, f32[2048,256]{1,0:T(8,128)} %targets.1, f32[2048,256]{1,0:T(8,128)} %targets.1), custom_call_target="tpu_custom_call" | custom-call | tf_op jit(solution)/shard_map/pick/pallas_call | solution.py:112
  43.7 2.7 %collective-permute-start.13 = (bf16[6,32,512]{2,1,0:T(8,128)(2,1)S(1)}, bf16[6,32,512]{2,1,0:T(8,128)(2,1)S(1)}, u32[]{:S(2)}, u32[]{:S(2)}) collective-permute-start(bf16[6,32,512]{2,1,0:T(8,128)(2,1)S(1)} %select_select_fusion), channel_id=1, source_target_pairs={{0,4},{1,5},{2,6},{3,7},{4,0},{5,1},{6,2},{7,3},{8,12},{9,13},{10,... | collective-permute-start | bytes 589832 | tf_op jit(solution)/shard_map/ppermute | solution.py:32
  46.4 9.8 %collective-permute-done.13 = bf16[6,32,512]{2,1,0:T(8,128)(2,1)S(1)} collective-permute-done((bf16[6,32,512]{2,1,0:T(8,128)(2,1)S(1)}, bf16[6,32,512]{2,1,0:T(8,128)(2,1)S(1)}, u32[]{:S(2)}, u32[]{:S(2)}) %collective-permute-start.13) | collective-permute-done | bytes 196640 | tf_op jit(solution)/shard_map/ppermute | solution.py:32
  56.9 5.1 %collective-permute-done.14 = bf16[1,6,32,512]{3,2,1,0:T(8,128)(2,1)S(1)} collective-permute-done((bf16[1,6,32,512]{3,2,1,0:T(8,128)(2,1)S(1)}, bf16[1,6,32,512]{3,2,1,0:T(8,128)(2,1)S(1)}, u32[]{:S(2)}, u32[]{:S(2)}) %collective-permute-start.14) | collective-permute-done | bytes 196640 | tf_op jit(solution)/shard_map/ppermute | solution.py:32
  65.8 4.1 %collective-permute-done.15 = bf16[2,6,32,512]{3,2,1,0:T(8,128)(2,1)S(1)} collective-permute-done((bf16[2,6,32,512]{3,2,1,0:T(8,128)(2,1)S(1)}, bf16[2,6,32,512]{3,2,1,0:T(8,128)(2,1)S(1)}, u32[]{:S(2)}, u32[]{:S(2)}) %collective-permute-start.15) | collective-permute-done | bytes 393248 | tf_op jit(solution)/shard_map/ppermute | solution.py:32
  70.0 1.6 collective-permute-start.16
  73.7 4.3 %collective-permute-done.2 = bf16[6,64,256]{2,1,0:T(8,128)(2,1)S(1)} collective-permute-done((bf16[6,64,256]{2,1,0:T(8,128)(2,1)S(1)}, bf16[6,64,256]{2,1,0:T(8,128)(2,1)S(1)}, u32[]{:S(2)}, u32[]{:S(2)}) %collective-permute-start.2) | collective-permute-done | bytes 196640 | tf_op jit(solution)/shard_map/ppermute | solution.py:32
  78.8 5.2 %collective-permute-done.16 = bf16[4,6,32,512]{3,2,1,0:T(8,128)(2,1)S(1)} collective-permute-done((bf16[4,6,32,512]{3,2,1,0:T(8,128)(2,1)S(1)}, bf16[4,6,32,512]{3,2,1,0:T(8,128)(2,1)S(1)}, u32[]{:S(2)}, u32[]{:S(2)}) %collective-permute-start.16) | collective-permute-done | bytes 786464 | tf_op jit(solution)/shard_map/ppermute | solution.py:32
  84.4 2.2 %collective-permute-start.4 = (bf16[6,32,256]{2,1,0:T(8,128)(2,1)S(1)}, bf16[6,32,256]{2,1,0:T(8,128)(2,1)S(1)}, u32[]{:S(2)}, u32[]{:S(2)}) collective-permute-start(bf16[6,32,256]{2,1,0:T(8,128)(2,1)S(1)} %select_select_fusion.1), channel_id=1, source_target_pairs={{0,4},{1,5},{2,6},{3,7},{4,0},{5,1},{6,2},{7,3},{8,12},{9,13},{10,... | collective-permute-start | bytes 294920 | tf_op jit(solution)/shard_map/ppermute | solution.py:32
  86.6 6.0 %collective-permute-done.4 = bf16[6,32,256]{2,1,0:T(8,128)(2,1)S(1)} collective-permute-done((bf16[6,32,256]{2,1,0:T(8,128)(2,1)S(1)}, bf16[6,32,256]{2,1,0:T(8,128)(2,1)S(1)}, u32[]{:S(2)}, u32[]{:S(2)}) %collective-permute-start.4) | collective-permute-done | bytes 98336 | tf_op jit(solution)/shard_map/ppermute | solution.py:32
  93.2 4.2 %collective-permute-done.5 = bf16[1,6,32,256]{3,2,1,0:T(8,128)(2,1)S(1)} collective-permute-done((bf16[1,6,32,256]{3,2,1,0:T(8,128)(2,1)S(1)}, bf16[1,6,32,256]{3,2,1,0:T(8,128)(2,1)S(1)}, u32[]{:S(2)}, u32[]{:S(2)}) %collective-permute-start.5) | collective-permute-done | bytes 98336 | tf_op jit(solution)/shard_map/ppermute | solution.py:32
  97.8 5.4 %collective-permute-done.6 = bf16[2,6,32,256]{3,2,1,0:T(8,128)(2,1)S(1)} collective-permute-done((bf16[2,6,32,256]{3,2,1,0:T(8,128)(2,1)S(1)}, bf16[2,6,32,256]{3,2,1,0:T(8,128)(2,1)S(1)}, u32[]{:S(2)}, u32[]{:S(2)}) %collective-permute-start.6) | collective-permute-done | bytes 196640 | tf_op jit(solution)/shard_map/ppermute | solution.py:32
  104.1 8.8 %prepare.1 = (f32[2048,128]{1,0:T(8,128)}, bf16[6,512,512]{2,1,0:T(8,128)(2,1)}, bf16[6,512,512]{2,1,0:T(8,128)(2,1)}) custom-call(bf16[2048,512]{1,0:T(8,128)(2,1)} %src_b.3, f32[6,512,512]{2,1,0:T(8,128)} %inverse.1), custom_call_target="tpu_custom_call" | custom-call | bytes 16777216 | tf_op jit(solution)/shard_map/prepare/pallas_call | solution.py:164
  113.8 8.0 %assemble.1 = (bf16[6,512,512]{2,1,0:T(8,128)(2,1)}, f32[6,8,512]{2,1,0:T(8,128)}, f32[6,512,128]{2,1,0:T(8,128)}) custom-call(s32[16]{0:T(128)} %stack.67.rows_ref.piece_rows, bf16[8,6,32,512]{3,2,1,0:T(8,128)(2,1)} %copy-done.3, bf16[8,6,32,512]{3,2,1,0:T(8,128)(2,1)} %collective-permute-done.17.other), custom_call_target="tpu_custom_call" | custom-call | bytes 12582912 | tf_op jit(solution)/shard_map/assemble/pallas_call | solution.py:197
  121.8 9.5 %gram.7.rest_2_ = bf16[8,512,512]{2,1,0:T(8,128)(2,1)} custom-call(s32[8]{0:T(128)} %constant.80.clone.left_ids, s32[8]{0:T(128)} %constant.83.clone.right_ids, bf16[4,512,512]{2,1,0:T(8,128)(2,1)} %bitcast.22, bf16[6,512,512]{2,1,0:T(8,128)(2,1)} %get-tuple-element.22.left.right, f32[4,512,128]{2,1,0:T(8,128)} %bitcast.25, ...), custom_call_target="tpu_custom_call" | custom-call | flops 2147483648 | bytes 4194304 | tf_op jit(solution)/shard_map/gram/pallas_call | solution.py:228
  131.2 9.5 %gram.6.rest_1_ = bf16[8,512,512]{2,1,0:T(8,128)(2,1)} custom-call(s32[8]{0:T(128)} %constant.80.clone.left_ids, s32[8]{0:T(128)} %constant.82.clone.right_ids, bf16[4,512,512]{2,1,0:T(8,128)(2,1)} %bitcast.23, bf16[6,512,512]{2,1,0:T(8,128)(2,1)} %get-tuple-element.22.left.right, f32[4,512,128]{2,1,0:T(8,128)} %bitcast.26, ...), custom_call_target="tpu_custom_call" | custom-call | flops 2147483648 | bytes 4194304 | tf_op jit(solution)/shard_map/gram/pallas_call | solution.py:228
  140.7 9.5 %gram.5.rest_0_ = bf16[8,512,512]{2,1,0:T(8,128)(2,1)} custom-call(s32[8]{0:T(128)} %constant.80.clone.left_ids, s32[8]{0:T(128)} %constant.81.clone.right_ids, bf16[4,512,512]{2,1,0:T(8,128)(2,1)} %bitcast.24, bf16[6,512,512]{2,1,0:T(8,128)(2,1)} %get-tuple-element.22.left.right, f32[4,512,128]{2,1,0:T(8,128)} %bitcast.27, ...), custom_call_target="tpu_custom_call" | custom-call | flops 2147483648 | bytes 4194304 | tf_op jit(solution)/shard_map/gram/pallas_call | solution.py:228
  150.3 16.2 %gram.4.among = bf16[15,512,512]{2,1,0:T(8,128)(2,1)} custom-call(s32[15]{0:T(128)} %constant.84.clone.left_ids, s32[15]{0:T(128)} %constant.85.clone.right_ids, bf16[6,512,512]{2,1,0:T(8,128)(2,1)} %get-tuple-element.22.left.right, bf16[6,512,512]{2,1,0:T(8,128)(2,1)} %get-tuple-element.22.left.right, f32[6,512,128]{2,1,0:T(8,128)} %get-tuple-element.23.down, ...), custom_call_target="tpu_custom_call" | custom-call | flops 4026531840 | bytes 7864320 | tf_op jit(solution)/shard_map/gram/pallas_call | solution.py:228
  166.5 19.1 %solve.1 = (f32[2048,256]{1,0:T(8,128)}, bf16[6,512,256]{2,1,0:T(8,128)(2,1)}, f32[6,8,128]{2,1,0:T(8,128)S(1)}) custom-call(s32[6]{0:T(128)S(1)} %copy-done.1, s32[6]{0:T(128)S(1)} %get-tuple-element.44.own, s32[6]{0:T(128)S(1)} %get-tuple-element.33.offset, s32[16]{0:T(128)S(1)} %copy-done.2, bf16[8,6,32,256]{3,2,1,0:T(8,128)(2,1)S(1)} %pad_maximum_fusion.1.mine, ...), custom_call_target="tpu_custom_call" | custom-call | tf_op jit(solution)/shard_map/solve/pallas_call | solution.py:342
  188.0 2.7 %collective-permute-done.19 = f32[6,8,128]{2,1,0:T(8,128)S(1)} collective-permute-done((f32[6,8,128]{2,1,0:T(8,128)S(1)}, f32[6,8,128]{2,1,0:T(8,128)S(1)}, u32[]{:S(2)}, u32[]{:S(2)}) %collective-permute-start.19) | collective-permute-done | bytes 24608 | tf_op jit(solution)/shard_map/ppermute | solution.py:32
  191.4 3.1 %collective-permute-done.20 = f32[6,8,128]{2,1,0:T(8,128)S(1)} collective-permute-done((f32[6,8,128]{2,1,0:T(8,128)S(1)}, f32[6,8,128]{2,1,0:T(8,128)S(1)}, u32[]{:S(2)}, u32[]{:S(2)}) %collective-permute-start.20) | collective-permute-done | bytes 24608 | tf_op jit(solution)/shard_map/ppermute | solution.py:32
  195.1 3.2 %collective-permute-done.21 = f32[6,8,128]{2,1,0:T(8,128)S(1)} collective-permute-done((f32[6,8,128]{2,1,0:T(8,128)S(1)}, f32[6,8,128]{2,1,0:T(8,128)S(1)}, u32[]{:S(2)}, u32[]{:S(2)}) %collective-permute-start.21) | collective-permute-done | bytes 24608 | tf_op jit(solution)/shard_map/ppermute | solution.py:32
  198.4 2.1 %collective-permute-start.22 = (f32[6,8,128]{2,1,0:T(8,128)S(1)}, f32[6,8,128]{2,1,0:T(8,128)S(1)}, u32[]{:S(2)}, u32[]{:S(2)}) collective-permute-start(f32[6,8,128]{2,1,0:T(8,128)S(1)} %add.211), channel_id=1, source_target_pairs={{0,4},{1,5},{2,6},{3,7},{4,0},{5,1},{6,2},{7,3},{8,12},{9,13},{10,... | collective-permute-start | bytes 73736 | tf_op jit(solution)/shard_map/ppermute | solution.py:32
  200.5 2.6 %collective-permute-done.22 = f32[6,8,128]{2,1,0:T(8,128)S(1)} collective-permute-done((f32[6,8,128]{2,1,0:T(8,128)S(1)}, f32[6,8,128]{2,1,0:T(8,128)S(1)}, u32[]{:S(2)}, u32[]{:S(2)}) %collective-permute-start.22) | collective-permute-done | bytes 24608 | tf_op jit(solution)/shard_map/ppermute | solution.py:32
  (60 shorter events, 17.9 us)
Async XLA Ops:
  2.4 5.8 %copy-start.1 = (s32[6]{0:T(128)S(1)}, s32[6]{0:T(128)}, u32[]{:S(2)}) copy-start(s32[6]{0:T(128)} %plan.1) | copy-start | bytes 76
  7.8 3.7 %collective-permute-start.9 = (bf16[6,256,512]{2,1,0:T(8,128)(2,1)}, bf16[6,256,512]{2,1,0:T(8,128)(2,1)S(1)}, u32[]{:S(2)}, u32[]{:S(2)}) collective-permute-start(bf16[6,256,512]{2,1,0:T(8,128)(2,1)} %get-tuple-element.21), channel_id=1, source_target_pairs={{0,8},{1,9},{2,10},{3,11},{4,12},{5,13},{6,14},{7,15},{8,0},{9,1},... | collective-permute-start | bytes 4718600 | tf_op jit(solution)/shard_map/ppermute | solution.py:32
  14.4 13.0 %collective-permute-start.10 = (bf16[6,128,512]{2,1,0:T(8,128)(2,1)}, bf16[6,128,512]{2,1,0:T(8,128)(2,1)S(1)}, u32[]{:S(2)}, u32[]{:S(2)}) collective-permute-start(bf16[6,128,512]{2,1,0:T(8,128)(2,1)} %get-tuple-element.35), channel_id=1, source_target_pairs={{0,1},{1,0},{2,3},{3,2},{4,5},{5,4},{6,7},{7,6},{8,24},{9,25},{10,... | collective-permute-start | bytes 2359304 | tf_op jit(solution)/shard_map/ppermute | solution.py:32
  27.8 7.9 %collective-permute-start.11 = (bf16[6,64,512]{2,1,0:T(8,128)(2,1)S(1)}, bf16[6,64,512]{2,1,0:T(8,128)(2,1)S(1)}, u32[]{:S(2)}, u32[]{:S(2)}) collective-permute-start(bf16[6,64,512]{2,1,0:T(8,128)(2,1)S(1)} %get-tuple-element.37), channel_id=1, source_target_pairs={{0,2},{1,3},{2,0},{3,1},{4,6},{5,7},{6,4},{7,5},{8,9},{9,8},{10,11... | collective-permute-start | bytes 1179656 | tf_op jit(solution)/shard_map/ppermute | solution.py:32
  35.9 7.7 %collective-permute-start.12 = (bf16[6,32,512]{2,1,0:T(8,128)(2,1)S(1)}, bf16[6,32,512]{2,1,0:T(8,128)(2,1)S(1)}, u32[]{:S(2)}, u32[]{:S(2)}) collective-permute-start(bf16[6,32,512]{2,1,0:T(8,128)(2,1)S(1)} %dynamic-slice_select_fusion.6), channel_id=1, source_target_pairs={{0,16},{1,17},{2,18},{3,19},{4,20},{5,21},{6,22},{7,23},{8,10},{9,... | collective-permute-start | bytes 589832 | tf_op jit(solution)/shard_map/ppermute | solution.py:32
  43.5 19.3 %copy-start.4 = (bf16[6,256,256]{2,1,0:T(8,128)(2,1)S(1)}, bf16[6,256,256]{2,1,0:T(8,128)(2,1)}, u32[]{:S(2)}) copy-start(bf16[6,256,256]{2,1,0:T(8,128)(2,1)} %get-tuple-element.16) | copy-start | bytes 2359300
  43.5 19.3 %collective-permute-start = (bf16[6,256,256]{2,1,0:T(8,128)(2,1)}, bf16[6,256,256]{2,1,0:T(8,128)(2,1)}, u32[]{:S(2)}, u32[]{:S(2)}) collective-permute-start(bf16[6,256,256]{2,1,0:T(8,128)(2,1)} %get-tuple-element.17), channel_id=1, source_target_pairs={{0,8},{1,9},{2,10},{3,11},{4,12},{5,13},{6,14},{7,15},{8,0},{9,1},... | collective-permute-start | bytes 2359304 | tf_op jit(solution)/shard_map/ppermute | solution.py:32
  43.7 12.5 %collective-permute-start.13 = (bf16[6,32,512]{2,1,0:T(8,128)(2,1)S(1)}, bf16[6,32,512]{2,1,0:T(8,128)(2,1)S(1)}, u32[]{:S(2)}, u32[]{:S(2)}) collective-permute-start(bf16[6,32,512]{2,1,0:T(8,128)(2,1)S(1)} %select_select_fusion), channel_id=1, source_target_pairs={{0,4},{1,5},{2,6},{3,7},{4,0},{5,1},{6,2},{7,3},{8,12},{9,13},{10,... | collective-permute-start | bytes 589832 | tf_op jit(solution)/shard_map/ppermute | solution.py:32
  56.3 5.7 %collective-permute-start.14 = (bf16[1,6,32,512]{3,2,1,0:T(8,128)(2,1)S(1)}, bf16[1,6,32,512]{3,2,1,0:T(8,128)(2,1)S(1)}, u32[]{:S(2)}, u32[]{:S(2)}) collective-permute-start(bf16[1,6,32,512]{3,2,1,0:T(8,128)(2,1)S(1)} %select_bitcast_fusion), channel_id=1, source_target_pairs={{0,16},{1,17},{2,18},{3,19},{4,20},{5,21},{6,22},{7,23},{8,10},{9,... | collective-permute-start | bytes 589832 | tf_op jit(solution)/shard_map/ppermute | solution.py:32
  62.0 7.8 %collective-permute-start.15 = (bf16[2,6,32,512]{3,2,1,0:T(8,128)(2,1)S(1)}, bf16[2,6,32,512]{3,2,1,0:T(8,128)(2,1)S(1)}, u32[]{:S(2)}, u32[]{:S(2)}) collective-permute-start(bf16[2,6,32,512]{3,2,1,0:T(8,128)(2,1)S(1)} %pad_maximum_fusion.4), channel_id=1, source_target_pairs={{0,2},{1,3},{2,0},{3,1},{4,6},{5,7},{6,4},{7,5},{8,9},{9,8},{10,11... | collective-permute-start | bytes 1179656 | tf_op jit(solution)/shard_map/ppermute | solution.py:32
  64.3 7.8 %collective-permute-start.1 = (bf16[6,128,256]{2,1,0:T(8,128)(2,1)S(1)}, bf16[6,128,256]{2,1,0:T(8,128)(2,1)S(1)}, u32[]{:S(2)}, u32[]{:S(2)}) collective-permute-start(bf16[6,128,256]{2,1,0:T(8,128)(2,1)S(1)} %get-tuple-element.39), channel_id=1, source_target_pairs={{0,1},{1,0},{2,3},{3,2},{4,5},{5,4},{6,7},{7,6},{8,24},{9,25},{10,... | collective-permute-start | bytes 1179656 | tf_op jit(solution)/shard_map/ppermute | solution.py:32
  70.0 14.0 %collective-permute-start.16 = (bf16[4,6,32,512]{3,2,1,0:T(8,128)(2,1)S(1)}, bf16[4,6,32,512]{3,2,1,0:T(8,128)(2,1)S(1)}, u32[]{:S(2)}, u32[]{:S(2)}) collective-permute-start(bf16[4,6,32,512]{3,2,1,0:T(8,128)(2,1)S(1)} %pad_maximum_fusion.2), channel_id=1, source_target_pairs={{0,1},{1,0},{2,3},{3,2},{4,5},{5,4},{6,7},{7,6},{8,24},{9,25},{10,... | collective-permute-start | bytes 2359304 | tf_op jit(solution)/shard_map/ppermute | solution.py:32
  72.3 5.7 %collective-permute-start.2 = (bf16[6,64,256]{2,1,0:T(8,128)(2,1)S(1)}, bf16[6,64,256]{2,1,0:T(8,128)(2,1)S(1)}, u32[]{:S(2)}, u32[]{:S(2)}) collective-permute-start(bf16[6,64,256]{2,1,0:T(8,128)(2,1)S(1)} %get-tuple-element.41), channel_id=1, source_target_pairs={{0,2},{1,3},{2,0},{3,1},{4,6},{5,7},{6,4},{7,5},{8,9},{9,8},{10,11... | collective-permute-start | bytes 589832 | tf_op jit(solution)/shard_map/ppermute | solution.py:32
  78.1 6.1 %collective-permute-start.3 = (bf16[6,32,256]{2,1,0:T(8,128)(2,1)S(1)}, bf16[6,32,256]{2,1,0:T(8,128)(2,1)S(1)}, u32[]{:S(2)}, u32[]{:S(2)}) collective-permute-start(bf16[6,32,256]{2,1,0:T(8,128)(2,1)S(1)} %dynamic-slice_select_fusion.9), channel_id=1, source_target_pairs={{0,16},{1,17},{2,18},{3,19},{4,20},{5,21},{6,22},{7,23},{8,10},{9,... | collective-permute-start | bytes 294920 | tf_op jit(solution)/shard_map/ppermute | solution.py:32
  84.2 28.8 %copy-start.3 = (bf16[8,6,32,512]{3,2,1,0:T(8,128)(2,1)}, bf16[8,6,32,512]{3,2,1,0:T(8,128)(2,1)S(1)}, u32[]{:S(2)}) copy-start(bf16[8,6,32,512]{3,2,1,0:T(8,128)(2,1)S(1)} %pad_maximum_fusion.mine) | copy-start | bytes 4718596
  84.2 29.6 %collective-permute-start.17 = (bf16[8,6,32,512]{3,2,1,0:T(8,128)(2,1)S(1)}, bf16[8,6,32,512]{3,2,1,0:T(8,128)(2,1)}, u32[]{:S(2)}, u32[]{:S(2)}) collective-permute-start(bf16[8,6,32,512]{3,2,1,0:T(8,128)(2,1)S(1)} %pad_maximum_fusion.mine), channel_id=1, source_target_pairs={{0,8},{1,9},{2,10},{3,11},{4,12},{5,13},{6,14},{7,15},{8,0},{9,1},... | collective-permute-start | bytes 4718600 | tf_op jit(solution)/shard_map/ppermute | solution.py:32
  84.4 8.3 %collective-permute-start.4 = (bf16[6,32,256]{2,1,0:T(8,128)(2,1)S(1)}, bf16[6,32,256]{2,1,0:T(8,128)(2,1)S(1)}, u32[]{:S(2)}, u32[]{:S(2)}) collective-permute-start(bf16[6,32,256]{2,1,0:T(8,128)(2,1)S(1)} %select_select_fusion.1), channel_id=1, source_target_pairs={{0,4},{1,5},{2,6},{3,7},{4,0},{5,1},{6,2},{7,3},{8,12},{9,13},{10,... | collective-permute-start | bytes 294920 | tf_op jit(solution)/shard_map/ppermute | solution.py:32
  92.7 4.7 %collective-permute-start.5 = (bf16[1,6,32,256]{3,2,1,0:T(8,128)(2,1)S(1)}, bf16[1,6,32,256]{3,2,1,0:T(8,128)(2,1)S(1)}, u32[]{:S(2)}, u32[]{:S(2)}) collective-permute-start(bf16[1,6,32,256]{3,2,1,0:T(8,128)(2,1)S(1)} %select_bitcast_fusion.1), channel_id=1, source_target_pairs={{0,16},{1,17},{2,18},{3,19},{4,20},{5,21},{6,22},{7,23},{8,10},{9,... | collective-permute-start | bytes 294920 | tf_op jit(solution)/shard_map/ppermute | solution.py:32
  97.4 5.7 %collective-permute-start.6 = (bf16[2,6,32,256]{3,2,1,0:T(8,128)(2,1)S(1)}, bf16[2,6,32,256]{3,2,1,0:T(8,128)(2,1)S(1)}, u32[]{:S(2)}, u32[]{:S(2)}) collective-permute-start(bf16[2,6,32,256]{3,2,1,0:T(8,128)(2,1)S(1)} %pad_maximum_fusion.5), channel_id=1, source_target_pairs={{0,2},{1,3},{2,0},{3,1},{4,6},{5,7},{6,4},{7,5},{8,9},{9,8},{10,11... | collective-permute-start | bytes 589832 | tf_op jit(solution)/shard_map/ppermute | solution.py:32
  103.2 10.4 %collective-permute-start.7 = (bf16[4,6,32,256]{3,2,1,0:T(8,128)(2,1)S(1)}, bf16[4,6,32,256]{3,2,1,0:T(8,128)(2,1)S(1)}, u32[]{:S(2)}, u32[]{:S(2)}) collective-permute-start(bf16[4,6,32,256]{3,2,1,0:T(8,128)(2,1)S(1)} %pad_maximum_fusion.3), channel_id=1, source_target_pairs={{0,1},{1,0},{2,3},{3,2},{4,5},{5,4},{6,7},{7,6},{8,24},{9,25},{10,... | collective-permute-start | bytes 1179656 | tf_op jit(solution)/shard_map/ppermute | solution.py:32
  113.7 52.8 %collective-permute-start.8 = (bf16[8,6,32,256]{3,2,1,0:T(8,128)(2,1)S(1)}, bf16[8,6,32,256]{3,2,1,0:T(8,128)(2,1)}, u32[]{:S(2)}, u32[]{:S(2)}) collective-permute-start(bf16[8,6,32,256]{3,2,1,0:T(8,128)(2,1)S(1)} %pad_maximum_fusion.1.mine), channel_id=1, source_target_pairs={{0,8},{1,9},{2,10},{3,11},{4,12},{5,13},{6,14},{7,15},{8,0},{9,1},... | collective-permute-start | bytes 2359304 | tf_op jit(solution)/shard_map/ppermute | solution.py:32
  150.3 16.2 %copy-start = (f32[2048,256]{1,0:T(8,128)S(1)}, f32[2048,256]{1,0:T(8,128)}, u32[]{:S(2)}) copy-start(f32[2048,256]{1,0:T(8,128)} %targets.1) | copy-start | bytes 6291460
  150.3 16.2 %copy-start.2 = (s32[16]{0:T(128)S(1)}, s32[16]{0:T(128)}, u32[]{:S(2)}) copy-start(s32[16]{0:T(128)} %stack.67.rows_ref.piece_rows) | copy-start | bytes 196
  185.6 1.3 collective-permute-start.18
  186.9 3.8 %collective-permute-start.19 = (f32[6,8,128]{2,1,0:T(8,128)S(1)}, f32[6,8,128]{2,1,0:T(8,128)S(1)}, u32[]{:S(2)}, u32[]{:S(2)}) collective-permute-start(f32[6,8,128]{2,1,0:T(8,128)S(1)} %add.208), channel_id=1, source_target_pairs={{0,1},{1,0},{2,3},{3,2},{4,5},{5,4},{6,7},{7,6},{8,9},{9,8},{10,11... | collective-permute-start | bytes 73736 | tf_op jit(solution)/shard_map/ppermute | solution.py:32
  190.7 3.8 %collective-permute-start.20 = (f32[6,8,128]{2,1,0:T(8,128)S(1)}, f32[6,8,128]{2,1,0:T(8,128)S(1)}, u32[]{:S(2)}, u32[]{:S(2)}) collective-permute-start(f32[6,8,128]{2,1,0:T(8,128)S(1)} %add.209), channel_id=1, source_target_pairs={{0,2},{1,3},{2,0},{3,1},{4,6},{5,7},{6,4},{7,5},{8,10},{9,11},{10,... | collective-permute-start | bytes 73736 | tf_op jit(solution)/shard_map/ppermute | solution.py:32
  194.6 3.8 %collective-permute-start.21 = (f32[6,8,128]{2,1,0:T(8,128)S(1)}, f32[6,8,128]{2,1,0:T(8,128)S(1)}, u32[]{:S(2)}, u32[]{:S(2)}) collective-permute-start(f32[6,8,128]{2,1,0:T(8,128)S(1)} %add.210), channel_id=1, source_target_pairs={{0,16},{1,17},{2,18},{3,19},{4,20},{5,21},{6,22},{7,23},{8,24},{9,... | collective-permute-start | bytes 73736 | tf_op jit(solution)/shard_map/ppermute | solution.py:32
  198.4 4.7 %collective-permute-start.22 = (f32[6,8,128]{2,1,0:T(8,128)S(1)}, f32[6,8,128]{2,1,0:T(8,128)S(1)}, u32[]{:S(2)}, u32[]{:S(2)}) collective-permute-start(f32[6,8,128]{2,1,0:T(8,128)S(1)} %add.211), channel_id=1, source_target_pairs={{0,4},{1,5},{2,6},{3,7},{4,0},{5,1},{6,2},{7,3},{8,12},{9,13},{10,... | collective-permute-start | bytes 73736 | tf_op jit(solution)/shard_map/ppermute | solution.py:32

commit v2 on v0

v2 whole, which is shorter than its diff:
```python
import functools
import math

import jax
import jax.numpy as jnp
from jax import lax
from jax.experimental import pallas as pl
from jax.experimental.pallas import tpu as pltpu
from jax.sharding import PartitionSpec as P

RIDGE = 1.0
AXES = ("row", "col")
HALVINGS = 3
NT = (((1,), (1,)), ((), ()))
LOG2E = math.log2(math.e)
MIB = 1 << 20
SOLVE_VMEM = 16 * MIB
SMEM = pl.BlockSpec(memory_space=pltpu.SMEM)
VMEM = pl.BlockSpec(memory_space=pltpu.VMEM)
HBM = pl.BlockSpec(memory_space=pltpu.HBM)


def stage_bits(mesh_shape, late):
    cols = mesh_shape["col"].bit_length() - 1
    rows = mesh_shape["row"].bit_length() - 1
    core = cols
    along_col = list(range(cols))
    along_row = list(range(cols + 1, cols + rows))
    rest = along_col[2:] + along_row[1:]
    near, far, other = along_col[0], along_col[1], along_row[0]
    if late:
        return core, ([far, near, other] + rest, [far, other, near] + rest)
    return core, ([near, far, other] + rest, [other, near, far] + rest)


def swap(x, devices, bit_of):
    return lax.ppermute(x, AXES, [(i, i ^ (1 << bit_of(i))) for i in range(devices)])


class Route:
    def __init__(self, mesh_shape, late=False):
        self.devices = mesh_shape["row"] * mesh_shape["col"]
        self.core, self.orders = stage_bits(mesh_shape, late)
        self.stages = len(self.orders[0])
        self.halvings = min(HALVINGS, self.stages)
        self.here = lax.axis_index("row") * mesh_shape["col"] + lax.axis_index("col")
        self.side = (self.here >> self.core) & 1

    def swap_core(self, x):
        return swap(x, self.devices, lambda i: self.core)

    def swap_stage(self, x, k):
        return swap(x, self.devices, lambda i: self.orders[(i >> self.core) & 1][k])

    def bit(self, index, k, side=None):
        side = self.side if side is None else side
        first, second = self.orders
        return jnp.where(side == 0, (index >> first[k]) & 1, (index >> second[k]) & 1)

    def piece_rows(self, blocksize):
        count = 1 << self.halvings
        pieces = []
        for side in (self.side, 1 - self.side):
            for p in range(count):
                row = side * (blocksize // 2)
                for k in range(self.halvings):
                    flipped = self.bit(self.here, k, side) ^ ((p >> (self.halvings - 1 - k)) & 1)
                    row = row + flipped * (blocksize >> (k + 2))
                pieces.append(row)
        return pieces

    def spread(self, send, keep, owner):
        recv, = yield (self.swap_core, send),
        mine = keep
        same = ((owner >> self.core) & 1) == self.side
        for k in range(self.halvings):
            bit = self.bit(self.here, k)
            rows = mine.shape[1] // 2

            def half(which):
                return jnp.where(
                    same[:, None, None],
                    lax.dynamic_slice_in_dim(mine, which * rows, rows, 1),
                    lax.dynamic_slice_in_dim(recv, which * rows, rows, 1),
                )

            going, staying = half(1 - bit), half(bit)
            recv, = yield (functools.partial(self.swap_stage, k=k), going),
            mine = staying
            same = self.bit(owner, k) == bit
        for k in range(self.halvings, self.stages):
            mine = jnp.where(same[:, None, None], mine, recv)
            recv, = yield (functools.partial(self.swap_stage, k=k), mine),
            same = self.bit(owner, k) == self.bit(self.here, k)
        mine = jnp.where(same[:, None, None], mine, recv)
        for k in reversed(range(1, self.halvings)):
            recv, = yield (functools.partial(self.swap_stage, k=k), mine),
            mine = jnp.concatenate([mine, recv], 1)
        last = functools.partial(self.swap_stage, k=0)
        recv, mine_over = yield (last, mine), (self.swap_core, mine)
        self.early = mine, mine_over
        recv_over, = yield (self.swap_core, recv),
        return (mine, recv), (mine_over, recv_over)

    def total(self, x):
        x = x + self.swap_core(x)
        for k in range(self.stages):
            x = x + swap(x, self.devices, lambda i: self.orders[0][k])
        return x


class Stream:
    def __init__(self, steps):
        self.steps = steps
        self.result = None
        self.advance(None)

    def advance(self, recv):
        try:
            pairs = self.steps.send(recv)
            self.swaps = [swap for swap, _ in pairs]
            self.sends = tuple(send for _, send in pairs)
        except StopIteration as stop:
            self.swaps = self.sends = ()
            self.result = stop.value

    def go(self):
        self.advance(tuple(swap(send) for swap, send in zip(self.swaps, self.sends)))

    def after(self, *others):
        self.sends, others = lax.optimization_barrier((self.sends, others))
        return others


def together(*streams):
    sends = lax.optimization_barrier(tuple(s.sends for s in streams))
    for stream, ready in zip(streams, sends):
        stream.sends = ready
    for stream in streams:
        stream.go()


def block_offset(plan, r, here, rows, size):
    return pl.multiple_of(jnp.clip(plan[r] * size - here * rows, 0, rows - size), size)


def pick_points_kernel(mesh_shape, plan, points, going, staying, sems):
    slots, half, _ = going.shape
    route = Route(mesh_shape)
    copies = []
    for j, (dst, side) in enumerate(((going, 1 - route.side), (staying, route.side))):
        for r in range(slots):
            at = block_offset(plan, r, route.here, points.shape[0], 2 * half) + side * half
            src = points.at[pl.ds(pl.multiple_of(at, half), half)]
            copies.append(pltpu.make_async_copy(src, dst.at[r], sems.at[j * slots + r]))
            copies[-1].start()
    for copy in copies:
        copy.wait()


def pick_points(mesh_shape, plan, points, size):
    part = pltpu.VMEM((plan.shape[0], size // 2, points.shape[1]), points.dtype)
    return pl.pallas_call(
        functools.partial(pick_points_kernel, mesh_shape),
        out_shape=(part, part),
        in_specs=[SMEM, HBM],
        out_specs=(VMEM, VMEM),
        scratch_shapes=[pltpu.SemaphoreType.DMA((2 * plan.shape[0],))],
        name="pick_points",
    )(plan, points)


def pick_targets_kernel(mesh_shape, plan, targets, going, staying, landing, sems):
    slots, half, _ = going.shape
    route = Route(mesh_shape)
    away = pl.multiple_of((1 - route.side) * half, half)
    stay = pl.multiple_of(route.side * half, half)
    copies = []
    for r in range(slots):
        at = block_offset(plan, r, route.here, targets.shape[0], 2 * half)
        copies.append(pltpu.make_async_copy(
            targets.at[pl.ds(at, 2 * half)], landing.at[r], sems.at[r]))
        copies[-1].start()
    for r in range(slots):
        copies[r].wait()
        going[r] = landing[r, pl.ds(away, half), :].astype(going.dtype)
        staying[r] = landing[r, pl.ds(stay, half), :].astype(staying.dtype)


def pick_targets(mesh_shape, plan, targets, size):
    slots, width = plan.shape[0], targets.shape[1]
    part = pltpu.VMEM((slots, size // 2, width), jnp.bfloat16)
    return pl.pallas_call(
        functools.partial(pick_targets_kernel, mesh_shape),
        out_shape=(part, part),
        in_specs=[SMEM, HBM],
        out_specs=(VMEM, VMEM),
        scratch_shapes=[
            pltpu.VMEM((slots, size, width), targets.dtype),
            pltpu.SemaphoreType.DMA((slots,)),
        ],
        name="pick_targets",
    )(plan, targets)


def lane_sums(p, scale):
    wide = p.astype(jnp.float32)
    sums = scale * jnp.sum(wide * wide, axis=1, keepdims=True)
    return jnp.broadcast_to(sums, (p.shape[0], 128))


def norms_kernel(scale, points, norms):
    norms[...] = lane_sums(points[...], scale)


def point_norms(points, scale):
    rows, features = points.shape
    tile = rows // 2
    return pl.pallas_call(
        functools.partial(norms_kernel, scale),
        out_shape=jax.ShapeDtypeStruct((rows, 128), jnp.float32),
        grid=(rows // tile,),
        in_specs=[pl.BlockSpec((tile, features), lambda t: (t, 0))],
        out_specs=pl.BlockSpec((tile, 128), lambda t: (t, 0)),
        cost_estimate=pl.CostEstimate(flops=0, bytes_accessed=6 * MIB, transcendentals=0),
        name="norms",
    )(points)


def kernel_values(left, right, down, across, scale):
    inner = lax.dot_general(left, right, NT, preferred_element_type=jnp.float32)
    offset = jnp.concatenate([down] * (inner.shape[1] // 128), axis=1) + across
    return jnp.exp2(inner * scale + offset).astype(jnp.bfloat16)


def tall_kernel(norm_scale, scale, mine, other, points, norms, out):
    slots = mine.shape[0]
    tile = points.shape[0] // 2
    for r in range(slots):
        right = jnp.concatenate([mine[r], other[r]], axis=0)
        row = lane_sums(right, norm_scale).T[0:1, :]
        for t in range(2):
            where = pl.ds(t * tile, tile)
            out[r, where, :] = kernel_values(points[where, :], right, norms[where, :], row, scale)


def tall_matrices(points, norms, mine, other, norm_scale, scale):
    slots, quarter, features = mine.shape
    rows = points.shape[0]
    return pl.pallas_call(
        functools.partial(tall_kernel, norm_scale, scale),
        out_shape=pltpu.VMEM((slots, rows, 2 * quarter), jnp.bfloat16),
        in_specs=[VMEM] * 4,
        out_specs=VMEM,
        compiler_params=pltpu.CompilerParams(vmem_limit_bytes=12 * MIB),
        cost_estimate=pl.CostEstimate(
            flops=4 * slots * rows * quarter * features,
            bytes_accessed=8 * slots * rows * quarter,
            transcendentals=2 * slots * rows * quarter,
        ),
        name="tall",
    )(mine, other, points, norms)


def among_kernel(mesh_shape, norm_scale, scale, *refs):
    quarters = refs[0:4]
    out, blocks, down, across = refs[4:]
    rounds, size, _ = blocks.shape
    piece_rows = Route(mesh_shape).piece_rows(size)
    count = len(piece_rows)
    piece = size // count
    per = count // 4
    for r in range(rounds):
        for p in range(count):
            at = pl.multiple_of(piece_rows[p], piece)
            blocks[r, pl.ds(at, piece), :] = quarters[p // per][r, pl.ds(p % per * piece, piece), :]
        sums = lane_sums(blocks[r], norm_scale)
        down[r] = sums
        across[r] = sums.T[0:8, :]
    for s in range(rounds - 1):
        for r in range(s + 1, rounds):
            at = r * (r - 1) // 2 + s
            out[at] = kernel_values(blocks[r], blocks[s], down[r], across[s, 0:1, :], scale)


def among_matrices(mesh_shape, quarters, norm_scale, scale):
    rounds, quarter, features = quarters[0].shape
    size = 4 * quarter
    pairs = rounds * (rounds - 1) // 2
    return pl.pallas_call(
        functools.partial(among_kernel, mesh_shape, norm_scale, scale),
        out_shape=pltpu.VMEM((pairs, size, size), jnp.bfloat16),
        in_specs=[VMEM] * 4,
        out_specs=VMEM,
        scratch_shapes=[
            pltpu.VMEM((rounds, size, features), jnp.bfloat16),
            pltpu.VMEM((rounds, size, 128), jnp.float32),
            pltpu.VMEM((rounds, 8, size), jnp.float32),
        ],
        compiler_params=pltpu.CompilerParams(vmem_limit_bytes=12 * MIB),
        cost_estimate=pl.CostEstimate(
            flops=2 * pairs * size * size * features,
            bytes_accessed=4 * pairs * size * size,
            transcendentals=pairs * size * size,
        ),
        name="among",
    )(*quarters)


def solve_kernel(mesh_shape, plan, *refs):
    quarters = refs[0:4]
    inverse, among, targets, tall_a, tall_b, residual, steps, losses = refs[4:12]
    start, wide, turned = refs[12:]
    rounds, size, width = steps.shape
    rows = residual.shape[0]
    tiles = rows // size
    route = Route(mesh_shape)
    piece_rows = route.piece_rows(size)
    count = len(piece_rows)
    piece = size // count
    per = count // 4

    for r in range(rounds):
        for p in range(count):
            at = pl.multiple_of(piece_rows[p], piece)
            start[r, pl.ds(at, piece), :] = quarters[p // per][r, pl.ds(p % per * piece, piece), :]

    for r in range(rounds):
        value = start[r].astype(jnp.float32)
        first = r * (r - 1) // 2
        for s in range(r):
            value = value - jnp.dot(among[first + s], steps[s], preferred_element_type=jnp.float32)
            value = value - jnp.where(plan[s] == plan[r], RIDGE * wide[s], 0.0)
        top = value.astype(jnp.bfloat16)
        bottom = (value - top.astype(jnp.float32)).astype(jnp.bfloat16)
        matrix = inverse[r]
        high = matrix.astype(jnp.bfloat16)
        low = (matrix - high.astype(jnp.float32)).astype(jnp.bfloat16)
        step = jnp.dot(high, top, preferred_element_type=jnp.float32)
        step = step + jnp.dot(low, top, preferred_element_type=jnp.float32)
        step = step + jnp.dot(high, bottom, preferred_element_type=jnp.float32)
        wide[r] = step
        steps[r] = step.astype(jnp.bfloat16)
        for j, q in enumerate((0, 2, 1, 3)):
            for p in range(per):
                at = pl.multiple_of(piece_rows[q * per + p], piece)
                turned[r, pl.ds((j * per + p) * piece, piece), :] = steps[r, pl.ds(at, piece), :]

        begin = plan[r] * size - route.here * rows
        source = targets if r == 0 else residual
        total = jnp.zeros((8, width), jnp.float32)
        for t in range(tiles):
            where = pl.ds(t * size, size)
            part = source[where, :] - jnp.where(begin == t * size, RIDGE * wide[r], 0.0)
            for j, tall in enumerate((tall_a, tall_b)):
                rhs = turned[r, pl.ds(j * (size // 2), size // 2), :]
                part = part - jnp.dot(tall[r, where, :], rhs, preferred_element_type=jnp.float32)
            residual[where, :] = part
            total = total + jnp.sum((part * part).reshape(size // 8, 8, width), axis=0)
        folded = total[:, 0:128]
        for c in range(1, width // 128):
            folded = folded + total[:, c * 128:(c + 1) * 128]
        losses[r] = folded


def solve(mesh_shape, plan, quarters, inverse, among, tall_a, tall_b, targets):
    rounds, size, _ = inverse.shape
    rows, width = targets.shape
    return pl.pallas_call(
        functools.partial(solve_kernel, mesh_shape),
        out_shape=(
            jax.ShapeDtypeStruct((rows, width), jnp.float32),
            jax.ShapeDtypeStruct((rounds, size, width), jnp.bfloat16),
            jax.ShapeDtypeStruct((rounds, 8, 128), jnp.float32),
        ),
        in_specs=[SMEM] + [VMEM] * 9,
        out_specs=(VMEM, VMEM, VMEM),
        scratch_shapes=[
            pltpu.VMEM((rounds, size, width), jnp.bfloat16),
            pltpu.VMEM((rounds, size, width), jnp.float32),
            pltpu.VMEM((rounds, size, width), jnp.bfloat16),
        ],
        compiler_params=pltpu.CompilerParams(vmem_limit_bytes=SOLVE_VMEM),
        name="solve",
    )(plan, *quarters, inverse, among, targets, tall_a, tall_b)


def on_device(mesh_shape, points, targets, plan, block_inverse):
    rows, features = points.shape
    width = targets.shape[1]
    size = block_inverse.shape[1]
    route = Route(mesh_shape)
    total = rows * route.devices * width
    gamma = 2.0 / features
    norm_scale = -gamma * LOG2E
    inner_scale = 2.0 * gamma * LOG2E

    owner = plan * size // rows

    lead = Stream(route.spread(*pick_points(mesh_shape, plan, points, size), owner))
    trail = None
    tall_a = None
    stage = 0
    while lead.result is None:
        if stage == 1:
            held, = lead.after(targets)
            trail = Stream(route.spread(*pick_targets(mesh_shape, plan, held, size), owner))
        if stage == 2:
            held, = lead.after(points)
            norms = point_norms(held, norm_scale)
        if stage == 3:
            norms, = lead.after(norms)
        if hasattr(route, "early") and tall_a is None:
            tall_a = tall_matrices(points, norms, *route.early, norm_scale, inner_scale)
            tall_a, = lead.after(tall_a)
        if stage == 0:
            lead.go()
        elif stage == 1:
            lead.go()
            trail.go()
        else:
            together(lead, trail)
        stage += 1
    (first_mine, last_mine), (first_other, last_other) = lead.result

    if trail.result is None:
        last_mine, = trail.after(last_mine)
    tall_b = tall_matrices(points, norms, last_mine, last_other, norm_scale, inner_scale)
    ready = (first_mine, last_mine, first_other, last_other)
    if trail.result is None:
        trail.go()
        if trail.result is None:
            tall_b, ready = trail.after(tall_b, ready)
    among = among_matrices(mesh_shape, ready, norm_scale, inner_scale)
    while trail.result is None:
        trail.go()
    (a, b), (c, d) = trail.result
    residual, steps, partial = solve(
        mesh_shape, plan, (a, b, c, d), block_inverse, among, tall_a, tall_b, targets)
    losses = jnp.sum(route.total(partial), axis=(1, 2)) / total
    return residual, steps, losses


def solution(mesh):
    placed = (P(AXES, None), P(AXES, None), P(), P())
    return jax.shard_map(
        functools.partial(on_device, dict(mesh.shape)),
        mesh=mesh,
        in_specs=placed,
        out_specs=(P(AXES, None), P(), P()),
        check_vma=False,
    )
```

time: 837 us -> 139 us (0.17)
  waiting for transfers between devices: 640 us -> 59.6 us
  matrix products: 52.5 us -> 0 us
  blocking collectives: 40.5 us -> 0 us
  other arithmetic: 46.1 us -> 8.04 us
  Pallas kernels: 0 us -> 37.8 us
  local copies, waits for them, and re-layouts: 31.5 us -> 0.05 us
  starting transfers between devices: 0.9 us -> 31.7 us
  between operations: 22.2 us -> 0.94 us
    psum x12 -> x0, waiting for transfers between devices: 639 us -> none  [broadcast(): return lax.psum(block, axis)]
    ppermute x0 -> x25, waiting for transfers between devices: none -> 59.6 us  [swap(): lax.ppermute(x, AXES, [(i, i ^ 1 << bit_of(i)) for i in range(devices)])]
    dot_general x12 -> x0, matrix products: 52.5 us -> none  [the longest x6 32.4 us: on_device(): jnp.dot(kernel, shared_step, preferred_element_type=jnp.float32)]
    psum x1 -> x0, blocking collectives: 40.5 us -> none  [on_device(): losses.append(lax.psum(partial_sum, ('row', 'col')) / total)]
    pallas_call x0 -> x7, Pallas kernels: none -> 37.8 us  [the longest x1 15.9 us: solve(): pl.pallas_call(functools.partial(solve_kernel, mesh_shape), out_shape=(ja...]
    ppermute x0 -> x25, starting transfers between devices: none -> 31.7 us  [swap(): lax.ppermute(x, AXES, [(i, i ^ 1 << bit_of(i)) for i in range(devices)])]
    reduce_sum x13 -> x1, other arithmetic: 22.9 us -> 0.13 us  [on_device(): losses = jnp.sum(route.total(partial), axis=(1, 2)) / total]
    dynamic_update_slice x6 -> x0, local copies, waits for them, and re-layouts: 17.7 us -> none  [on_device(): residual = lax.dynamic_update_slice_in_dim(residual, owned, offset, 0)]
  transfers between devices with their start and end apart: 12 -> 25, of which waited for: 12 -> 19; matrix products, arithmetic and copies ran while one was open for 2% -> 2% of each run, Pallas kernels for 0% -> 14%
where the time goes in v2:
time: 139 us; the launch traced here: 138 us
  waiting for transfers between devices  59.6 us (43%)
  Pallas kernels  37.8 us (27%)
  starting transfers between devices  31.7 us (23%)
  other arithmetic  8.04 us (6%)
    ppermute x25, waiting for transfers between devices, swap(): lax.ppermute(x, AXES, [(i, i ^ 1 << bit_of(i)) for i in range(devices)])  59.6 us
    ppermute x25, starting transfers between devices, swap(): lax.ppermute(x, AXES, [(i, i ^ 1 << bit_of(i)) for i in range(devices)])  31.7 us
    pallas_call x1, Pallas kernels, solve(): pl.pallas_call(functools.partial(solve_kernel, mesh_shape), out_shape=(ja...  15.9 us
    pallas_call x2, Pallas kernels, tall_matrices(): pl.pallas_call(functools.partial(tall_kernel, norm_scale, scale), out_sha...  7.17 us
    select_n x6, other arithmetic, half(): jnp.where(same[:, None, None], lax.dynamic_slice_in_dim(mine, which * row...  6.75 us
    pallas_call x1, Pallas kernels, among_matrices(): pl.pallas_call(functools.partial(among_kernel, mesh_shape, norm_scale, sc...  6.08 us
    pallas_call x1, Pallas kernels, pick_targets(): pl.pallas_call(functools.partial(pick_targets_kernel, mesh_shape), out_sh...  3.07 us
    pallas_call x1, Pallas kernels, pick_points(): pl.pallas_call(functools.partial(pick_points_kernel, mesh_shape), out_sha...  2.95 us
  transfers between devices with their start and end apart: 25, of which 19 were waited for; matrix products, arithmetic and copies ran while one was open for 2% of the time, Pallas kernels for 14%

profile of v2, /device:TPU:0, one launch (start us, length us, event | category | flops | bytes accessed | tf_op | source)
XLA Modules:
  0.0 138.1 jit_solution(1472193981952167586)
XLA Ops:
  0.6 2.9 %pick_points.1 = (bf16[6,256,512]{2,1,0:T(8,128)(2,1)S(1)}, bf16[6,256,512]{2,1,0:T(8,128)(2,1)S(1)}) custom-call(s32[6]{0:T(128)} %plan.5, bf16[2048,512]{1,0:T(8,128)(2,1)} %points.6), custom_call_target="tpu_custom_call" | custom-call | tf_op jit(solution)/shard_map/pick_points/pallas_call | solution.py:163
  4.1 3.1 %collective-permute-done = bf16[6,256,512]{2,1,0:T(8,128)(2,1)} collective-permute-done((bf16[6,256,512]{2,1,0:T(8,128)(2,1)S(1)}, bf16[6,256,512]{2,1,0:T(8,128)(2,1)}, u32[]{:S(2)}, u32[]{:S(2)}) %collective-permute-start) | collective-permute-done | bytes 1572896 | tf_op jit(solution)/shard_map/ppermute | solution.py:37
  7.2 3.1 %dynamic-slice_select_fusion = (bf16[6,128,512]{2,1,0:T(8,128)(2,1)}, bf16[6,128,512]{2,1,0:T(8,128)(2,1)}) fusion(bf16[6,256,512]{2,1,0:T(8,128)(2,1)} %collective-permute-done, s32[]{:T(128)S(6)} %select_n.146, bf16[6,256,512]{2,1,0:T(8,128)(2,1)S(1)} %get-tuple-element.36, pred[6]{0:T(512)(128)(4,1)S(1)} %get-tuple-element.80, s32[]{:T(128)S(6)} %select_n.144), kind=kLoop, calls=%fused_computation.1 | loop fusion | flops 786432 | bytes 4718606 | tf_op jit(solution)/shard_map/jit(_where)/select_n | solution.py:81
  10.4 2.9 %collective-permute-start.2 = (bf16[6,128,512]{2,1,0:T(8,128)(2,1)}, bf16[6,128,512]{2,1,0:T(8,128)(2,1)}, u32[]{:S(2)}, u32[]{:S(2)}) collective-permute-start(bf16[6,128,512]{2,1,0:T(8,128)(2,1)} %get-tuple-element.41), channel_id=1, source_target_pairs={{0,1},{1,0},{2,3},{3,2},{4,5},{5,4},{6,7},{7,6},{8,24},{9,25},{10,... | collective-permute-start | bytes 2359304 | tf_op jit(solution)/shard_map/ppermute | solution.py:37
  13.3 3.1 %pick_targets.1 = (bf16[6,256,256]{2,1,0:T(8,128)(2,1)S(1)}, bf16[6,256,256]{2,1,0:T(8,128)(2,1)S(1)}) custom-call(s32[6]{0:T(128)} %plan.5, f32[2048,256]{1,0:T(8,128)} %refs_6_.1), custom_call_target="tpu_custom_call" | custom-call | tf_op jit(solution)/shard_map/pick_targets/pallas_call | solution.py:193
  16.5 7.1 %collective-permute-done.2 = bf16[6,128,512]{2,1,0:T(8,128)(2,1)} collective-permute-done((bf16[6,128,512]{2,1,0:T(8,128)(2,1)}, bf16[6,128,512]{2,1,0:T(8,128)(2,1)}, u32[]{:S(2)}, u32[]{:S(2)}) %collective-permute-start.2) | collective-permute-done | bytes 786464 | tf_op jit(solution)/shard_map/ppermute | solution.py:37
  23.6 2.2 %dynamic-slice_select_fusion.2 = (bf16[6,64,512]{2,1,0:T(8,128)(2,1)S(1)}, bf16[6,64,512]{2,1,0:T(8,128)(2,1)}) fusion(bf16[6,128,512]{2,1,0:T(8,128)(2,1)} %collective-permute-done.2, s32[]{:T(128)S(6)} %select_n.148, bf16[6,128,512]{2,1,0:T(8,128)(2,1)S(1)} %copy-done.5, pred[6]{0:T(512)(128)(4,1)S(1)} %get-tuple-element.82, s32[]{:T(128)S(6)} %select_n.150), kind=kLoop, calls=%fused_computation.5 | loop fusion | flops 393216 | bytes 2359310 | tf_op jit(solution)/shard_map/jit(_where)/select_n | solution.py:81
  26.8 2.2 %collective-permute-start.4 = (bf16[6,64,512]{2,1,0:T(8,128)(2,1)}, bf16[6,64,512]{2,1,0:T(8,128)(2,1)S(1)}, u32[]{:S(2)}, u32[]{:S(2)}) collective-permute-start(bf16[6,64,512]{2,1,0:T(8,128)(2,1)} %get-tuple-element.44), channel_id=1, source_target_pairs={{0,2},{1,3},{2,0},{3,1},{4,6},{5,7},{6,4},{7,5},{8,9},{9,8},{10,11... | collective-permute-start | bytes 1179656 | tf_op jit(solution)/shard_map/ppermute | solution.py:37
  30.5 2.6 %norms.1 = f32[2048,128]{1,0:T(8,128)} custom-call(bf16[2048,512]{1,0:T(8,128)(2,1)} %points.6), custom_call_target="tpu_custom_call" | custom-call | bytes 6291456 | tf_op jit(solution)/shard_map/norms/pallas_call | solution.py:219
  33.1 1.9 %collective-permute-done.4 = bf16[6,64,512]{2,1,0:T(8,128)(2,1)S(1)} collective-permute-done((bf16[6,64,512]{2,1,0:T(8,128)(2,1)}, bf16[6,64,512]{2,1,0:T(8,128)(2,1)S(1)}, u32[]{:S(2)}, u32[]{:S(2)}) %collective-permute-start.4) | collective-permute-done | bytes 393248 | tf_op jit(solution)/shard_map/ppermute | solution.py:37
  35.1 2.6 %collective-permute-done.3 = bf16[6,128,256]{2,1,0:T(8,128)(2,1)S(1)} collective-permute-done((bf16[6,128,256]{2,1,0:T(8,128)(2,1)S(1)}, bf16[6,128,256]{2,1,0:T(8,128)(2,1)S(1)}, u32[]{:S(2)}, u32[]{:S(2)}) %collective-permute-start.3) | collective-permute-done | bytes 393248 | tf_op jit(solution)/shard_map/ppermute | solution.py:37
  37.9 1.9 %collective-permute-start.5 = (bf16[6,64,256]{2,1,0:T(8,128)(2,1)S(1)}, bf16[6,64,256]{2,1,0:T(8,128)(2,1)S(1)}, u32[]{:S(2)}, u32[]{:S(2)}) collective-permute-start(bf16[6,64,256]{2,1,0:T(8,128)(2,1)S(1)} %get-tuple-element.47), channel_id=1, source_target_pairs={{0,2},{1,3},{2,0},{3,1},{4,6},{5,7},{6,4},{7,5},{8,9},{9,8},{10,11... | collective-permute-start | bytes 589832 | tf_op jit(solution)/shard_map/ppermute | solution.py:37
  41.3 3.0 %collective-permute-done.5 = bf16[6,64,256]{2,1,0:T(8,128)(2,1)S(1)} collective-permute-done((bf16[6,64,256]{2,1,0:T(8,128)(2,1)S(1)}, bf16[6,64,256]{2,1,0:T(8,128)(2,1)S(1)}, u32[]{:S(2)}, u32[]{:S(2)}) %collective-permute-start.5) | collective-permute-done | bytes 196640 | tf_op jit(solution)/shard_map/ppermute | solution.py:37
  47.2 2.6 %collective-permute-start.8 = (bf16[6,32,512]{2,1,0:T(8,128)(2,1)S(1)}, bf16[6,32,512]{2,1,0:T(8,128)(2,1)S(1)}, u32[]{:S(2)}, u32[]{:S(2)}) collective-permute-start(bf16[6,32,512]{2,1,0:T(8,128)(2,1)S(1)} %select_select_fusion), channel_id=1, source_target_pairs={{0,4},{1,5},{2,6},{3,7},{4,0},{5,1},{6,2},{7,3},{8,12},{9,13},{10,... | collective-permute-start | bytes 589832 | tf_op jit(solution)/shard_map/ppermute | solution.py:37
  50.4 7.1 %collective-permute-done.8 = bf16[6,32,512]{2,1,0:T(8,128)(2,1)S(1)} collective-permute-done((bf16[6,32,512]{2,1,0:T(8,128)(2,1)S(1)}, bf16[6,32,512]{2,1,0:T(8,128)(2,1)S(1)}, u32[]{:S(2)}, u32[]{:S(2)}) %collective-permute-start.8) | collective-permute-done | bytes 196640 | tf_op jit(solution)/shard_map/ppermute | solution.py:37
  58.2 5.3 %collective-permute-done.9 = bf16[6,32,256]{2,1,0:T(8,128)(2,1)S(1)} collective-permute-done((bf16[6,32,256]{2,1,0:T(8,128)(2,1)S(1)}, bf16[6,32,256]{2,1,0:T(8,128)(2,1)S(1)}, u32[]{:S(2)}, u32[]{:S(2)}) %collective-permute-start.9) | collective-permute-done | bytes 98336 | tf_op jit(solution)/shard_map/ppermute | solution.py:37
  63.7 1.9 %collective-permute-start.12 = (bf16[6,64,512]{2,1,0:T(8,128)(2,1)S(1)}, bf16[6,64,512]{2,1,0:T(8,128)(2,1)S(1)}, u32[]{:S(2)}, u32[]{:S(2)}) collective-permute-start(bf16[6,64,512]{2,1,0:T(8,128)(2,1)S(1)} %pad_maximum_fusion.1), channel_id=1, source_target_pairs={{0,2},{1,3},{2,0},{3,1},{4,6},{5,7},{6,4},{7,5},{8,9},{9,8},{10,11... | collective-permute-start | bytes 1179656 | tf_op jit(solution)/shard_map/ppermute | solution.py:37
  66.9 3.3 %collective-permute-done.11 = bf16[6,32,256]{2,1,0:T(8,128)(2,1)S(1)} collective-permute-done((bf16[6,32,256]{2,1,0:T(8,128)(2,1)S(1)}, bf16[6,32,256]{2,1,0:T(8,128)(2,1)S(1)}, u32[]{:S(2)}, u32[]{:S(2)}) %collective-permute-start.11) | collective-permute-done | bytes 98336 | tf_op jit(solution)/shard_map/ppermute | solution.py:37
  71.7 2.6 %collective-permute-start.14 = (bf16[6,128,512]{2,1,0:T(8,128)(2,1)S(1)}, bf16[6,128,512]{2,1,0:T(8,128)(2,1)S(1)}, u32[]{:S(2)}, u32[]{:S(2)}) collective-permute-start(bf16[6,128,512]{2,1,0:T(8,128)(2,1)S(1)} %pad_maximum_fusion.mine.refs_0_), channel_id=1, source_target_pairs={{0,1},{1,0},{2,3},{3,2},{4,5},{5,4},{6,7},{7,6},{8,24},{9,25},{10,... | collective-permute-start | bytes 2359304 | tf_op jit(solution)/shard_map/ppermute | solution.py:37
  74.3 2.0 %collective-permute-start.13 = (bf16[6,64,256]{2,1,0:T(8,128)(2,1)S(1)}, bf16[6,64,256]{2,1,0:T(8,128)(2,1)S(1)}, u32[]{:S(2)}, u32[]{:S(2)}) collective-permute-start(bf16[6,64,256]{2,1,0:T(8,128)(2,1)S(1)} %pad_maximum_fusion.3), channel_id=1, source_target_pairs={{0,2},{1,3},{2,0},{3,1},{4,6},{5,7},{6,4},{7,5},{8,9},{9,8},{10,11... | collective-permute-start | bytes 589832 | tf_op jit(solution)/shard_map/ppermute | solution.py:37
  76.3 3.6 %collective-permute-done.13 = bf16[6,64,256]{2,1,0:T(8,128)(2,1)S(1)} collective-permute-done((bf16[6,64,256]{2,1,0:T(8,128)(2,1)S(1)}, bf16[6,64,256]{2,1,0:T(8,128)(2,1)S(1)}, u32[]{:S(2)}, u32[]{:S(2)}) %collective-permute-start.13) | collective-permute-done | bytes 196640 | tf_op jit(solution)/shard_map/ppermute | solution.py:37
  80.0 3.6 %tall.2.refs_7_ = bf16[6,2048,256]{2,1,0:T(8,128)(2,1)S(1)} custom-call(bf16[6,128,512]{2,1,0:T(8,128)(2,1)S(1)} %pad_maximum_fusion.mine.refs_0_, bf16[6,128,512]{2,1,0:T(8,128)(2,1)S(1)} %collective-permute-done.15.other.refs_2_, bf16[2048,512]{1,0:T(8,128)(2,1)S(1)} %copy-done.1, f32[2048,128]{1,0:T(8,128)S(1)} %copy-done.2), custom_call_target="tpu_custom_call" | custom-call | flops 3221225472 | bytes 12582912 | tf_op jit(solution)/shard_map/tall/pallas_call | solution.py:250
  83.6 2.8 %collective-permute-done.14.refs_1_.mine = bf16[6,128,512]{2,1,0:T(8,128)(2,1)S(1)} collective-permute-done((bf16[6,128,512]{2,1,0:T(8,128)(2,1)S(1)}, bf16[6,128,512]{2,1,0:T(8,128)(2,1)S(1)}, u32[]{:S(2)}, u32[]{:S(2)}) %collective-permute-start.14) | collective-permute-done | bytes 786464 | tf_op jit(solution)/shard_map/ppermute | solution.py:37
  88.2 6.0 %collective-permute-done.16.refs_1_ = bf16[6,128,256]{2,1,0:T(8,128)(2,1)S(1)} collective-permute-done((bf16[6,128,256]{2,1,0:T(8,128)(2,1)S(1)}, bf16[6,128,256]{2,1,0:T(8,128)(2,1)S(1)}, u32[]{:S(2)}, u32[]{:S(2)}) %collective-permute-start.16) | collective-permute-done | bytes 393248 | tf_op jit(solution)/shard_map/ppermute | solution.py:37
  94.2 3.6 %tall.3.refs_8_ = bf16[6,2048,256]{2,1,0:T(8,128)(2,1)S(1)} custom-call(bf16[6,128,512]{2,1,0:T(8,128)(2,1)S(1)} %collective-permute-done.14.refs_1_.mine, bf16[6,128,512]{2,1,0:T(8,128)(2,1)S(1)} %collective-permute-done.19.refs_3_.other, bf16[2048,512]{1,0:T(8,128)(2,1)S(1)} %copy-done.1, f32[2048,128]{1,0:T(8,128)S(1)} %copy-done.2), custom_call_target="tpu_custom_call" | custom-call | flops 3221225472 | bytes 12582912 | tf_op jit(solution)/shard_map/tall/pallas_call | solution.py:250
  97.8 6.1 %among.1.refs_5_ = bf16[15,512,512]{2,1,0:T(8,128)(2,1)S(1)} custom-call(bf16[6,128,512]{2,1,0:T(8,128)(2,1)S(1)} %pad_maximum_fusion.mine.refs_0_, bf16[6,128,512]{2,1,0:T(8,128)(2,1)S(1)} %collective-permute-done.14.refs_1_.mine, bf16[6,128,512]{2,1,0:T(8,128)(2,1)S(1)} %collective-permute-done.15.other.refs_2_, ...), custom_call_target="tpu_custom_call" | custom-call | flops 4026531840 | bytes 15728640 | tf_op jit(solution)/shard_map/among/pallas_call | solution.py:290
  104.0 15.9 %solve.1 = (f32[2048,256]{1,0:T(8,128)}, bf16[6,512,256]{2,1,0:T(8,128)(2,1)}, f32[6,8,128]{2,1,0:T(8,128)S(1)}) custom-call(s32[6]{0:T(128)S(1)} %copy-done.4, bf16[6,128,256]{2,1,0:T(8,128)(2,1)S(1)} %pad_maximum_fusion.2.refs_0_, bf16[6,128,256]{2,1,0:T(8,128)(2,1)S(1)} %collective-permute-done.16.refs_1_, ...), custom_call_target="tpu_custom_call" | custom-call | tf_op jit(solution)/shard_map/solve/pallas_call | solution.py:369
  123.0 2.0 %collective-permute-done.21 = f32[6,8,128]{2,1,0:T(8,128)S(1)} collective-permute-done((f32[6,8,128]{2,1,0:T(8,128)S(1)}, f32[6,8,128]{2,1,0:T(8,128)S(1)}, u32[]{:S(2)}, u32[]{:S(2)}) %collective-permute-start.21) | collective-permute-done | bytes 24608 | tf_op jit(solution)/shard_map/ppermute | solution.py:37
  125.1 2.0 %collective-permute-start.22 = (f32[6,8,128]{2,1,0:T(8,128)S(1)}, f32[6,8,128]{2,1,0:T(8,128)S(1)}, u32[]{:S(2)}, u32[]{:S(2)}) collective-permute-start(f32[6,8,128]{2,1,0:T(8,128)S(1)} %add.63), channel_id=1, source_target_pairs={{0,2},{1,3},{2,0},{3,1},{4,6},{5,7},{6,4},{7,5},{8,10},{9,11},{10,... | collective-permute-start | bytes 73736 | tf_op jit(solution)/shard_map/ppermute | solution.py:37
  127.1 1.8 %collective-permute-done.22 = f32[6,8,128]{2,1,0:T(8,128)S(1)} collective-permute-done((f32[6,8,128]{2,1,0:T(8,128)S(1)}, f32[6,8,128]{2,1,0:T(8,128)S(1)}, u32[]{:S(2)}, u32[]{:S(2)}) %collective-permute-start.22) | collective-permute-done | bytes 24608 | tf_op jit(solution)/shard_map/ppermute | solution.py:37
  129.5 3.2 %collective-permute-done.23 = f32[6,8,128]{2,1,0:T(8,128)S(1)} collective-permute-done((f32[6,8,128]{2,1,0:T(8,128)S(1)}, f32[6,8,128]{2,1,0:T(8,128)S(1)}, u32[]{:S(2)}, u32[]{:S(2)}) %collective-permute-start.23) | collective-permute-done | bytes 24608 | tf_op jit(solution)/shard_map/ppermute | solution.py:37
  134.5 2.9 %collective-permute-done.24 = f32[6,8,128]{2,1,0:T(8,128)S(1)} collective-permute-done((f32[6,8,128]{2,1,0:T(8,128)S(1)}, f32[6,8,128]{2,1,0:T(8,128)S(1)}, u32[]{:S(2)}, u32[]{:S(2)}) %collective-permute-start.24) | collective-permute-done | bytes 24608 | tf_op jit(solution)/shard_map/ppermute | solution.py:37
  (66 shorter events, 20.2 us)
Async XLA Ops:
  3.6 3.6 %collective-permute-start = (bf16[6,256,512]{2,1,0:T(8,128)(2,1)S(1)}, bf16[6,256,512]{2,1,0:T(8,128)(2,1)}, u32[]{:S(2)}, u32[]{:S(2)}) collective-permute-start(bf16[6,256,512]{2,1,0:T(8,128)(2,1)S(1)} %get-tuple-element.37), channel_id=1, source_target_pairs={{0,8},{1,9},{2,10},{3,11},{4,12},{5,13},{6,14},{7,15},{8,0},{9,1},... | collective-permute-start | bytes 4718600 | tf_op jit(solution)/shard_map/ppermute | solution.py:37
  4.1 6.3 %copy-start.6 = (pred[6]{0:T(512)(128)(4,1)}, pred[6]{0:T(512)(128)(4,1)S(1)}, u32[]{:S(2)}) copy-start(pred[6]{0:T(512)(128)(4,1)S(1)} %get-tuple-element.80) | copy-start | bytes 22
  10.4 13.2 %copy-start.5 = (bf16[6,128,512]{2,1,0:T(8,128)(2,1)S(1)}, bf16[6,128,512]{2,1,0:T(8,128)(2,1)}, u32[]{:S(2)}) copy-start(bf16[6,128,512]{2,1,0:T(8,128)(2,1)} %get-tuple-element.71) | copy-start | bytes 2359300
  10.4 13.2 %collective-permute-start.2 = (bf16[6,128,512]{2,1,0:T(8,128)(2,1)}, bf16[6,128,512]{2,1,0:T(8,128)(2,1)}, u32[]{:S(2)}, u32[]{:S(2)}) collective-permute-start(bf16[6,128,512]{2,1,0:T(8,128)(2,1)} %get-tuple-element.41), channel_id=1, source_target_pairs={{0,1},{1,0},{2,3},{3,2},{4,5},{5,4},{6,7},{7,6},{8,24},{9,25},{10,... | collective-permute-start | bytes 2359304 | tf_op jit(solution)/shard_map/ppermute | solution.py:37
  16.4 9.4 %collective-permute-start.1 = (bf16[6,256,256]{2,1,0:T(8,128)(2,1)S(1)}, bf16[6,256,256]{2,1,0:T(8,128)(2,1)S(1)}, u32[]{:S(2)}, u32[]{:S(2)}) collective-permute-start(bf16[6,256,256]{2,1,0:T(8,128)(2,1)S(1)} %get-tuple-element.40), channel_id=1, source_target_pairs={{0,8},{1,9},{2,10},{3,11},{4,12},{5,13},{6,14},{7,15},{8,0},{9,1},... | collective-permute-start | bytes 2359304 | tf_op jit(solution)/shard_map/ppermute | solution.py:37
  26.8 8.1 %collective-permute-start.4 = (bf16[6,64,512]{2,1,0:T(8,128)(2,1)}, bf16[6,64,512]{2,1,0:T(8,128)(2,1)S(1)}, u32[]{:S(2)}, u32[]{:S(2)}) collective-permute-start(bf16[6,64,512]{2,1,0:T(8,128)(2,1)} %get-tuple-element.44), channel_id=1, source_target_pairs={{0,2},{1,3},{2,0},{3,1},{4,6},{5,7},{6,4},{7,5},{8,9},{9,8},{10,11... | collective-permute-start | bytes 1179656 | tf_op jit(solution)/shard_map/ppermute | solution.py:37
  29.0 8.7 %collective-permute-start.3 = (bf16[6,128,256]{2,1,0:T(8,128)(2,1)S(1)}, bf16[6,128,256]{2,1,0:T(8,128)(2,1)S(1)}, u32[]{:S(2)}, u32[]{:S(2)}) collective-permute-start(bf16[6,128,256]{2,1,0:T(8,128)(2,1)S(1)} %get-tuple-element.43), channel_id=1, source_target_pairs={{0,1},{1,0},{2,3},{3,2},{4,5},{5,4},{6,7},{7,6},{8,24},{9,25},{10,... | collective-permute-start | bytes 1179656 | tf_op jit(solution)/shard_map/ppermute | solution.py:37
  37.9 6.4 %collective-permute-start.5 = (bf16[6,64,256]{2,1,0:T(8,128)(2,1)S(1)}, bf16[6,64,256]{2,1,0:T(8,128)(2,1)S(1)}, u32[]{:S(2)}, u32[]{:S(2)}) collective-permute-start(bf16[6,64,256]{2,1,0:T(8,128)(2,1)S(1)} %get-tuple-element.47), channel_id=1, source_target_pairs={{0,2},{1,3},{2,0},{3,1},{4,6},{5,7},{6,4},{7,5},{8,9},{9,8},{10,11... | collective-permute-start | bytes 589832 | tf_op jit(solution)/shard_map/ppermute | solution.py:37
  39.7 5.7 %collective-permute-start.6 = (bf16[6,32,512]{2,1,0:T(8,128)(2,1)S(1)}, bf16[6,32,512]{2,1,0:T(8,128)(2,1)S(1)}, u32[]{:S(2)}, u32[]{:S(2)}) collective-permute-start(bf16[6,32,512]{2,1,0:T(8,128)(2,1)S(1)} %dynamic-slice_select_fusion.7), channel_id=1, source_target_pairs={{0,16},{1,17},{2,18},{3,19},{4,20},{5,21},{6,22},{7,23},{8,10},{9,... | collective-permute-start | bytes 589832 | tf_op jit(solution)/shard_map/ppermute | solution.py:37
  45.6 4.7 %collective-permute-start.7 = (bf16[6,32,256]{2,1,0:T(8,128)(2,1)S(1)}, bf16[6,32,256]{2,1,0:T(8,128)(2,1)S(1)}, u32[]{:S(2)}, u32[]{:S(2)}) collective-permute-start(bf16[6,32,256]{2,1,0:T(8,128)(2,1)S(1)} %dynamic-slice_select_fusion.9), channel_id=1, source_target_pairs={{0,16},{1,17},{2,18},{3,19},{4,20},{5,21},{6,22},{7,23},{8,10},{9,... | collective-permute-start | bytes 294920 | tf_op jit(solution)/shard_map/ppermute | solution.py:37
  47.2 10.3 %collective-permute-start.8 = (bf16[6,32,512]{2,1,0:T(8,128)(2,1)S(1)}, bf16[6,32,512]{2,1,0:T(8,128)(2,1)S(1)}, u32[]{:S(2)}, u32[]{:S(2)}) collective-permute-start(bf16[6,32,512]{2,1,0:T(8,128)(2,1)S(1)} %select_select_fusion), channel_id=1, source_target_pairs={{0,4},{1,5},{2,6},{3,7},{4,0},{5,1},{6,2},{7,3},{8,12},{9,13},{10,... | collective-permute-start | bytes 589832 | tf_op jit(solution)/shard_map/ppermute | solution.py:37
  57.6 5.9 %collective-permute-start.9 = (bf16[6,32,256]{2,1,0:T(8,128)(2,1)S(1)}, bf16[6,32,256]{2,1,0:T(8,128)(2,1)S(1)}, u32[]{:S(2)}, u32[]{:S(2)}) collective-permute-start(bf16[6,32,256]{2,1,0:T(8,128)(2,1)S(1)} %select_select_fusion.1), channel_id=1, source_target_pairs={{0,4},{1,5},{2,6},{3,7},{4,0},{5,1},{6,2},{7,3},{8,12},{9,13},{10,... | collective-permute-start | bytes 294920 | tf_op jit(solution)/shard_map/ppermute | solution.py:37
  57.7 5.9 %collective-permute-start.10 = (bf16[6,32,512]{2,1,0:T(8,128)(2,1)S(1)}, bf16[6,32,512]{2,1,0:T(8,128)(2,1)S(1)}, u32[]{:S(2)}, u32[]{:S(2)}) collective-permute-start(bf16[6,32,512]{2,1,0:T(8,128)(2,1)S(1)} %broadcast_select_fusion), channel_id=1, source_target_pairs={{0,16},{1,17},{2,18},{3,19},{4,20},{5,21},{6,22},{7,23},{8,10},{9,... | collective-permute-start | bytes 589832 | tf_op jit(solution)/shard_map/ppermute | solution.py:37
  63.6 16.4 %copy-start.2 = (f32[2048,128]{1,0:T(8,128)S(1)}, f32[2048,128]{1,0:T(8,128)}, u32[]{:S(2)}) copy-start(f32[2048,128]{1,0:T(8,128)} %norms.1) | copy-start | bytes 3145732
  63.7 16.3 %copy-start.1 = (bf16[2048,512]{1,0:T(8,128)(2,1)S(1)}, bf16[2048,512]{1,0:T(8,128)(2,1)}, u32[]{:S(2)}) copy-start(bf16[2048,512]{1,0:T(8,128)(2,1)} %points.6) | copy-start | bytes 6291460
  63.7 7.8 %collective-permute-start.12 = (bf16[6,64,512]{2,1,0:T(8,128)(2,1)S(1)}, bf16[6,64,512]{2,1,0:T(8,128)(2,1)S(1)}, u32[]{:S(2)}, u32[]{:S(2)}) collective-permute-start(bf16[6,64,512]{2,1,0:T(8,128)(2,1)S(1)} %pad_maximum_fusion.1), channel_id=1, source_target_pairs={{0,2},{1,3},{2,0},{3,1},{4,6},{5,7},{6,4},{7,5},{8,9},{9,8},{10,11... | collective-permute-start | bytes 1179656 | tf_op jit(solution)/shard_map/ppermute | solution.py:37
  65.5 4.6 %collective-permute-start.11 = (bf16[6,32,256]{2,1,0:T(8,128)(2,1)S(1)}, bf16[6,32,256]{2,1,0:T(8,128)(2,1)S(1)}, u32[]{:S(2)}, u32[]{:S(2)}) collective-permute-start(bf16[6,32,256]{2,1,0:T(8,128)(2,1)S(1)} %broadcast_select_fusion.1), channel_id=1, source_target_pairs={{0,16},{1,17},{2,18},{3,19},{4,20},{5,21},{6,22},{7,23},{8,10},{9,... | collective-permute-start | bytes 294920 | tf_op jit(solution)/shard_map/ppermute | solution.py:37
  71.6 8.4 %collective-permute-start.15 = (bf16[6,128,512]{2,1,0:T(8,128)(2,1)S(1)}, bf16[6,128,512]{2,1,0:T(8,128)(2,1)S(1)}, u32[]{:S(2)}, u32[]{:S(2)}) collective-permute-start(bf16[6,128,512]{2,1,0:T(8,128)(2,1)S(1)} %pad_maximum_fusion.mine.refs_0_), channel_id=1, source_target_pairs={{0,8},{1,9},{2,10},{3,11},{4,12},{5,13},{6,14},{7,15},{8,0},{9,1},... | collective-permute-start | bytes 2359304 | tf_op jit(solution)/shard_map/ppermute | solution.py:37
  71.7 14.7 %collective-permute-start.14 = (bf16[6,128,512]{2,1,0:T(8,128)(2,1)S(1)}, bf16[6,128,512]{2,1,0:T(8,128)(2,1)S(1)}, u32[]{:S(2)}, u32[]{:S(2)}) collective-permute-start(bf16[6,128,512]{2,1,0:T(8,128)(2,1)S(1)} %pad_maximum_fusion.mine.refs_0_), channel_id=1, source_target_pairs={{0,1},{1,0},{2,3},{3,2},{4,5},{5,4},{6,7},{7,6},{8,24},{9,25},{10,... | collective-permute-start | bytes 2359304 | tf_op jit(solution)/shard_map/ppermute | solution.py:37
  74.3 5.7 %collective-permute-start.13 = (bf16[6,64,256]{2,1,0:T(8,128)(2,1)S(1)}, bf16[6,64,256]{2,1,0:T(8,128)(2,1)S(1)}, u32[]{:S(2)}, u32[]{:S(2)}) collective-permute-start(bf16[6,64,256]{2,1,0:T(8,128)(2,1)S(1)} %pad_maximum_fusion.3), channel_id=1, source_target_pairs={{0,2},{1,3},{2,0},{3,1},{4,6},{5,7},{6,4},{7,5},{8,9},{9,8},{10,11... | collective-permute-start | bytes 589832 | tf_op jit(solution)/shard_map/ppermute | solution.py:37
  86.4 7.8 %collective-permute-start.19 = (bf16[6,128,512]{2,1,0:T(8,128)(2,1)S(1)}, bf16[6,128,512]{2,1,0:T(8,128)(2,1)S(1)}, u32[]{:S(2)}, u32[]{:S(2)}) collective-permute-start(bf16[6,128,512]{2,1,0:T(8,128)(2,1)S(1)} %collective-permute-done.14.refs_1_.mine), channel_id=1, source_target_pairs={{0,8},{1,9},{2,10},{3,11},{4,12},{5,13},{6,14},{7,15},{8,0},{9,1},... | collective-permute-start | bytes 2359304 | tf_op jit(solution)/shard_map/ppermute | solution.py:37
  86.4 7.8 %collective-permute-start.16 = (bf16[6,128,256]{2,1,0:T(8,128)(2,1)S(1)}, bf16[6,128,256]{2,1,0:T(8,128)(2,1)S(1)}, u32[]{:S(2)}, u32[]{:S(2)}) collective-permute-start(bf16[6,128,256]{2,1,0:T(8,128)(2,1)S(1)} %pad_maximum_fusion.2.refs_0_), channel_id=1, source_target_pairs={{0,1},{1,0},{2,3},{3,2},{4,5},{5,4},{6,7},{7,6},{8,24},{9,25},{10,... | collective-permute-start | bytes 1179656 | tf_op jit(solution)/shard_map/ppermute | solution.py:37
  88.2 15.7 %collective-permute-start.17 = (bf16[6,128,256]{2,1,0:T(8,128)(2,1)S(1)}, bf16[6,128,256]{2,1,0:T(8,128)(2,1)S(1)}, u32[]{:S(2)}, u32[]{:S(2)}) collective-permute-start(bf16[6,128,256]{2,1,0:T(8,128)(2,1)S(1)} %pad_maximum_fusion.2.refs_0_), channel_id=1, source_target_pairs={{0,8},{1,9},{2,10},{3,11},{4,12},{5,13},{6,14},{7,15},{8,0},{9,1},... | collective-permute-start | bytes 1179656 | tf_op jit(solution)/shard_map/ppermute | solution.py:37
  94.2 9.7 %collective-permute-start.18 = (bf16[6,128,256]{2,1,0:T(8,128)(2,1)S(1)}, bf16[6,128,256]{2,1,0:T(8,128)(2,1)S(1)}, u32[]{:S(2)}, u32[]{:S(2)}) collective-permute-start(bf16[6,128,256]{2,1,0:T(8,128)(2,1)S(1)} %collective-permute-done.16.refs_1_), channel_id=1, source_target_pairs={{0,8},{1,9},{2,10},{3,11},{4,12},{5,13},{6,14},{7,15},{8,0},{9,1},... | collective-permute-start | bytes 1179656 | tf_op jit(solution)/shard_map/ppermute | solution.py:37
  94.2 9.8 %slice-start = ((s8[6291456]{0:T(1024)(128)(4,1)}), s8[4194304]{0:T(1024)(128)(4,1)S(1)}, s32[]{:S(2)}) async-start(s8[6291456]{0:T(1024)(128)(4,1)} %bitcast), calls=%async_computation | async-start | bytes 8388608
  97.8 6.2 %copy-start = (f32[2048,256]{1,0:T(8,128)S(1)}, f32[2048,256]{1,0:T(8,128)}, u32[]{:S(2)}) copy-start(f32[2048,256]{1,0:T(8,128)} %refs_6_.1) | copy-start | bytes 6291460
  97.8 6.2 %slice-start.1 = ((s8[6291456]{0:T(1024)(128)(4,1)}), s8[2097152]{0:T(1024)(128)(4,1)S(1)}, s32[]{:S(2)}) async-start(s8[6291456]{0:T(1024)(128)(4,1)} %bitcast), calls=%async_computation.1 | async-start | bytes 4194304
  119.9 1.4 collective-permute-start.20
  121.2 3.8 %collective-permute-start.21 = (f32[6,8,128]{2,1,0:T(8,128)S(1)}, f32[6,8,128]{2,1,0:T(8,128)S(1)}, u32[]{:S(2)}, u32[]{:S(2)}) collective-permute-start(f32[6,8,128]{2,1,0:T(8,128)S(1)} %add.62), channel_id=1, source_target_pairs={{0,1},{1,0},{2,3},{3,2},{4,5},{5,4},{6,7},{7,6},{8,9},{9,8},{10,11... | collective-permute-start | bytes 73736 | tf_op jit(solution)/shard_map/ppermute | solution.py:37
  125.1 3.8 %collective-permute-start.22 = (f32[6,8,128]{2,1,0:T(8,128)S(1)}, f32[6,8,128]{2,1,0:T(8,128)S(1)}, u32[]{:S(2)}, u32[]{:S(2)}) collective-permute-start(f32[6,8,128]{2,1,0:T(8,128)S(1)} %add.63), channel_id=1, source_target_pairs={{0,2},{1,3},{2,0},{3,1},{4,6},{5,7},{6,4},{7,5},{8,10},{9,11},{10,... | collective-permute-start | bytes 73736 | tf_op jit(solution)/shard_map/ppermute | solution.py:37
  128.9 3.8 %collective-permute-start.23 = (f32[6,8,128]{2,1,0:T(8,128)S(1)}, f32[6,8,128]{2,1,0:T(8,128)S(1)}, u32[]{:S(2)}, u32[]{:S(2)}) collective-permute-start(f32[6,8,128]{2,1,0:T(8,128)S(1)} %add.64), channel_id=1, source_target_pairs={{0,16},{1,17},{2,18},{3,19},{4,20},{5,21},{6,22},{7,23},{8,24},{9,... | collective-permute-start | bytes 73736 | tf_op jit(solution)/shard_map/ppermute | solution.py:37
  132.7 4.7 %collective-permute-start.24 = (f32[6,8,128]{2,1,0:T(8,128)S(1)}, f32[6,8,128]{2,1,0:T(8,128)S(1)}, u32[]{:S(2)}, u32[]{:S(2)}) collective-permute-start(f32[6,8,128]{2,1,0:T(8,128)S(1)} %add.65), channel_id=1, source_target_pairs={{0,4},{1,5},{2,6},{3,7},{4,0},{5,1},{6,2},{7,3},{8,12},{9,13},{10,... | collective-permute-start | bytes 73736 | tf_op jit(solution)/shard_map/ppermute | solution.py:37
  (2 other events, 9.6 us)

commit v3 on v2

--- a/solution.py
+++ b/solution.py
@@ -39,12 +39,17 @@
 
 class Route:
     def __init__(self, mesh_shape, late=False):
+        self.mesh_shape = mesh_shape
+        self.blocks = mesh_shape.get("blocks", 1)
         self.devices = mesh_shape["row"] * mesh_shape["col"]
         self.core, self.orders = stage_bits(mesh_shape, late)
         self.stages = len(self.orders[0])
         self.halvings = min(HALVINGS, self.stages)
         self.here = lax.axis_index("row") * mesh_shape["col"] + lax.axis_index("col")
         self.side = (self.here >> self.core) & 1
+
+    def owner(self, block):
+        return lax.div(block, self.blocks)
 
     def swap_core(self, x):
         return swap(x, self.devices, lambda i: self.core)
@@ -69,7 +74,7 @@
                 pieces.append(row)
         return pieces
 
-    def spread(self, send, keep, owner):
+    def spread(self, send, keep, plan, owner):
         recv, = yield (self.swap_core, send),
         mine = keep
         same = ((owner >> self.core) & 1) == self.side
@@ -84,7 +89,10 @@
                     lax.dynamic_slice_in_dim(recv, which * rows, rows, 1),
                 )
 
-            going, staying = half(1 - bit), half(bit)
+            if k < 2 and mine.shape[2] > 256:
+                going, staying = halve(self.mesh_shape, k, plan, mine, recv)
+            else:
+                going, staying = half(1 - bit), half(bit)
             recv, = yield (functools.partial(self.swap_stage, k=k), going),
             mine = staying
             same = self.bit(owner, k) == bit
@@ -132,12 +140,14 @@
         return others
 
 
-def together(*streams):
-    sends = lax.optimization_barrier(tuple(s.sends for s in streams))
-    for stream, ready in zip(streams, sends):
-        stream.sends = ready
-    for stream in streams:
-        stream.go()
+def together(lead, trail, before):
+    if before is not None:
+        lead.sends, _ = lax.optimization_barrier((lead.sends, before))
+    trail.sends, _ = lax.optimization_barrier((trail.sends, lead.sends))
+    before = trail.sends
+    lead.go()
+    trail.go()
+    return before
 
 
 def block_offset(plan, r, here, rows, size):
@@ -168,6 +178,41 @@
         scratch_shapes=[pltpu.SemaphoreType.DMA((2 * plan.shape[0],))],
         name="pick_points",
     )(plan, points)
+
+
+def halve_kernel(mesh_shape, k, plan, mine, recv, going, staying):
+    slots, rows, _ = going.shape
+    route = Route(mesh_shape)
+    bit = route.bit(route.here, k)
+    for r in range(slots):
+        owner = route.owner(plan[r])
+        if k == 0:
+            same = ((owner >> route.core) & 1) == route.side
+        else:
+            same = route.bit(owner, k - 1) == route.bit(route.here, k - 1)
+        for dst, which in ((going, 1 - bit), (staying, bit)):
+            part = pl.ds(pl.multiple_of(which * rows, rows), rows)
+
+            @pl.when(same)
+            def _():
+                dst[r] = mine[r, part, :]
+
+            @pl.when(jnp.logical_not(same))
+            def _():
+                dst[r] = recv[r, part, :]
+
+
+def halve(mesh_shape, k, plan, mine, recv):
+    slots, rows, width = recv.shape
+    part = jax.ShapeDtypeStruct((slots, rows // 2, width), recv.dtype)
+    return pl.pallas_call(
+        functools.partial(halve_kernel, mesh_shape, k),
+        out_shape=(part, part),
+        in_specs=[SMEM, VMEM, VMEM],
+        out_specs=(VMEM, VMEM),
+        compiler_params=pltpu.CompilerParams(vmem_limit_bytes=8 * MIB),
+        name="halve",
+    )(plan, mine, recv)
 
 
 def pick_targets_kernel(mesh_shape, plan, targets, going, staying, landing, sems):
@@ -332,13 +377,11 @@
             value = value - jnp.dot(among[first + s], steps[s], preferred_element_type=jnp.float32)
             value = value - jnp.where(plan[s] == plan[r], RIDGE * wide[s], 0.0)
         top = value.astype(jnp.bfloat16)
-        bottom = (value - top.astype(jnp.float32)).astype(jnp.bfloat16)
         matrix = inverse[r]
         high = matrix.astype(jnp.bfloat16)
         low = (matrix - high.astype(jnp.float32)).astype(jnp.bfloat16)
         step = jnp.dot(high, top, preferred_element_type=jnp.float32)
         step = step + jnp.dot(low, top, preferred_element_type=jnp.float32)
-        step = step + jnp.dot(high, bottom, preferred_element_type=jnp.float32)
         wide[r] = step
         steps[r] = step.astype(jnp.bfloat16)
         for j, q in enumerate((0, 2, 1, 3)):
@@ -389,6 +432,7 @@
     rows, features = points.shape
     width = targets.shape[1]
     size = block_inverse.shape[1]
+    mesh_shape = dict(mesh_shape, blocks=rows // size)
     route = Route(mesh_shape)
     total = rows * route.devices * width
     gamma = 2.0 / features
@@ -397,14 +441,15 @@
 
     owner = plan * size // rows
 
-    lead = Stream(route.spread(*pick_points(mesh_shape, plan, points, size), owner))
+    lead = Stream(route.spread(*pick_points(mesh_shape, plan, points, size), plan, owner))
     trail = None
+    before = None
     tall_a = None
     stage = 0
     while lead.result is None:
         if stage == 1:
             held, = lead.after(targets)
-            trail = Stream(route.spread(*pick_targets(mesh_shape, plan, held, size), owner))
+            trail = Stream(route.spread(*pick_targets(mesh_shape, plan, held, size), plan, owner))
         if stage == 2:
             held, = lead.after(points)
             norms = point_norms(held, norm_scale)
@@ -419,18 +464,15 @@
             lead.go()
             trail.go()
         else:
-            together(lead, trail)
+            before = together(lead, trail, before)
         stage += 1
     (first_mine, last_mine), (first_other, last_other) = lead.result
 
+    tall_b = tall_matrices(points, norms, last_mine, last_other, norm_scale, inner_scale)
     if trail.result is None:
-        last_mine, = trail.after(last_mine)
-    tall_b = tall_matrices(points, norms, last_mine, last_other, norm_scale, inner_scale)
+        tall_b, = trail.after(tall_b)
+        trail.go()
     ready = (first_mine, last_mine, first_other, last_other)
-    if trail.result is None:
-        trail.go()
-        if trail.result is None:
-            tall_b, ready = trail.after(tall_b, ready)
     among = among_matrices(mesh_shape, ready, norm_scale, inner_scale)
     while trail.result is None:
         trail.go()

time: 139 us -> 128 us (0.921)
  waiting for transfers between devices: 59.6 us -> 50.9 us
  other arithmetic: 8.04 us -> 3.09 us
    ppermute x25, waiting for transfers between devices: 59.6 us -> 50.9 us  [swap(): lax.ppermute(x, AXES, [(i, i ^ 1 << bit_of(i)) for i in range(devices)])]
    select_n x6 -> x4, other arithmetic: 6.75 us -> 1.83 us  [half(): jnp.where(same[:, None, None], lax.dynamic_slice_in_dim(mine, which * row...]
    pallas_call x0 -> x2, Pallas kernels: none -> 2.38 us  [halve(): pl.pallas_call(functools.partial(halve_kernel, mesh_shape, k), out_shape=...]
    pallas_call x1, Pallas kernels: 15.9 us -> 14.1 us  [solve(): pl.pallas_call(functools.partial(solve_kernel, mesh_shape), out_shape=(ja...]
  transfers between devices with their start and end apart: 25 -> 25, of which waited for: 19 -> 20; matrix products, arithmetic and copies ran while one was open for 2% -> 2% of each run, Pallas kernels for 14% -> 16%
where the time goes in v3:
time: 128 us; the launch traced here: 127 us
  waiting for transfers between devices  50.9 us (40%)
  Pallas kernels  39.1 us (31%)
  starting transfers between devices  32.5 us (25%)
  other arithmetic  3.09 us (2%)
    ppermute x25, waiting for transfers between devices, swap(): lax.ppermute(x, AXES, [(i, i ^ 1 << bit_of(i)) for i in range(devices)])  50.9 us
    ppermute x25, starting transfers between devices, swap(): lax.ppermute(x, AXES, [(i, i ^ 1 << bit_of(i)) for i in range(devices)])  32.5 us
    pallas_call x1, Pallas kernels, solve(): pl.pallas_call(functools.partial(solve_kernel, mesh_shape), out_shape=(ja...  14.1 us
    pallas_call x2, Pallas kernels, tall_matrices(): pl.pallas_call(functools.partial(tall_kernel, norm_scale, scale), out_sha...  7.17 us
    pallas_call x1, Pallas kernels, among_matrices(): pl.pallas_call(functools.partial(among_kernel, mesh_shape, norm_scale, sc...  6.04 us
    pallas_call x1, Pallas kernels, pick_targets(): pl.pallas_call(functools.partial(pick_targets_kernel, mesh_shape), out_sh...  3.95 us
    pallas_call x1, Pallas kernels, pick_points(): pl.pallas_call(functools.partial(pick_points_kernel, mesh_shape), out_sha...  2.95 us
    pallas_call x1, Pallas kernels, point_norms(): pl.pallas_call(functools.partial(norms_kernel, scale), out_shape=jax.Shap...  2.61 us
  transfers between devices with their start and end apart: 25, of which 20 were waited for; matrix products, arithmetic and copies ran while one was open for 2% of the time, Pallas kernels for 16%

profile of v3, /device:TPU:0, one launch (start us, length us, event | category | flops | bytes accessed | tf_op | source)
XLA Modules:
  0.0 127.4 jit_solution(1763648546501796986)
XLA Ops:
  0.6 2.9 %pick_points.1 = (bf16[6,256,512]{2,1,0:T(8,128)(2,1)S(1)}, bf16[6,256,512]{2,1,0:T(8,128)(2,1)S(1)}) custom-call(s32[6]{0:T(128)} %plan.9, bf16[2048,512]{1,0:T(8,128)(2,1)} %points.6), custom_call_target="tpu_custom_call" | custom-call | tf_op jit(solution)/shard_map/pick_points/pallas_call | solution.py:173
  4.1 3.0 %collective-permute-done.recv = bf16[6,256,512]{2,1,0:T(8,128)(2,1)S(1)} collective-permute-done((bf16[6,256,512]{2,1,0:T(8,128)(2,1)S(1)}, bf16[6,256,512]{2,1,0:T(8,128)(2,1)S(1)}, u32[]{:S(2)}, u32[]{:S(2)}) %collective-permute-start) | collective-permute-done | bytes 1572896 | tf_op jit(solution)/shard_map/ppermute | solution.py:37
  7.1 1.7 %halve.2 = (bf16[6,128,512]{2,1,0:T(8,128)(2,1)}, bf16[6,128,512]{2,1,0:T(8,128)(2,1)S(1)}) custom-call(s32[6]{0:T(128)S(1)} %copy-done.5, bf16[6,256,512]{2,1,0:T(8,128)(2,1)S(1)} %get-tuple-element.39.mine, bf16[6,256,512]{2,1,0:T(8,128)(2,1)S(1)} %collective-permute-done.recv), custom_call_target="tpu_custom_call" | custom-call | tf_op jit(solution)/shard_map/halve/pallas_call | solution.py:208
  9.6 2.9 %collective-permute-start.2 = (bf16[6,128,512]{2,1,0:T(8,128)(2,1)}, bf16[6,128,512]{2,1,0:T(8,128)(2,1)S(1)}, u32[]{:S(2)}, u32[]{:S(2)}) collective-permute-start(bf16[6,128,512]{2,1,0:T(8,128)(2,1)} %get-tuple-element.46), channel_id=1, source_target_pairs={{0,1},{1,0},{2,3},{3,2},{4,5},{5,4},{6,7},{7,6},{8,24},{9,25},{10,... | collective-permute-start | bytes 2359304 | tf_op jit(solution)/shard_map/ppermute | solution.py:37
  12.5 3.9 %pick_targets.1 = (bf16[6,256,256]{2,1,0:T(8,128)(2,1)}, bf16[6,256,256]{2,1,0:T(8,128)(2,1)S(1)}) custom-call(s32[6]{0:T(128)} %plan.9, f32[2048,256]{1,0:T(8,128)} %refs_6_.1), custom_call_target="tpu_custom_call" | custom-call | tf_op jit(solution)/shard_map/pick_targets/pallas_call | solution.py:238
  16.7 6.1 %collective-permute-done.2.recv = bf16[6,128,512]{2,1,0:T(8,128)(2,1)S(1)} collective-permute-done((bf16[6,128,512]{2,1,0:T(8,128)(2,1)}, bf16[6,128,512]{2,1,0:T(8,128)(2,1)S(1)}, u32[]{:S(2)}, u32[]{:S(2)}) %collective-permute-start.2) | collective-permute-done | bytes 786464 | tf_op jit(solution)/shard_map/ppermute | solution.py:37
  23.5 2.2 %collective-permute-start.4 = (bf16[6,64,512]{2,1,0:T(8,128)(2,1)S(1)}, bf16[6,64,512]{2,1,0:T(8,128)(2,1)S(1)}, u32[]{:S(2)}, u32[]{:S(2)}) collective-permute-start(bf16[6,64,512]{2,1,0:T(8,128)(2,1)S(1)} %get-tuple-element.48), channel_id=1, source_target_pairs={{0,2},{1,3},{2,0},{3,1},{4,6},{5,7},{6,4},{7,5},{8,9},{9,8},{10,11... | collective-permute-start | bytes 1179656 | tf_op jit(solution)/shard_map/ppermute | solution.py:37
  25.6 1.4 %dynamic-slice_select_fusion.1 = (bf16[6,128,256]{2,1,0:T(8,128)(2,1)S(1)}, bf16[6,128,256]{2,1,0:T(8,128)(2,1)S(1)}) fusion(bf16[6,256,256]{2,1,0:T(8,128)(2,1)} %collective-permute-done.1, s32[]{:T(128)S(6)} %select_n.119, bf16[6,256,256]{2,1,0:T(8,128)(2,1)S(1)} %get-tuple-element.43, pred[6]{0:T(512)(128)(4,1)S(1)} %get-tuple-element.82, s32[]{:T(128)S(6)} %select_n.122), kind=kLoop, calls=%fused_computation.4 | loop fusion | flops 393216 | bytes 2359310 | tf_op jit(solution)/shard_map/jit(_where)/select_n | solution.py:86
  27.1 1.6 %collective-permute-start.3 = (bf16[6,128,256]{2,1,0:T(8,128)(2,1)S(1)}, bf16[6,128,256]{2,1,0:T(8,128)(2,1)S(1)}, u32[]{:S(2)}, u32[]{:S(2)}) collective-permute-start(bf16[6,128,256]{2,1,0:T(8,128)(2,1)S(1)} %get-tuple-element.49), channel_id=1, source_target_pairs={{0,1},{1,0},{2,3},{3,2},{4,5},{5,4},{6,7},{7,6},{8,24},{9,25},{10,... | collective-permute-start | bytes 1179656 | tf_op jit(solution)/shard_map/ppermute | solution.py:37
  28.6 2.6 %norms.1 = f32[2048,128]{1,0:T(8,128)} custom-call(bf16[2048,512]{1,0:T(8,128)(2,1)} %points.6), custom_call_target="tpu_custom_call" | custom-call | bytes 6291456 | tf_op jit(solution)/shard_map/norms/pallas_call | solution.py:264
  31.5 2.1 %collective-permute-start.6 = (bf16[6,32,512]{2,1,0:T(8,128)(2,1)S(1)}, bf16[6,32,512]{2,1,0:T(8,128)(2,1)S(1)}, u32[]{:S(2)}, u32[]{:S(2)}) collective-permute-start(bf16[6,32,512]{2,1,0:T(8,128)(2,1)S(1)} %dynamic-slice_select_fusion.2), channel_id=1, source_target_pairs={{0,16},{1,17},{2,18},{3,19},{4,20},{5,21},{6,22},{7,23},{8,10},{9,... | collective-permute-start | bytes 589832 | tf_op jit(solution)/shard_map/ppermute | solution.py:37
  37.5 3.0 %collective-permute-start.8 = (bf16[6,32,512]{2,1,0:T(8,128)(2,1)S(1)}, bf16[6,32,512]{2,1,0:T(8,128)(2,1)S(1)}, u32[]{:S(2)}, u32[]{:S(2)}) collective-permute-start(bf16[6,32,512]{2,1,0:T(8,128)(2,1)S(1)} %select_select_fusion), channel_id=1, source_target_pairs={{0,4},{1,5},{2,6},{3,7},{4,0},{5,1},{6,2},{7,3},{8,12},{9,13},{10,... | collective-permute-start | bytes 589832 | tf_op jit(solution)/shard_map/ppermute | solution.py:37
  40.5 4.5 %collective-permute-done.5 = bf16[6,64,256]{2,1,0:T(8,128)(2,1)S(1)} collective-permute-done((bf16[6,64,256]{2,1,0:T(8,128)(2,1)S(1)}, bf16[6,64,256]{2,1,0:T(8,128)(2,1)S(1)}, u32[]{:S(2)}, u32[]{:S(2)}) %collective-permute-start.5) | collective-permute-done | bytes 196640 | tf_op jit(solution)/shard_map/ppermute | solution.py:37
  45.1 2.4 %collective-permute-start.7 = (bf16[6,32,256]{2,1,0:T(8,128)(2,1)S(1)}, bf16[6,32,256]{2,1,0:T(8,128)(2,1)S(1)}, u32[]{:S(2)}, u32[]{:S(2)}) collective-permute-start(bf16[6,32,256]{2,1,0:T(8,128)(2,1)S(1)} %dynamic-slice_select_fusion.5), channel_id=1, source_target_pairs={{0,16},{1,17},{2,18},{3,19},{4,20},{5,21},{6,22},{7,23},{8,10},{9,... | collective-permute-start | bytes 294920 | tf_op jit(solution)/shard_map/ppermute | solution.py:37
  48.5 1.7 %collective-permute-done.7 = bf16[6,32,256]{2,1,0:T(8,128)(2,1)S(1)} collective-permute-done((bf16[6,32,256]{2,1,0:T(8,128)(2,1)S(1)}, bf16[6,32,256]{2,1,0:T(8,128)(2,1)S(1)}, u32[]{:S(2)}, u32[]{:S(2)}) %collective-permute-start.7) | collective-permute-done | bytes 98336 | tf_op jit(solution)/shard_map/ppermute | solution.py:37
  50.3 3.7 %collective-permute-done.10 = bf16[6,32,512]{2,1,0:T(8,128)(2,1)S(1)} collective-permute-done((bf16[6,32,512]{2,1,0:T(8,128)(2,1)S(1)}, bf16[6,32,512]{2,1,0:T(8,128)(2,1)S(1)}, u32[]{:S(2)}, u32[]{:S(2)}) %collective-permute-start.10) | collective-permute-done | bytes 196640 | tf_op jit(solution)/shard_map/ppermute | solution.py:37
  54.6 3.1 %collective-permute-start.9 = (bf16[6,32,256]{2,1,0:T(8,128)(2,1)S(1)}, bf16[6,32,256]{2,1,0:T(8,128)(2,1)S(1)}, u32[]{:S(2)}, u32[]{:S(2)}) collective-permute-start(bf16[6,32,256]{2,1,0:T(8,128)(2,1)S(1)} %select_select_fusion.1), channel_id=1, source_target_pairs={{0,4},{1,5},{2,6},{3,7},{4,0},{5,1},{6,2},{7,3},{8,12},{9,13},{10,... | collective-permute-start | bytes 294920 | tf_op jit(solution)/shard_map/ppermute | solution.py:37
  57.7 4.0 %collective-permute-done.9 = bf16[6,32,256]{2,1,0:T(8,128)(2,1)S(1)} collective-permute-done((bf16[6,32,256]{2,1,0:T(8,128)(2,1)S(1)}, bf16[6,32,256]{2,1,0:T(8,128)(2,1)S(1)}, u32[]{:S(2)}, u32[]{:S(2)}) %collective-permute-start.9) | collective-permute-done | bytes 98336 | tf_op jit(solution)/shard_map/ppermute | solution.py:37
  65.4 4.8 %collective-permute-done.11 = bf16[6,32,256]{2,1,0:T(8,128)(2,1)S(1)} collective-permute-done((bf16[6,32,256]{2,1,0:T(8,128)(2,1)S(1)}, bf16[6,32,256]{2,1,0:T(8,128)(2,1)S(1)}, u32[]{:S(2)}, u32[]{:S(2)}) %collective-permute-start.11) | collective-permute-done | bytes 98336 | tf_op jit(solution)/shard_map/ppermute | solution.py:37
  70.2 3.6 %tall.2.refs_7_ = bf16[6,2048,256]{2,1,0:T(8,128)(2,1)S(1)} custom-call(bf16[6,128,512]{2,1,0:T(8,128)(2,1)S(1)} %pad_maximum_fusion.mine.refs_0_, bf16[6,128,512]{2,1,0:T(8,128)(2,1)S(1)} %collective-permute-done.15.other.refs_2_, bf16[2048,512]{1,0:T(8,128)(2,1)S(1)} %copy-done.1, f32[2048,128]{1,0:T(8,128)S(1)} %copy-done.2), custom_call_target="tpu_custom_call" | custom-call | flops 3221225472 | bytes 12582912 | tf_op jit(solution)/shard_map/tall/pallas_call | solution.py:295
  75.5 1.7 %collective-permute-start.13 = (bf16[6,64,256]{2,1,0:T(8,128)(2,1)S(1)}, bf16[6,64,256]{2,1,0:T(8,128)(2,1)S(1)}, u32[]{:S(2)}, u32[]{:S(2)}) collective-permute-start(bf16[6,64,256]{2,1,0:T(8,128)(2,1)S(1)} %pad_maximum_fusion.3), channel_id=1, source_target_pairs={{0,2},{1,3},{2,0},{3,1},{4,6},{5,7},{6,4},{7,5},{8,9},{9,8},{10,11... | collective-permute-start | bytes 589832 | tf_op jit(solution)/shard_map/ppermute | solution.py:37
  77.1 4.0 %collective-permute-done.13 = bf16[6,64,256]{2,1,0:T(8,128)(2,1)S(1)} collective-permute-done((bf16[6,64,256]{2,1,0:T(8,128)(2,1)S(1)}, bf16[6,64,256]{2,1,0:T(8,128)(2,1)S(1)}, u32[]{:S(2)}, u32[]{:S(2)}) %collective-permute-start.13) | collective-permute-done | bytes 196640 | tf_op jit(solution)/shard_map/ppermute | solution.py:37
  82.6 3.6 %tall.3.refs_8_ = bf16[6,2048,256]{2,1,0:T(8,128)(2,1)S(1)} custom-call(bf16[6,128,512]{2,1,0:T(8,128)(2,1)S(1)} %collective-permute-done.14.mine.refs_1_, bf16[6,128,512]{2,1,0:T(8,128)(2,1)S(1)} %collective-permute-done.18.other.refs_3_, bf16[2048,512]{1,0:T(8,128)(2,1)S(1)} %copy-done.1, f32[2048,128]{1,0:T(8,128)S(1)} %copy-done.2), custom_call_target="tpu_custom_call" | custom-call | flops 3221225472 | bytes 12582912 | tf_op jit(solution)/shard_map/tall/pallas_call | solution.py:295
  86.2 2.8 %collective-permute-done.16.refs_1_ = bf16[6,128,256]{2,1,0:T(8,128)(2,1)S(1)} collective-permute-done((bf16[6,128,256]{2,1,0:T(8,128)(2,1)S(1)}, bf16[6,128,256]{2,1,0:T(8,128)(2,1)S(1)}, u32[]{:S(2)}, u32[]{:S(2)}) %collective-permute-start.16) | collective-permute-done | bytes 393248 | tf_op jit(solution)/shard_map/ppermute | solution.py:37
  89.0 6.0 %among.1.refs_5_ = bf16[15,512,512]{2,1,0:T(8,128)(2,1)S(1)} custom-call(bf16[6,128,512]{2,1,0:T(8,128)(2,1)S(1)} %pad_maximum_fusion.mine.refs_0_, bf16[6,128,512]{2,1,0:T(8,128)(2,1)S(1)} %collective-permute-done.14.mine.refs_1_, bf16[6,128,512]{2,1,0:T(8,128)(2,1)S(1)} %collective-permute-done.15.other.refs_2_, ...), custom_call_target="tpu_custom_call" | custom-call | flops 4026531840 | bytes 15728640 | tf_op jit(solution)/shard_map/among/pallas_call | solution.py:335
  95.1 14.1 %solve.1 = (f32[2048,256]{1,0:T(8,128)}, bf16[6,512,256]{2,1,0:T(8,128)(2,1)}, f32[6,8,128]{2,1,0:T(8,128)S(1)}) custom-call(s32[6]{0:T(128)S(1)} %copy-done.6, bf16[6,128,256]{2,1,0:T(8,128)(2,1)S(1)} %pad_maximum_fusion.2.refs_0_, bf16[6,128,256]{2,1,0:T(8,128)(2,1)S(1)} %collective-permute-done.16.refs_1_, ...), custom_call_target="tpu_custom_call" | custom-call | tf_op jit(solution)/shard_map/solve/pallas_call | solution.py:412
  111.9 2.5 %collective-permute-done.21 = f32[6,8,128]{2,1,0:T(8,128)S(1)} collective-permute-done((f32[6,8,128]{2,1,0:T(8,128)S(1)}, f32[6,8,128]{2,1,0:T(8,128)S(1)}, u32[]{:S(2)}, u32[]{:S(2)}) %collective-permute-start.21) | collective-permute-done | bytes 24608 | tf_op jit(solution)/shard_map/ppermute | solution.py:37
  114.4 1.7 %collective-permute-start.22 = (f32[6,8,128]{2,1,0:T(8,128)S(1)}, f32[6,8,128]{2,1,0:T(8,128)S(1)}, u32[]{:S(2)}, u32[]{:S(2)}) collective-permute-start(f32[6,8,128]{2,1,0:T(8,128)S(1)} %add.55), channel_id=1, source_target_pairs={{0,2},{1,3},{2,0},{3,1},{4,6},{5,7},{6,4},{7,5},{8,10},{9,11},{10,... | collective-permute-start | bytes 73736 | tf_op jit(solution)/shard_map/ppermute | solution.py:37
  116.0 2.2 %collective-permute-done.22 = f32[6,8,128]{2,1,0:T(8,128)S(1)} collective-permute-done((f32[6,8,128]{2,1,0:T(8,128)S(1)}, f32[6,8,128]{2,1,0:T(8,128)S(1)}, u32[]{:S(2)}, u32[]{:S(2)}) %collective-permute-start.22) | collective-permute-done | bytes 24608 | tf_op jit(solution)/shard_map/ppermute | solution.py:37
  119.6 2.4 %collective-permute-done.23 = f32[6,8,128]{2,1,0:T(8,128)S(1)} collective-permute-done((f32[6,8,128]{2,1,0:T(8,128)S(1)}, f32[6,8,128]{2,1,0:T(8,128)S(1)}, u32[]{:S(2)}, u32[]{:S(2)}) %collective-permute-start.23) | collective-permute-done | bytes 24608 | tf_op jit(solution)/shard_map/ppermute | solution.py:37
  122.1 2.3 %collective-permute-start.24 = (f32[6,8,128]{2,1,0:T(8,128)S(1)}, f32[6,8,128]{2,1,0:T(8,128)S(1)}, u32[]{:S(2)}, u32[]{:S(2)}) collective-permute-start(f32[6,8,128]{2,1,0:T(8,128)S(1)} %add.57), channel_id=1, source_target_pairs={{0,4},{1,5},{2,6},{3,7},{4,0},{5,1},{6,2},{7,3},{8,12},{9,13},{10,... | collective-permute-start | bytes 73736 | tf_op jit(solution)/shard_map/ppermute | solution.py:37
  124.3 2.5 %collective-permute-done.24 = f32[6,8,128]{2,1,0:T(8,128)S(1)} collective-permute-done((f32[6,8,128]{2,1,0:T(8,128)S(1)}, f32[6,8,128]{2,1,0:T(8,128)S(1)}, u32[]{:S(2)}, u32[]{:S(2)}) %collective-permute-start.24) | collective-permute-done | bytes 24608 | tf_op jit(solution)/shard_map/ppermute | solution.py:37
  (66 shorter events, 19.4 us)
Async XLA Ops:
  3.6 3.5 %collective-permute-start = (bf16[6,256,512]{2,1,0:T(8,128)(2,1)S(1)}, bf16[6,256,512]{2,1,0:T(8,128)(2,1)S(1)}, u32[]{:S(2)}, u32[]{:S(2)}) collective-permute-start(bf16[6,256,512]{2,1,0:T(8,128)(2,1)S(1)} %get-tuple-element.40), channel_id=1, source_target_pairs={{0,8},{1,9},{2,10},{3,11},{4,12},{5,13},{6,14},{7,15},{8,0},{9,1},... | collective-permute-start | bytes 4718600 | tf_op jit(solution)/shard_map/ppermute | solution.py:37
  9.6 7.0 %copy-start.6 = (s32[6]{0:T(128)S(1)}, s32[6]{0:T(128)}, u32[]{:S(2)}) copy-start(s32[6]{0:T(128)} %plan.9) | copy-start | bytes 76
  9.6 13.1 %copy-start.4 = (bf16[6,128,512]{2,1,0:T(8,128)(2,1)S(1)}, bf16[6,128,512]{2,1,0:T(8,128)(2,1)}, u32[]{:S(2)}) copy-start(bf16[6,128,512]{2,1,0:T(8,128)(2,1)} %copy-done.3) | copy-start | bytes 2359300
  9.6 13.1 %collective-permute-start.2 = (bf16[6,128,512]{2,1,0:T(8,128)(2,1)}, bf16[6,128,512]{2,1,0:T(8,128)(2,1)S(1)}, u32[]{:S(2)}, u32[]{:S(2)}) collective-permute-start(bf16[6,128,512]{2,1,0:T(8,128)(2,1)} %get-tuple-element.46), channel_id=1, source_target_pairs={{0,1},{1,0},{2,3},{3,2},{4,5},{5,4},{6,7},{7,6},{8,24},{9,25},{10,... | collective-permute-start | bytes 2359304 | tf_op jit(solution)/shard_map/ppermute | solution.py:37
  16.5 9.1 %collective-permute-start.1 = (bf16[6,256,256]{2,1,0:T(8,128)(2,1)}, bf16[6,256,256]{2,1,0:T(8,128)(2,1)}, u32[]{:S(2)}, u32[]{:S(2)}) collective-permute-start(bf16[6,256,256]{2,1,0:T(8,128)(2,1)} %get-tuple-element.44), channel_id=1, source_target_pairs={{0,8},{1,9},{2,10},{3,11},{4,12},{5,13},{6,14},{7,15},{8,0},{9,1},... | collective-permute-start | bytes 2359304 | tf_op jit(solution)/shard_map/ppermute | solution.py:37
  23.5 7.9 %collective-permute-start.4 = (bf16[6,64,512]{2,1,0:T(8,128)(2,1)S(1)}, bf16[6,64,512]{2,1,0:T(8,128)(2,1)S(1)}, u32[]{:S(2)}, u32[]{:S(2)}) collective-permute-start(bf16[6,64,512]{2,1,0:T(8,128)(2,1)S(1)} %get-tuple-element.48), channel_id=1, source_target_pairs={{0,2},{1,3},{2,0},{3,1},{4,6},{5,7},{6,4},{7,5},{8,9},{9,8},{10,11... | collective-permute-start | bytes 1179656 | tf_op jit(solution)/shard_map/ppermute | solution.py:37
  27.1 7.8 %collective-permute-start.3 = (bf16[6,128,256]{2,1,0:T(8,128)(2,1)S(1)}, bf16[6,128,256]{2,1,0:T(8,128)(2,1)S(1)}, u32[]{:S(2)}, u32[]{:S(2)}) collective-permute-start(bf16[6,128,256]{2,1,0:T(8,128)(2,1)S(1)} %get-tuple-element.49), channel_id=1, source_target_pairs={{0,1},{1,0},{2,3},{3,2},{4,5},{5,4},{6,7},{7,6},{8,24},{9,25},{10,... | collective-permute-start | bytes 1179656 | tf_op jit(solution)/shard_map/ppermute | solution.py:37
  31.5 5.8 %collective-permute-start.6 = (bf16[6,32,512]{2,1,0:T(8,128)(2,1)S(1)}, bf16[6,32,512]{2,1,0:T(8,128)(2,1)S(1)}, u32[]{:S(2)}, u32[]{:S(2)}) collective-permute-start(bf16[6,32,512]{2,1,0:T(8,128)(2,1)S(1)} %dynamic-slice_select_fusion.2), channel_id=1, source_target_pairs={{0,16},{1,17},{2,18},{3,19},{4,20},{5,21},{6,22},{7,23},{8,10},{9,... | collective-permute-start | bytes 589832 | tf_op jit(solution)/shard_map/ppermute | solution.py:37
  35.1 9.9 %collective-permute-start.5 = (bf16[6,64,256]{2,1,0:T(8,128)(2,1)S(1)}, bf16[6,64,256]{2,1,0:T(8,128)(2,1)S(1)}, u32[]{:S(2)}, u32[]{:S(2)}) collective-permute-start(bf16[6,64,256]{2,1,0:T(8,128)(2,1)S(1)} %get-tuple-element.54), channel_id=1, source_target_pairs={{0,2},{1,3},{2,0},{3,1},{4,6},{5,7},{6,4},{7,5},{8,9},{9,8},{10,11... | collective-permute-start | bytes 589832 | tf_op jit(solution)/shard_map/ppermute | solution.py:37
  37.5 10.7 %collective-permute-start.8 = (bf16[6,32,512]{2,1,0:T(8,128)(2,1)S(1)}, bf16[6,32,512]{2,1,0:T(8,128)(2,1)S(1)}, u32[]{:S(2)}, u32[]{:S(2)}) collective-permute-start(bf16[6,32,512]{2,1,0:T(8,128)(2,1)S(1)} %select_select_fusion), channel_id=1, source_target_pairs={{0,4},{1,5},{2,6},{3,7},{4,0},{5,1},{6,2},{7,3},{8,12},{9,13},{10,... | collective-permute-start | bytes 589832 | tf_op jit(solution)/shard_map/ppermute | solution.py:37
  45.1 5.0 %collective-permute-start.7 = (bf16[6,32,256]{2,1,0:T(8,128)(2,1)S(1)}, bf16[6,32,256]{2,1,0:T(8,128)(2,1)S(1)}, u32[]{:S(2)}, u32[]{:S(2)}) collective-permute-start(bf16[6,32,256]{2,1,0:T(8,128)(2,1)S(1)} %dynamic-slice_select_fusion.5), channel_id=1, source_target_pairs={{0,16},{1,17},{2,18},{3,19},{4,20},{5,21},{6,22},{7,23},{8,10},{9,... | collective-permute-start | bytes 294920 | tf_op jit(solution)/shard_map/ppermute | solution.py:37
  48.3 5.7 %collective-permute-start.10 = (bf16[6,32,512]{2,1,0:T(8,128)(2,1)S(1)}, bf16[6,32,512]{2,1,0:T(8,128)(2,1)S(1)}, u32[]{:S(2)}, u32[]{:S(2)}) collective-permute-start(bf16[6,32,512]{2,1,0:T(8,128)(2,1)S(1)} %broadcast_select_fusion), channel_id=1, source_target_pairs={{0,16},{1,17},{2,18},{3,19},{4,20},{5,21},{6,22},{7,23},{8,10},{9,... | collective-permute-start | bytes 589832 | tf_op jit(solution)/shard_map/ppermute | solution.py:37
  50.2 20.1 %copy-start.2 = (f32[2048,128]{1,0:T(8,128)S(1)}, f32[2048,128]{1,0:T(8,128)}, u32[]{:S(2)}) copy-start(f32[2048,128]{1,0:T(8,128)} %norms.1) | copy-start | bytes 3145732
  50.3 20.0 %copy-start.1 = (bf16[2048,512]{1,0:T(8,128)(2,1)S(1)}, bf16[2048,512]{1,0:T(8,128)(2,1)}, u32[]{:S(2)}) copy-start(bf16[2048,512]{1,0:T(8,128)(2,1)} %points.6) | copy-start | bytes 6291460
  54.1 8.9 %collective-permute-start.12 = (bf16[6,64,512]{2,1,0:T(8,128)(2,1)S(1)}, bf16[6,64,512]{2,1,0:T(8,128)(2,1)S(1)}, u32[]{:S(2)}, u32[]{:S(2)}) collective-permute-start(bf16[6,64,512]{2,1,0:T(8,128)(2,1)S(1)} %pad_maximum_fusion.1), channel_id=1, source_target_pairs={{0,2},{1,3},{2,0},{3,1},{4,6},{5,7},{6,4},{7,5},{8,9},{9,8},{10,11... | collective-permute-start | bytes 1179656 | tf_op jit(solution)/shard_map/ppermute | solution.py:37
  54.6 7.1 %collective-permute-start.9 = (bf16[6,32,256]{2,1,0:T(8,128)(2,1)S(1)}, bf16[6,32,256]{2,1,0:T(8,128)(2,1)S(1)}, u32[]{:S(2)}, u32[]{:S(2)}) collective-permute-start(bf16[6,32,256]{2,1,0:T(8,128)(2,1)S(1)} %select_select_fusion.1), channel_id=1, source_target_pairs={{0,4},{1,5},{2,6},{3,7},{4,0},{5,1},{6,2},{7,3},{8,12},{9,13},{10,... | collective-permute-start | bytes 294920 | tf_op jit(solution)/shard_map/ppermute | solution.py:37
  63.0 7.2 %collective-permute-start.15 = (bf16[6,128,512]{2,1,0:T(8,128)(2,1)S(1)}, bf16[6,128,512]{2,1,0:T(8,128)(2,1)S(1)}, u32[]{:S(2)}, u32[]{:S(2)}) collective-permute-start(bf16[6,128,512]{2,1,0:T(8,128)(2,1)S(1)} %pad_maximum_fusion.mine.refs_0_), channel_id=1, source_target_pairs={{0,8},{1,9},{2,10},{3,11},{4,12},{5,13},{6,14},{7,15},{8,0},{9,1},... | collective-permute-start | bytes 2359304 | tf_op jit(solution)/shard_map/ppermute | solution.py:37
  63.1 12.1 %collective-permute-start.14 = (bf16[6,128,512]{2,1,0:T(8,128)(2,1)S(1)}, bf16[6,128,512]{2,1,0:T(8,128)(2,1)S(1)}, u32[]{:S(2)}, u32[]{:S(2)}) collective-permute-start(bf16[6,128,512]{2,1,0:T(8,128)(2,1)S(1)} %pad_maximum_fusion.mine.refs_0_), channel_id=1, source_target_pairs={{0,1},{1,0},{2,3},{3,2},{4,5},{5,4},{6,7},{7,6},{8,24},{9,25},{10,... | collective-permute-start | bytes 2359304 | tf_op jit(solution)/shard_map/ppermute | solution.py:37
  64.5 5.7 %collective-permute-start.11 = (bf16[6,32,256]{2,1,0:T(8,128)(2,1)S(1)}, bf16[6,32,256]{2,1,0:T(8,128)(2,1)S(1)}, u32[]{:S(2)}, u32[]{:S(2)}) collective-permute-start(bf16[6,32,256]{2,1,0:T(8,128)(2,1)S(1)} %broadcast_select_fusion.1), channel_id=1, source_target_pairs={{0,16},{1,17},{2,18},{3,19},{4,20},{5,21},{6,22},{7,23},{8,10},{9,... | collective-permute-start | bytes 294920 | tf_op jit(solution)/shard_map/ppermute | solution.py:37
  75.2 7.4 %collective-permute-start.18 = (bf16[6,128,512]{2,1,0:T(8,128)(2,1)S(1)}, bf16[6,128,512]{2,1,0:T(8,128)(2,1)S(1)}, u32[]{:S(2)}, u32[]{:S(2)}) collective-permute-start(bf16[6,128,512]{2,1,0:T(8,128)(2,1)S(1)} %collective-permute-done.14.mine.refs_1_), channel_id=1, source_target_pairs={{0,8},{1,9},{2,10},{3,11},{4,12},{5,13},{6,14},{7,15},{8,0},{9,1},... | collective-permute-start | bytes 2359304 | tf_op jit(solution)/shard_map/ppermute | solution.py:37
  75.5 5.7 %collective-permute-start.13 = (bf16[6,64,256]{2,1,0:T(8,128)(2,1)S(1)}, bf16[6,64,256]{2,1,0:T(8,128)(2,1)S(1)}, u32[]{:S(2)}, u32[]{:S(2)}) collective-permute-start(bf16[6,64,256]{2,1,0:T(8,128)(2,1)S(1)} %pad_maximum_fusion.3), channel_id=1, source_target_pairs={{0,2},{1,3},{2,0},{3,1},{4,6},{5,7},{6,4},{7,5},{8,9},{9,8},{10,11... | collective-permute-start | bytes 589832 | tf_op jit(solution)/shard_map/ppermute | solution.py:37
  81.2 7.8 %collective-permute-start.16 = (bf16[6,128,256]{2,1,0:T(8,128)(2,1)S(1)}, bf16[6,128,256]{2,1,0:T(8,128)(2,1)S(1)}, u32[]{:S(2)}, u32[]{:S(2)}) collective-permute-start(bf16[6,128,256]{2,1,0:T(8,128)(2,1)S(1)} %pad_maximum_fusion.2.refs_0_), channel_id=1, source_target_pairs={{0,1},{1,0},{2,3},{3,2},{4,5},{5,4},{6,7},{7,6},{8,24},{9,25},{10,... | collective-permute-start | bytes 1179656 | tf_op jit(solution)/shard_map/ppermute | solution.py:37
  82.6 12.5 %collective-permute-start.17 = (bf16[6,128,256]{2,1,0:T(8,128)(2,1)S(1)}, bf16[6,128,256]{2,1,0:T(8,128)(2,1)S(1)}, u32[]{:S(2)}, u32[]{:S(2)}) collective-permute-start(bf16[6,128,256]{2,1,0:T(8,128)(2,1)S(1)} %pad_maximum_fusion.2.refs_0_), channel_id=1, source_target_pairs={{0,8},{1,9},{2,10},{3,11},{4,12},{5,13},{6,14},{7,15},{8,0},{9,1},... | collective-permute-start | bytes 1179656 | tf_op jit(solution)/shard_map/ppermute | solution.py:37
  82.6 12.5 %slice-start = ((s8[6291456]{0:T(1024)(128)(4,1)}), s8[4194304]{0:T(1024)(128)(4,1)S(1)}, s32[]{:S(2)}) async-start(s8[6291456]{0:T(1024)(128)(4,1)} %bitcast), calls=%async_computation | async-start | bytes 8388608
  86.2 8.9 %copy-start = (f32[2048,256]{1,0:T(8,128)S(1)}, f32[2048,256]{1,0:T(8,128)}, u32[]{:S(2)}) copy-start(f32[2048,256]{1,0:T(8,128)} %refs_6_.1) | copy-start | bytes 6291460
  86.2 8.9 %slice-start.1 = ((s8[6291456]{0:T(1024)(128)(4,1)}), s8[2097152]{0:T(1024)(128)(4,1)S(1)}, s32[]{:S(2)}) async-start(s8[6291456]{0:T(1024)(128)(4,1)} %bitcast), calls=%async_computation.1 | async-start | bytes 4194304
  89.0 6.1 %collective-permute-start.19 = (bf16[6,128,256]{2,1,0:T(8,128)(2,1)S(1)}, bf16[6,128,256]{2,1,0:T(8,128)(2,1)S(1)}, u32[]{:S(2)}, u32[]{:S(2)}) collective-permute-start(bf16[6,128,256]{2,1,0:T(8,128)(2,1)S(1)} %collective-permute-done.16.refs_1_), channel_id=1, source_target_pairs={{0,8},{1,9},{2,10},{3,11},{4,12},{5,13},{6,14},{7,15},{8,0},{9,1},... | collective-permute-start | bytes 1179656 | tf_op jit(solution)/shard_map/ppermute | solution.py:37
  109.2 1.4 %collective-permute-start.20 = (f32[6,8,128]{2,1,0:T(8,128)S(1)}, f32[6,8,128]{2,1,0:T(8,128)S(1)}, u32[]{:S(2)}, u32[]{:S(2)}) collective-permute-start(f32[6,8,128]{2,1,0:T(8,128)S(1)} %get-tuple-element.74), channel_id=1, source_target_pairs={{0,8},{1,9},{2,10},{3,11},{4,12},{5,13},{6,14},{7,15},{8,0},{9,1},... | collective-permute-start | bytes 73736 | tf_op jit(solution)/shard_map/ppermute | solution.py:37
  110.6 3.8 %collective-permute-start.21 = (f32[6,8,128]{2,1,0:T(8,128)S(1)}, f32[6,8,128]{2,1,0:T(8,128)S(1)}, u32[]{:S(2)}, u32[]{:S(2)}) collective-permute-start(f32[6,8,128]{2,1,0:T(8,128)S(1)} %add.54), channel_id=1, source_target_pairs={{0,1},{1,0},{2,3},{3,2},{4,5},{5,4},{6,7},{7,6},{8,9},{9,8},{10,11... | collective-permute-start | bytes 73736 | tf_op jit(solution)/shard_map/ppermute | solution.py:37
  114.4 3.8 %collective-permute-start.22 = (f32[6,8,128]{2,1,0:T(8,128)S(1)}, f32[6,8,128]{2,1,0:T(8,128)S(1)}, u32[]{:S(2)}, u32[]{:S(2)}) collective-permute-start(f32[6,8,128]{2,1,0:T(8,128)S(1)} %add.55), channel_id=1, source_target_pairs={{0,2},{1,3},{2,0},{3,1},{4,6},{5,7},{6,4},{7,5},{8,10},{9,11},{10,... | collective-permute-start | bytes 73736 | tf_op jit(solution)/shard_map/ppermute | solution.py:37
  118.2 3.8 %collective-permute-start.23 = (f32[6,8,128]{2,1,0:T(8,128)S(1)}, f32[6,8,128]{2,1,0:T(8,128)S(1)}, u32[]{:S(2)}, u32[]{:S(2)}) collective-permute-start(f32[6,8,128]{2,1,0:T(8,128)S(1)} %add.56), channel_id=1, source_target_pairs={{0,16},{1,17},{2,18},{3,19},{4,20},{5,21},{6,22},{7,23},{8,24},{9,... | collective-permute-start | bytes 73736 | tf_op jit(solution)/shard_map/ppermute | solution.py:37
  122.1 4.7 %collective-permute-start.24 = (f32[6,8,128]{2,1,0:T(8,128)S(1)}, f32[6,8,128]{2,1,0:T(8,128)S(1)}, u32[]{:S(2)}, u32[]{:S(2)}) collective-permute-start(f32[6,8,128]{2,1,0:T(8,128)S(1)} %add.57), channel_id=1, source_target_pairs={{0,4},{1,5},{2,6},{3,7},{4,0},{5,1},{6,2},{7,3},{8,12},{9,13},{10,... | collective-permute-start | bytes 73736 | tf_op jit(solution)/shard_map/ppermute | solution.py:37
  (2 other events, 7.4 us)

commit v4 on v3

--- a/solution.py
+++ b/solution.py
@@ -458,6 +458,7 @@
         if hasattr(route, "early") and tall_a is None:
             tall_a = tall_matrices(points, norms, *route.early, norm_scale, inner_scale)
             tall_a, = lead.after(tall_a)
+            lead.sends, _ = lax.optimization_barrier((lead.sends, trail.sends))
         if stage == 0:
             lead.go()
         elif stage == 1:

time: 128 us -> 125 us (0.977)
  waiting for transfers between devices: 50.9 us -> 44.7 us
  starting transfers between devices: 32.5 us -> 36.2 us
    ppermute x25, waiting for transfers between devices: 50.9 us -> 44.7 us  [swap(): lax.ppermute(x, AXES, [(i, i ^ 1 << bit_of(i)) for i in range(devices)])]
    ppermute x25, starting transfers between devices: 32.5 us -> 36.2 us  [swap(): lax.ppermute(x, AXES, [(i, i ^ 1 << bit_of(i)) for i in range(devices)])]
  transfers between devices with their start and end apart: 25 -> 25, of which waited for: 20 -> 21; matrix products, arithmetic and copies ran while one was open for 2% -> 2% of each run, Pallas kernels for 16% -> 16%
where the time goes in v4:
time: 125 us
  waiting for transfers between devices  44.7 us (36%)
  Pallas kernels  39.2 us (31%)
  starting transfers between devices  36.2 us (29%)
  other arithmetic  3.09 us (2%)
    ppermute x25, waiting for transfers between devices, swap(): lax.ppermute(x, AXES, [(i, i ^ 1 << bit_of(i)) for i in range(devices)])  44.7 us
    ppermute x25, starting transfers between devices, swap(): lax.ppermute(x, AXES, [(i, i ^ 1 << bit_of(i)) for i in range(devices)])  36.2 us
    pallas_call x1, Pallas kernels, solve(): pl.pallas_call(functools.partial(solve_kernel, mesh_shape), out_shape=(ja...  14.1 us
    pallas_call x2, Pallas kernels, tall_matrices(): pl.pallas_call(functools.partial(tall_kernel, norm_scale, scale), out_sha...  7.16 us
    pallas_call x1, Pallas kernels, among_matrices(): pl.pallas_call(functools.partial(among_kernel, mesh_shape, norm_scale, sc...  6.04 us
    pallas_call x1, Pallas kernels, pick_targets(): pl.pallas_call(functools.partial(pick_targets_kernel, mesh_shape), out_sh...  3.98 us
    pallas_call x1, Pallas kernels, pick_points(): pl.pallas_call(functools.partial(pick_points_kernel, mesh_shape), out_sha...  2.95 us
    pallas_call x1, Pallas kernels, point_norms(): pl.pallas_call(functools.partial(norms_kernel, scale), out_shape=jax.Shap...  2.61 us
  transfers between devices with their start and end apart: 25, of which 21 were waited for; matrix products, arithmetic and copies ran while one was open for 2% of the time, Pallas kernels for 16%

profile of v4, /device:TPU:0, one launch (start us, length us, event | category | flops | bytes accessed | tf_op | source)
XLA Modules:
  0.0 125.0 jit_solution(983693671622232237)
XLA Ops:
  0.6 2.9 %pick_points.1 = (bf16[6,256,512]{2,1,0:T(8,128)(2,1)S(1)}, bf16[6,256,512]{2,1,0:T(8,128)(2,1)S(1)}) custom-call(s32[6]{0:T(128)} %plan.9, bf16[2048,512]{1,0:T(8,128)(2,1)} %points.6), custom_call_target="tpu_custom_call" | custom-call | tf_op jit(solution)/shard_map/pick_points/pallas_call | solution.py:173
  4.0 3.0 %collective-permute-done.recv = bf16[6,256,512]{2,1,0:T(8,128)(2,1)S(1)} collective-permute-done((bf16[6,256,512]{2,1,0:T(8,128)(2,1)S(1)}, bf16[6,256,512]{2,1,0:T(8,128)(2,1)S(1)}, u32[]{:S(2)}, u32[]{:S(2)}) %collective-permute-start) | collective-permute-done | bytes 1572896 | tf_op jit(solution)/shard_map/ppermute | solution.py:37
  7.1 1.7 %halve.2 = (bf16[6,128,512]{2,1,0:T(8,128)(2,1)}, bf16[6,128,512]{2,1,0:T(8,128)(2,1)S(1)}) custom-call(s32[6]{0:T(128)S(1)} %copy-done.5, bf16[6,256,512]{2,1,0:T(8,128)(2,1)S(1)} %get-tuple-element.40.mine, bf16[6,256,512]{2,1,0:T(8,128)(2,1)S(1)} %collective-permute-done.recv), custom_call_target="tpu_custom_call" | custom-call | tf_op jit(solution)/shard_map/halve/pallas_call | solution.py:208
  9.6 2.9 %collective-permute-start.2 = (bf16[6,128,512]{2,1,0:T(8,128)(2,1)}, bf16[6,128,512]{2,1,0:T(8,128)(2,1)S(1)}, u32[]{:S(2)}, u32[]{:S(2)}) collective-permute-start(bf16[6,128,512]{2,1,0:T(8,128)(2,1)} %get-tuple-element.47), channel_id=1, source_target_pairs={{0,1},{1,0},{2,3},{3,2},{4,5},{5,4},{6,7},{7,6},{8,24},{9,25},{10,... | collective-permute-start | bytes 2359304 | tf_op jit(solution)/shard_map/ppermute | solution.py:37
  12.6 4.0 %pick_targets.1 = (bf16[6,256,256]{2,1,0:T(8,128)(2,1)}, bf16[6,256,256]{2,1,0:T(8,128)(2,1)S(1)}) custom-call(s32[6]{0:T(128)} %plan.9, f32[2048,256]{1,0:T(8,128)} %refs_6_.1), custom_call_target="tpu_custom_call" | custom-call | tf_op jit(solution)/shard_map/pick_targets/pallas_call | solution.py:238
  16.8 6.0 %collective-permute-done.2.recv = bf16[6,128,512]{2,1,0:T(8,128)(2,1)S(1)} collective-permute-done((bf16[6,128,512]{2,1,0:T(8,128)(2,1)}, bf16[6,128,512]{2,1,0:T(8,128)(2,1)S(1)}, u32[]{:S(2)}, u32[]{:S(2)}) %collective-permute-start.2) | collective-permute-done | bytes 786464 | tf_op jit(solution)/shard_map/ppermute | solution.py:37
  23.5 2.2 %collective-permute-start.4 = (bf16[6,64,512]{2,1,0:T(8,128)(2,1)S(1)}, bf16[6,64,512]{2,1,0:T(8,128)(2,1)S(1)}, u32[]{:S(2)}, u32[]{:S(2)}) collective-permute-start(bf16[6,64,512]{2,1,0:T(8,128)(2,1)S(1)} %get-tuple-element.49), channel_id=1, source_target_pairs={{0,2},{1,3},{2,0},{3,1},{4,6},{5,7},{6,4},{7,5},{8,9},{9,8},{10,11... | collective-permute-start | bytes 1179656 | tf_op jit(solution)/shard_map/ppermute | solution.py:37
  25.7 1.4 %dynamic-slice_select_fusion.1 = (bf16[6,128,256]{2,1,0:T(8,128)(2,1)S(1)}, bf16[6,128,256]{2,1,0:T(8,128)(2,1)S(1)}) fusion(bf16[6,256,256]{2,1,0:T(8,128)(2,1)} %collective-permute-done.1, s32[]{:T(128)S(6)} %select_n.119, bf16[6,256,256]{2,1,0:T(8,128)(2,1)S(1)} %get-tuple-element.44, pred[6]{0:T(512)(128)(4,1)S(1)} %get-tuple-element.84, s32[]{:T(128)S(6)} %select_n.122), kind=kLoop, calls=%fused_computation.4 | loop fusion | flops 393216 | bytes 2359310 | tf_op jit(solution)/shard_map/jit(_where)/select_n | solution.py:86
  27.1 1.6 %collective-permute-start.3 = (bf16[6,128,256]{2,1,0:T(8,128)(2,1)S(1)}, bf16[6,128,256]{2,1,0:T(8,128)(2,1)S(1)}, u32[]{:S(2)}, u32[]{:S(2)}) collective-permute-start(bf16[6,128,256]{2,1,0:T(8,128)(2,1)S(1)} %get-tuple-element.50), channel_id=1, source_target_pairs={{0,1},{1,0},{2,3},{3,2},{4,5},{5,4},{6,7},{7,6},{8,24},{9,25},{10,... | collective-permute-start | bytes 1179656 | tf_op jit(solution)/shard_map/ppermute | solution.py:37
  28.7 2.6 %norms.1 = f32[2048,128]{1,0:T(8,128)} custom-call(bf16[2048,512]{1,0:T(8,128)(2,1)} %points.6), custom_call_target="tpu_custom_call" | custom-call | bytes 6291456 | tf_op jit(solution)/shard_map/norms/pallas_call | solution.py:264
  31.5 2.4 %collective-permute-start.6 = (bf16[6,32,512]{2,1,0:T(8,128)(2,1)S(1)}, bf16[6,32,512]{2,1,0:T(8,128)(2,1)S(1)}, u32[]{:S(2)}, u32[]{:S(2)}) collective-permute-start(bf16[6,32,512]{2,1,0:T(8,128)(2,1)S(1)} %dynamic-slice_select_fusion.2), channel_id=1, source_target_pairs={{0,16},{1,17},{2,18},{3,19},{4,20},{5,21},{6,22},{7,23},{8,10},{9,... | collective-permute-start | bytes 589832 | tf_op jit(solution)/shard_map/ppermute | solution.py:37
  37.8 2.8 %collective-permute-start.8 = (bf16[6,32,512]{2,1,0:T(8,128)(2,1)S(1)}, bf16[6,32,512]{2,1,0:T(8,128)(2,1)S(1)}, u32[]{:S(2)}, u32[]{:S(2)}) collective-permute-start(bf16[6,32,512]{2,1,0:T(8,128)(2,1)S(1)} %select_select_fusion), channel_id=1, source_target_pairs={{0,4},{1,5},{2,6},{3,7},{4,0},{5,1},{6,2},{7,3},{8,12},{9,13},{10,... | collective-permute-start | bytes 589832 | tf_op jit(solution)/shard_map/ppermute | solution.py:37
  40.5 3.3 %collective-permute-done.5 = bf16[6,64,256]{2,1,0:T(8,128)(2,1)S(1)} collective-permute-done((bf16[6,64,256]{2,1,0:T(8,128)(2,1)S(1)}, bf16[6,64,256]{2,1,0:T(8,128)(2,1)S(1)}, u32[]{:S(2)}, u32[]{:S(2)}) %collective-permute-start.5) | collective-permute-done | bytes 196640 | tf_op jit(solution)/shard_map/ppermute | solution.py:37
  44.0 4.3 %collective-permute-start.7 = (bf16[6,32,256]{2,1,0:T(8,128)(2,1)S(1)}, bf16[6,32,256]{2,1,0:T(8,128)(2,1)S(1)}, u32[]{:S(2)}, u32[]{:S(2)}) collective-permute-start(bf16[6,32,256]{2,1,0:T(8,128)(2,1)S(1)} %dynamic-slice_select_fusion.5), channel_id=1, source_target_pairs={{0,16},{1,17},{2,18},{3,19},{4,20},{5,21},{6,22},{7,23},{8,10},{9,... | collective-permute-start | bytes 294920 | tf_op jit(solution)/shard_map/ppermute | solution.py:37
  48.7 2.1 %collective-permute-done.7 = bf16[6,32,256]{2,1,0:T(8,128)(2,1)S(1)} collective-permute-done((bf16[6,32,256]{2,1,0:T(8,128)(2,1)S(1)}, bf16[6,32,256]{2,1,0:T(8,128)(2,1)S(1)}, u32[]{:S(2)}, u32[]{:S(2)}) %collective-permute-start.7) | collective-permute-done | bytes 98336 | tf_op jit(solution)/shard_map/ppermute | solution.py:37
  50.9 3.5 %collective-permute-done.10 = bf16[6,32,512]{2,1,0:T(8,128)(2,1)S(1)} collective-permute-done((bf16[6,32,512]{2,1,0:T(8,128)(2,1)S(1)}, bf16[6,32,512]{2,1,0:T(8,128)(2,1)S(1)}, u32[]{:S(2)}, u32[]{:S(2)}) %collective-permute-start.10) | collective-permute-done | bytes 196640 | tf_op jit(solution)/shard_map/ppermute | solution.py:37
  54.9 3.4 %collective-permute-start.9 = (bf16[6,32,256]{2,1,0:T(8,128)(2,1)S(1)}, bf16[6,32,256]{2,1,0:T(8,128)(2,1)S(1)}, u32[]{:S(2)}, u32[]{:S(2)}) collective-permute-start(bf16[6,32,256]{2,1,0:T(8,128)(2,1)S(1)} %select_select_fusion.1), channel_id=1, source_target_pairs={{0,4},{1,5},{2,6},{3,7},{4,0},{5,1},{6,2},{7,3},{8,12},{9,13},{10,... | collective-permute-start | bytes 294920 | tf_op jit(solution)/shard_map/ppermute | solution.py:37
  58.3 4.0 %collective-permute-done.9 = bf16[6,32,256]{2,1,0:T(8,128)(2,1)S(1)} collective-permute-done((bf16[6,32,256]{2,1,0:T(8,128)(2,1)S(1)}, bf16[6,32,256]{2,1,0:T(8,128)(2,1)S(1)}, u32[]{:S(2)}, u32[]{:S(2)}) %collective-permute-start.9) | collective-permute-done | bytes 98336 | tf_op jit(solution)/shard_map/ppermute | solution.py:37
  65.6 2.6 %collective-permute-done.11 = bf16[6,32,256]{2,1,0:T(8,128)(2,1)S(1)} collective-permute-done((bf16[6,32,256]{2,1,0:T(8,128)(2,1)S(1)}, bf16[6,32,256]{2,1,0:T(8,128)(2,1)S(1)}, u32[]{:S(2)}, u32[]{:S(2)}) %collective-permute-start.11) | collective-permute-done | bytes 98336 | tf_op jit(solution)/shard_map/ppermute | solution.py:37
  68.2 3.0 %collective-permute-start.13 = (bf16[6,64,256]{2,1,0:T(8,128)(2,1)S(1)}, bf16[6,64,256]{2,1,0:T(8,128)(2,1)S(1)}, u32[]{:S(2)}, u32[]{:S(2)}) collective-permute-start(bf16[6,64,256]{2,1,0:T(8,128)(2,1)S(1)} %pad_maximum_fusion.3), channel_id=1, source_target_pairs={{0,2},{1,3},{2,0},{3,1},{4,6},{5,7},{6,4},{7,5},{8,9},{9,8},{10,11... | collective-permute-start | bytes 589832 | tf_op jit(solution)/shard_map/ppermute | solution.py:37
  71.2 3.6 %collective-permute-done.13 = bf16[6,64,256]{2,1,0:T(8,128)(2,1)S(1)} collective-permute-done((bf16[6,64,256]{2,1,0:T(8,128)(2,1)S(1)}, bf16[6,64,256]{2,1,0:T(8,128)(2,1)S(1)}, u32[]{:S(2)}, u32[]{:S(2)}) %collective-permute-start.13) | collective-permute-done | bytes 196640 | tf_op jit(solution)/shard_map/ppermute | solution.py:37
  74.9 3.6 %tall.2.refs_7_ = bf16[6,2048,256]{2,1,0:T(8,128)(2,1)S(1)} custom-call(bf16[6,128,512]{2,1,0:T(8,128)(2,1)S(1)} %pad_maximum_fusion.mine.refs_0_, bf16[6,128,512]{2,1,0:T(8,128)(2,1)S(1)} %collective-permute-done.15.other.refs_2_, bf16[2048,512]{1,0:T(8,128)(2,1)S(1)} %copy-done.1, f32[2048,128]{1,0:T(8,128)S(1)} %copy-done.2), custom_call_target="tpu_custom_call" | custom-call | flops 3221225472 | bytes 12582912 | tf_op jit(solution)/shard_map/tall/pallas_call | solution.py:295
  81.0 3.6 %tall.3.refs_8_ = bf16[6,2048,256]{2,1,0:T(8,128)(2,1)S(1)} custom-call(bf16[6,128,512]{2,1,0:T(8,128)(2,1)S(1)} %collective-permute-done.14.mine.refs_1_, bf16[6,128,512]{2,1,0:T(8,128)(2,1)S(1)} %collective-permute-done.18.other.refs_3_, bf16[2048,512]{1,0:T(8,128)(2,1)S(1)} %copy-done.1, f32[2048,128]{1,0:T(8,128)S(1)} %copy-done.2), custom_call_target="tpu_custom_call" | custom-call | flops 3221225472 | bytes 12582912 | tf_op jit(solution)/shard_map/tall/pallas_call | solution.py:295
  84.6 2.0 %collective-permute-done.16.refs_1_ = bf16[6,128,256]{2,1,0:T(8,128)(2,1)S(1)} collective-permute-done((bf16[6,128,256]{2,1,0:T(8,128)(2,1)S(1)}, bf16[6,128,256]{2,1,0:T(8,128)(2,1)S(1)}, u32[]{:S(2)}, u32[]{:S(2)}) %collective-permute-start.16) | collective-permute-done | bytes 393248 | tf_op jit(solution)/shard_map/ppermute | solution.py:37
  86.6 6.0 %among.1.refs_5_ = bf16[15,512,512]{2,1,0:T(8,128)(2,1)S(1)} custom-call(bf16[6,128,512]{2,1,0:T(8,128)(2,1)S(1)} %pad_maximum_fusion.mine.refs_0_, bf16[6,128,512]{2,1,0:T(8,128)(2,1)S(1)} %collective-permute-done.14.mine.refs_1_, bf16[6,128,512]{2,1,0:T(8,128)(2,1)S(1)} %collective-permute-done.15.other.refs_2_, ...), custom_call_target="tpu_custom_call" | custom-call | flops 4026531840 | bytes 15728640 | tf_op jit(solution)/shard_map/among/pallas_call | solution.py:335
  92.7 14.1 %solve.1 = (f32[2048,256]{1,0:T(8,128)}, bf16[6,512,256]{2,1,0:T(8,128)(2,1)}, f32[6,8,128]{2,1,0:T(8,128)S(1)}) custom-call(s32[6]{0:T(128)S(1)} %copy-done.6, bf16[6,128,256]{2,1,0:T(8,128)(2,1)S(1)} %pad_maximum_fusion.2.refs_0_, bf16[6,128,256]{2,1,0:T(8,128)(2,1)S(1)} %collective-permute-done.16.refs_1_, ...), custom_call_target="tpu_custom_call" | custom-call | tf_op jit(solution)/shard_map/solve/pallas_call | solution.py:412
  109.4 2.5 %collective-permute-done.21 = f32[6,8,128]{2,1,0:T(8,128)S(1)} collective-permute-done((f32[6,8,128]{2,1,0:T(8,128)S(1)}, f32[6,8,128]{2,1,0:T(8,128)S(1)}, u32[]{:S(2)}, u32[]{:S(2)}) %collective-permute-start.21) | collective-permute-done | bytes 24608 | tf_op jit(solution)/shard_map/ppermute | solution.py:37
  111.9 2.1 %collective-permute-start.22 = (f32[6,8,128]{2,1,0:T(8,128)S(1)}, f32[6,8,128]{2,1,0:T(8,128)S(1)}, u32[]{:S(2)}, u32[]{:S(2)}) collective-permute-start(f32[6,8,128]{2,1,0:T(8,128)S(1)} %add.55), channel_id=1, source_target_pairs={{0,2},{1,3},{2,0},{3,1},{4,6},{5,7},{6,4},{7,5},{8,10},{9,11},{10,... | collective-permute-start | bytes 73736 | tf_op jit(solution)/shard_map/ppermute | solution.py:37
  114.0 1.8 %collective-permute-done.22 = f32[6,8,128]{2,1,0:T(8,128)S(1)} collective-permute-done((f32[6,8,128]{2,1,0:T(8,128)S(1)}, f32[6,8,128]{2,1,0:T(8,128)S(1)}, u32[]{:S(2)}, u32[]{:S(2)}) %collective-permute-start.22) | collective-permute-done | bytes 24608 | tf_op jit(solution)/shard_map/ppermute | solution.py:37
  117.0 2.7 %collective-permute-done.23 = f32[6,8,128]{2,1,0:T(8,128)S(1)} collective-permute-done((f32[6,8,128]{2,1,0:T(8,128)S(1)}, f32[6,8,128]{2,1,0:T(8,128)S(1)}, u32[]{:S(2)}, u32[]{:S(2)}) %collective-permute-start.23) | collective-permute-done | bytes 24608 | tf_op jit(solution)/shard_map/ppermute | solution.py:37
  119.7 2.6 %collective-permute-start.24 = (f32[6,8,128]{2,1,0:T(8,128)S(1)}, f32[6,8,128]{2,1,0:T(8,128)S(1)}, u32[]{:S(2)}, u32[]{:S(2)}) collective-permute-start(f32[6,8,128]{2,1,0:T(8,128)S(1)} %add.57), channel_id=1, source_target_pairs={{0,4},{1,5},{2,6},{3,7},{4,0},{5,1},{6,2},{7,3},{8,12},{9,13},{10,... | collective-permute-start | bytes 73736 | tf_op jit(solution)/shard_map/ppermute | solution.py:37
  122.3 2.1 %collective-permute-done.24 = f32[6,8,128]{2,1,0:T(8,128)S(1)} collective-permute-done((f32[6,8,128]{2,1,0:T(8,128)S(1)}, f32[6,8,128]{2,1,0:T(8,128)S(1)}, u32[]{:S(2)}, u32[]{:S(2)}) %collective-permute-start.24) | collective-permute-done | bytes 24608 | tf_op jit(solution)/shard_map/ppermute | solution.py:37
  (66 shorter events, 17.9 us)
Async XLA Ops:
  3.6 3.5 %collective-permute-start = (bf16[6,256,512]{2,1,0:T(8,128)(2,1)S(1)}, bf16[6,256,512]{2,1,0:T(8,128)(2,1)S(1)}, u32[]{:S(2)}, u32[]{:S(2)}) collective-permute-start(bf16[6,256,512]{2,1,0:T(8,128)(2,1)S(1)} %get-tuple-element.41), channel_id=1, source_target_pairs={{0,8},{1,9},{2,10},{3,11},{4,12},{5,13},{6,14},{7,15},{8,0},{9,1},... | collective-permute-start | bytes 4718600 | tf_op jit(solution)/shard_map/ppermute | solution.py:37
  9.6 7.1 %copy-start.6 = (s32[6]{0:T(128)S(1)}, s32[6]{0:T(128)}, u32[]{:S(2)}) copy-start(s32[6]{0:T(128)} %plan.9) | copy-start | bytes 76
  9.6 13.1 %copy-start.4 = (bf16[6,128,512]{2,1,0:T(8,128)(2,1)S(1)}, bf16[6,128,512]{2,1,0:T(8,128)(2,1)}, u32[]{:S(2)}) copy-start(bf16[6,128,512]{2,1,0:T(8,128)(2,1)} %copy-done.3) | copy-start | bytes 2359300
  9.6 13.1 %collective-permute-start.2 = (bf16[6,128,512]{2,1,0:T(8,128)(2,1)}, bf16[6,128,512]{2,1,0:T(8,128)(2,1)S(1)}, u32[]{:S(2)}, u32[]{:S(2)}) collective-permute-start(bf16[6,128,512]{2,1,0:T(8,128)(2,1)} %get-tuple-element.47), channel_id=1, source_target_pairs={{0,1},{1,0},{2,3},{3,2},{4,5},{5,4},{6,7},{7,6},{8,24},{9,25},{10,... | collective-permute-start | bytes 2359304 | tf_op jit(solution)/shard_map/ppermute | solution.py:37
  16.5 9.1 %collective-permute-start.1 = (bf16[6,256,256]{2,1,0:T(8,128)(2,1)}, bf16[6,256,256]{2,1,0:T(8,128)(2,1)}, u32[]{:S(2)}, u32[]{:S(2)}) collective-permute-start(bf16[6,256,256]{2,1,0:T(8,128)(2,1)} %get-tuple-element.45), channel_id=1, source_target_pairs={{0,8},{1,9},{2,10},{3,11},{4,12},{5,13},{6,14},{7,15},{8,0},{9,1},... | collective-permute-start | bytes 2359304 | tf_op jit(solution)/shard_map/ppermute | solution.py:37
  23.5 7.9 %collective-permute-start.4 = (bf16[6,64,512]{2,1,0:T(8,128)(2,1)S(1)}, bf16[6,64,512]{2,1,0:T(8,128)(2,1)S(1)}, u32[]{:S(2)}, u32[]{:S(2)}) collective-permute-start(bf16[6,64,512]{2,1,0:T(8,128)(2,1)S(1)} %get-tuple-element.49), channel_id=1, source_target_pairs={{0,2},{1,3},{2,0},{3,1},{4,6},{5,7},{6,4},{7,5},{8,9},{9,8},{10,11... | collective-permute-start | bytes 1179656 | tf_op jit(solution)/shard_map/ppermute | solution.py:37
  27.1 7.8 %collective-permute-start.3 = (bf16[6,128,256]{2,1,0:T(8,128)(2,1)S(1)}, bf16[6,128,256]{2,1,0:T(8,128)(2,1)S(1)}, u32[]{:S(2)}, u32[]{:S(2)}) collective-permute-start(bf16[6,128,256]{2,1,0:T(8,128)(2,1)S(1)} %get-tuple-element.50), channel_id=1, source_target_pairs={{0,1},{1,0},{2,3},{3,2},{4,5},{5,4},{6,7},{7,6},{8,24},{9,25},{10,... | collective-permute-start | bytes 1179656 | tf_op jit(solution)/shard_map/ppermute | solution.py:37
  31.5 6.1 %collective-permute-start.6 = (bf16[6,32,512]{2,1,0:T(8,128)(2,1)S(1)}, bf16[6,32,512]{2,1,0:T(8,128)(2,1)S(1)}, u32[]{:S(2)}, u32[]{:S(2)}) collective-permute-start(bf16[6,32,512]{2,1,0:T(8,128)(2,1)S(1)} %dynamic-slice_select_fusion.2), channel_id=1, source_target_pairs={{0,16},{1,17},{2,18},{3,19},{4,20},{5,21},{6,22},{7,23},{8,10},{9,... | collective-permute-start | bytes 589832 | tf_op jit(solution)/shard_map/ppermute | solution.py:37
  35.1 8.7 %collective-permute-start.5 = (bf16[6,64,256]{2,1,0:T(8,128)(2,1)S(1)}, bf16[6,64,256]{2,1,0:T(8,128)(2,1)S(1)}, u32[]{:S(2)}, u32[]{:S(2)}) collective-permute-start(bf16[6,64,256]{2,1,0:T(8,128)(2,1)S(1)} %get-tuple-element.55), channel_id=1, source_target_pairs={{0,2},{1,3},{2,0},{3,1},{4,6},{5,7},{6,4},{7,5},{8,9},{9,8},{10,11... | collective-permute-start | bytes 589832 | tf_op jit(solution)/shard_map/ppermute | solution.py:37
  37.8 10.8 %collective-permute-start.8 = (bf16[6,32,512]{2,1,0:T(8,128)(2,1)S(1)}, bf16[6,32,512]{2,1,0:T(8,128)(2,1)S(1)}, u32[]{:S(2)}, u32[]{:S(2)}) collective-permute-start(bf16[6,32,512]{2,1,0:T(8,128)(2,1)S(1)} %select_select_fusion), channel_id=1, source_target_pairs={{0,4},{1,5},{2,6},{3,7},{4,0},{5,1},{6,2},{7,3},{8,12},{9,13},{10,... | collective-permute-start | bytes 589832 | tf_op jit(solution)/shard_map/ppermute | solution.py:37
  44.0 6.9 %collective-permute-start.7 = (bf16[6,32,256]{2,1,0:T(8,128)(2,1)S(1)}, bf16[6,32,256]{2,1,0:T(8,128)(2,1)S(1)}, u32[]{:S(2)}, u32[]{:S(2)}) collective-permute-start(bf16[6,32,256]{2,1,0:T(8,128)(2,1)S(1)} %dynamic-slice_select_fusion.5), channel_id=1, source_target_pairs={{0,16},{1,17},{2,18},{3,19},{4,20},{5,21},{6,22},{7,23},{8,10},{9,... | collective-permute-start | bytes 294920 | tf_op jit(solution)/shard_map/ppermute | solution.py:37
  48.7 5.7 %collective-permute-start.10 = (bf16[6,32,512]{2,1,0:T(8,128)(2,1)S(1)}, bf16[6,32,512]{2,1,0:T(8,128)(2,1)S(1)}, u32[]{:S(2)}, u32[]{:S(2)}) collective-permute-start(bf16[6,32,512]{2,1,0:T(8,128)(2,1)S(1)} %broadcast_select_fusion), channel_id=1, source_target_pairs={{0,16},{1,17},{2,18},{3,19},{4,20},{5,21},{6,22},{7,23},{8,10},{9,... | collective-permute-start | bytes 589832 | tf_op jit(solution)/shard_map/ppermute | solution.py:37
  54.4 20.5 %copy-start.2 = (f32[2048,128]{1,0:T(8,128)S(1)}, f32[2048,128]{1,0:T(8,128)}, u32[]{:S(2)}) copy-start(f32[2048,128]{1,0:T(8,128)} %norms.1) | copy-start | bytes 3145732
  54.4 20.5 %copy-start.1 = (bf16[2048,512]{1,0:T(8,128)(2,1)S(1)}, bf16[2048,512]{1,0:T(8,128)(2,1)}, u32[]{:S(2)}) copy-start(bf16[2048,512]{1,0:T(8,128)(2,1)} %points.6) | copy-start | bytes 6291460
  54.5 8.9 %collective-permute-start.12 = (bf16[6,64,512]{2,1,0:T(8,128)(2,1)S(1)}, bf16[6,64,512]{2,1,0:T(8,128)(2,1)S(1)}, u32[]{:S(2)}, u32[]{:S(2)}) collective-permute-start(bf16[6,64,512]{2,1,0:T(8,128)(2,1)S(1)} %pad_maximum_fusion.1), channel_id=1, source_target_pairs={{0,2},{1,3},{2,0},{3,1},{4,6},{5,7},{6,4},{7,5},{8,9},{9,8},{10,11... | collective-permute-start | bytes 1179656 | tf_op jit(solution)/shard_map/ppermute | solution.py:37
  54.9 7.4 %collective-permute-start.9 = (bf16[6,32,256]{2,1,0:T(8,128)(2,1)S(1)}, bf16[6,32,256]{2,1,0:T(8,128)(2,1)S(1)}, u32[]{:S(2)}, u32[]{:S(2)}) collective-permute-start(bf16[6,32,256]{2,1,0:T(8,128)(2,1)S(1)} %select_select_fusion.1), channel_id=1, source_target_pairs={{0,4},{1,5},{2,6},{3,7},{4,0},{5,1},{6,2},{7,3},{8,12},{9,13},{10,... | collective-permute-start | bytes 294920 | tf_op jit(solution)/shard_map/ppermute | solution.py:37
  63.4 11.5 %collective-permute-start.15 = (bf16[6,128,512]{2,1,0:T(8,128)(2,1)S(1)}, bf16[6,128,512]{2,1,0:T(8,128)(2,1)S(1)}, u32[]{:S(2)}, u32[]{:S(2)}) collective-permute-start(bf16[6,128,512]{2,1,0:T(8,128)(2,1)S(1)} %pad_maximum_fusion.mine.refs_0_), channel_id=1, source_target_pairs={{0,8},{1,9},{2,10},{3,11},{4,12},{5,13},{6,14},{7,15},{8,0},{9,1},... | collective-permute-start | bytes 2359304 | tf_op jit(solution)/shard_map/ppermute | solution.py:37
  63.5 4.7 %collective-permute-start.11 = (bf16[6,32,256]{2,1,0:T(8,128)(2,1)S(1)}, bf16[6,32,256]{2,1,0:T(8,128)(2,1)S(1)}, u32[]{:S(2)}, u32[]{:S(2)}) collective-permute-start(bf16[6,32,256]{2,1,0:T(8,128)(2,1)S(1)} %broadcast_select_fusion.1), channel_id=1, source_target_pairs={{0,16},{1,17},{2,18},{3,19},{4,20},{5,21},{6,22},{7,23},{8,10},{9,... | collective-permute-start | bytes 294920 | tf_op jit(solution)/shard_map/ppermute | solution.py:37
  64.6 14.1 %collective-permute-start.14 = (bf16[6,128,512]{2,1,0:T(8,128)(2,1)S(1)}, bf16[6,128,512]{2,1,0:T(8,128)(2,1)S(1)}, u32[]{:S(2)}, u32[]{:S(2)}) collective-permute-start(bf16[6,128,512]{2,1,0:T(8,128)(2,1)S(1)} %pad_maximum_fusion.mine.refs_0_), channel_id=1, source_target_pairs={{0,1},{1,0},{2,3},{3,2},{4,5},{5,4},{6,7},{7,6},{8,24},{9,25},{10,... | collective-permute-start | bytes 2359304 | tf_op jit(solution)/shard_map/ppermute | solution.py:37
  68.2 6.7 %collective-permute-start.13 = (bf16[6,64,256]{2,1,0:T(8,128)(2,1)S(1)}, bf16[6,64,256]{2,1,0:T(8,128)(2,1)S(1)}, u32[]{:S(2)}, u32[]{:S(2)}) collective-permute-start(bf16[6,64,256]{2,1,0:T(8,128)(2,1)S(1)} %pad_maximum_fusion.3), channel_id=1, source_target_pairs={{0,2},{1,3},{2,0},{3,1},{4,6},{5,7},{6,4},{7,5},{8,9},{9,8},{10,11... | collective-permute-start | bytes 589832 | tf_op jit(solution)/shard_map/ppermute | solution.py:37
  78.7 2.3 %collective-permute-start.18 = (bf16[6,128,512]{2,1,0:T(8,128)(2,1)S(1)}, bf16[6,128,512]{2,1,0:T(8,128)(2,1)S(1)}, u32[]{:S(2)}, u32[]{:S(2)}) collective-permute-start(bf16[6,128,512]{2,1,0:T(8,128)(2,1)S(1)} %collective-permute-done.14.mine.refs_1_), channel_id=1, source_target_pairs={{0,8},{1,9},{2,10},{3,11},{4,12},{5,13},{6,14},{7,15},{8,0},{9,1},... | collective-permute-start | bytes 2359304 | tf_op jit(solution)/shard_map/ppermute | solution.py:37
  78.8 7.8 %collective-permute-start.16 = (bf16[6,128,256]{2,1,0:T(8,128)(2,1)S(1)}, bf16[6,128,256]{2,1,0:T(8,128)(2,1)S(1)}, u32[]{:S(2)}, u32[]{:S(2)}) collective-permute-start(bf16[6,128,256]{2,1,0:T(8,128)(2,1)S(1)} %pad_maximum_fusion.2.refs_0_), channel_id=1, source_target_pairs={{0,1},{1,0},{2,3},{3,2},{4,5},{5,4},{6,7},{7,6},{8,24},{9,25},{10,... | collective-permute-start | bytes 1179656 | tf_op jit(solution)/shard_map/ppermute | solution.py:37
  80.1 12.5 %collective-permute-start.17 = (bf16[6,128,256]{2,1,0:T(8,128)(2,1)S(1)}, bf16[6,128,256]{2,1,0:T(8,128)(2,1)S(1)}, u32[]{:S(2)}, u32[]{:S(2)}) collective-permute-start(bf16[6,128,256]{2,1,0:T(8,128)(2,1)S(1)} %pad_maximum_fusion.2.refs_0_), channel_id=1, source_target_pairs={{0,8},{1,9},{2,10},{3,11},{4,12},{5,13},{6,14},{7,15},{8,0},{9,1},... | collective-permute-start | bytes 1179656 | tf_op jit(solution)/shard_map/ppermute | solution.py:37
  81.0 11.6 %slice-start = ((s8[6291456]{0:T(1024)(128)(4,1)}), s8[4194304]{0:T(1024)(128)(4,1)S(1)}, s32[]{:S(2)}) async-start(s8[6291456]{0:T(1024)(128)(4,1)} %bitcast), calls=%async_computation | async-start | bytes 8388608
  84.6 8.1 %copy-start = (f32[2048,256]{1,0:T(8,128)S(1)}, f32[2048,256]{1,0:T(8,128)}, u32[]{:S(2)}) copy-start(f32[2048,256]{1,0:T(8,128)} %refs_6_.1) | copy-start | bytes 6291460
  84.6 8.1 %slice-start.1 = ((s8[6291456]{0:T(1024)(128)(4,1)}), s8[2097152]{0:T(1024)(128)(4,1)S(1)}, s32[]{:S(2)}) async-start(s8[6291456]{0:T(1024)(128)(4,1)} %bitcast), calls=%async_computation.1 | async-start | bytes 4194304
  86.6 6.1 %collective-permute-start.19 = (bf16[6,128,256]{2,1,0:T(8,128)(2,1)S(1)}, bf16[6,128,256]{2,1,0:T(8,128)(2,1)S(1)}, u32[]{:S(2)}, u32[]{:S(2)}) collective-permute-start(bf16[6,128,256]{2,1,0:T(8,128)(2,1)S(1)} %collective-permute-done.16.refs_1_), channel_id=1, source_target_pairs={{0,8},{1,9},{2,10},{3,11},{4,12},{5,13},{6,14},{7,15},{8,0},{9,1},... | collective-permute-start | bytes 1179656 | tf_op jit(solution)/shard_map/ppermute | solution.py:37
  106.7 1.4 %collective-permute-start.20 = (f32[6,8,128]{2,1,0:T(8,128)S(1)}, f32[6,8,128]{2,1,0:T(8,128)S(1)}, u32[]{:S(2)}, u32[]{:S(2)}) collective-permute-start(f32[6,8,128]{2,1,0:T(8,128)S(1)} %get-tuple-element.76), channel_id=1, source_target_pairs={{0,8},{1,9},{2,10},{3,11},{4,12},{5,13},{6,14},{7,15},{8,0},{9,1},... | collective-permute-start | bytes 73736 | tf_op jit(solution)/shard_map/ppermute | solution.py:37
  108.1 3.8 %collective-permute-start.21 = (f32[6,8,128]{2,1,0:T(8,128)S(1)}, f32[6,8,128]{2,1,0:T(8,128)S(1)}, u32[]{:S(2)}, u32[]{:S(2)}) collective-permute-start(f32[6,8,128]{2,1,0:T(8,128)S(1)} %add.54), channel_id=1, source_target_pairs={{0,1},{1,0},{2,3},{3,2},{4,5},{5,4},{6,7},{7,6},{8,9},{9,8},{10,11... | collective-permute-start | bytes 73736 | tf_op jit(solution)/shard_map/ppermute | solution.py:37
  111.9 3.9 %collective-permute-start.22 = (f32[6,8,128]{2,1,0:T(8,128)S(1)}, f32[6,8,128]{2,1,0:T(8,128)S(1)}, u32[]{:S(2)}, u32[]{:S(2)}) collective-permute-start(f32[6,8,128]{2,1,0:T(8,128)S(1)} %add.55), channel_id=1, source_target_pairs={{0,2},{1,3},{2,0},{3,1},{4,6},{5,7},{6,4},{7,5},{8,10},{9,11},{10,... | collective-permute-start | bytes 73736 | tf_op jit(solution)/shard_map/ppermute | solution.py:37
  115.8 3.8 %collective-permute-start.23 = (f32[6,8,128]{2,1,0:T(8,128)S(1)}, f32[6,8,128]{2,1,0:T(8,128)S(1)}, u32[]{:S(2)}, u32[]{:S(2)}) collective-permute-start(f32[6,8,128]{2,1,0:T(8,128)S(1)} %add.56), channel_id=1, source_target_pairs={{0,16},{1,17},{2,18},{3,19},{4,20},{5,21},{6,22},{7,23},{8,24},{9,... | collective-permute-start | bytes 73736 | tf_op jit(solution)/shard_map/ppermute | solution.py:37
  119.7 4.7 %collective-permute-start.24 = (f32[6,8,128]{2,1,0:T(8,128)S(1)}, f32[6,8,128]{2,1,0:T(8,128)S(1)}, u32[]{:S(2)}, u32[]{:S(2)}) collective-permute-start(f32[6,8,128]{2,1,0:T(8,128)S(1)} %add.57), channel_id=1, source_target_pairs={{0,4},{1,5},{2,6},{3,7},{4,0},{5,1},{6,2},{7,3},{8,12},{9,13},{10,... | collective-permute-start | bytes 73736 | tf_op jit(solution)/shard_map/ppermute | solution.py:37
  (2 other events, 7.3 us)

commit v5 on v4

--- a/solution.py
+++ b/solution.py
@@ -403,7 +403,7 @@
         folded = total[:, 0:128]
         for c in range(1, width // 128):
             folded = folded + total[:, c * 128:(c + 1) * 128]
-        losses[r] = folded
+        losses[r:r + 1, :] = jnp.sum(folded, axis=0, keepdims=True)
 
 
 def solve(mesh_shape, plan, quarters, inverse, among, tall_a, tall_b, targets):
@@ -414,7 +414,7 @@
         out_shape=(
             jax.ShapeDtypeStruct((rows, width), jnp.float32),
             jax.ShapeDtypeStruct((rounds, size, width), jnp.bfloat16),
-            jax.ShapeDtypeStruct((rounds, 8, 128), jnp.float32),
+            jax.ShapeDtypeStruct((rounds, 128), jnp.float32),
         ),
         in_specs=[SMEM] + [VMEM] * 9,
         out_specs=(VMEM, VMEM, VMEM),
@@ -480,7 +480,7 @@
     (a, b), (c, d) = trail.result
     residual, steps, partial = solve(
         mesh_shape, plan, (a, b, c, d), block_inverse, among, tall_a, tall_b, targets)
-    losses = jnp.sum(route.total(partial), axis=(1, 2)) / total
+    losses = jnp.sum(route.total(partial), axis=1) / total
     return residual, steps, losses
 
 

time: 125 us -> 125 us (level)
  starting transfers between devices: 36.2 us -> 33.6 us
  waiting for transfers between devices: 44.7 us -> 47 us
    ppermute x25, starting transfers between devices: 36.2 us -> 33.6 us  [swap(): lax.ppermute(x, AXES, [(i, i ^ 1 << bit_of(i)) for i in range(devices)])]
    ppermute x25, waiting for transfers between devices: 44.7 us -> 47 us  [swap(): lax.ppermute(x, AXES, [(i, i ^ 1 << bit_of(i)) for i in range(devices)])]
where the time goes in v5:
time: 125 us
  waiting for transfers between devices  47 us (38%)
  Pallas kernels  39.1 us (31%)
  starting transfers between devices  33.6 us (27%)
  other arithmetic  3.07 us (2%)
    ppermute x25, waiting for transfers between devices, swap(): lax.ppermute(x, AXES, [(i, i ^ 1 << bit_of(i)) for i in range(devices)])  47 us
    ppermute x25, starting transfers between devices, swap(): lax.ppermute(x, AXES, [(i, i ^ 1 << bit_of(i)) for i in range(devices)])  33.6 us
    pallas_call x1, Pallas kernels, solve(): pl.pallas_call(functools.partial(solve_kernel, mesh_shape), out_shape=(ja...  14.1 us
    pallas_call x2, Pallas kernels, tall_matrices(): pl.pallas_call(functools.partial(tall_kernel, norm_scale, scale), out_sha...  7.11 us
    pallas_call x1, Pallas kernels, among_matrices(): pl.pallas_call(functools.partial(among_kernel, mesh_shape, norm_scale, sc...  6.03 us
    pallas_call x1, Pallas kernels, pick_targets(): pl.pallas_call(functools.partial(pick_targets_kernel, mesh_shape), out_sh...  3.94 us
    pallas_call x1, Pallas kernels, pick_points(): pl.pallas_call(functools.partial(pick_points_kernel, mesh_shape), out_sha...  2.95 us
    pallas_call x1, Pallas kernels, point_norms(): pl.pallas_call(functools.partial(norms_kernel, scale), out_shape=jax.Shap...  2.61 us
  transfers between devices with their start and end apart: 25, of which 21 were waited for; matrix products, arithmetic and copies ran while one was open for 2% of the time, Pallas kernels for 16%

profile of v5, /device:TPU:0, one launch (start us, length us, event | category | flops | bytes accessed | tf_op | source)
XLA Modules:
  0.0 124.7 jit_solution(16302395224561245090)
XLA Ops:
  0.6 2.9 %pick_points.1 = (bf16[6,256,512]{2,1,0:T(8,128)(2,1)S(1)}, bf16[6,256,512]{2,1,0:T(8,128)(2,1)S(1)}) custom-call(s32[6]{0:T(128)} %plan.9, bf16[2048,512]{1,0:T(8,128)(2,1)} %points.6), custom_call_target="tpu_custom_call" | custom-call | tf_op jit(solution)/shard_map/pick_points/pallas_call | solution.py:173
  4.2 3.0 %collective-permute-done.recv = bf16[6,256,512]{2,1,0:T(8,128)(2,1)S(1)} collective-permute-done((bf16[6,256,512]{2,1,0:T(8,128)(2,1)S(1)}, bf16[6,256,512]{2,1,0:T(8,128)(2,1)S(1)}, u32[]{:S(2)}, u32[]{:S(2)}) %collective-permute-start) | collective-permute-done | bytes 1572896 | tf_op jit(solution)/shard_map/ppermute | solution.py:37
  7.2 1.7 %halve.2 = (bf16[6,128,512]{2,1,0:T(8,128)(2,1)}, bf16[6,128,512]{2,1,0:T(8,128)(2,1)S(1)}) custom-call(s32[6]{0:T(128)S(1)} %copy-done.5, bf16[6,256,512]{2,1,0:T(8,128)(2,1)S(1)} %get-tuple-element.40.mine, bf16[6,256,512]{2,1,0:T(8,128)(2,1)S(1)} %collective-permute-done.recv), custom_call_target="tpu_custom_call" | custom-call | tf_op jit(solution)/shard_map/halve/pallas_call | solution.py:208
  9.8 2.8 %collective-permute-start.2 = (bf16[6,128,512]{2,1,0:T(8,128)(2,1)}, bf16[6,128,512]{2,1,0:T(8,128)(2,1)S(1)}, u32[]{:S(2)}, u32[]{:S(2)}) collective-permute-start(bf16[6,128,512]{2,1,0:T(8,128)(2,1)} %get-tuple-element.47), channel_id=1, source_target_pairs={{0,1},{1,0},{2,3},{3,2},{4,5},{5,4},{6,7},{7,6},{8,24},{9,25},{10,... | collective-permute-start | bytes 2359304 | tf_op jit(solution)/shard_map/ppermute | solution.py:37
  12.6 3.9 %pick_targets.1 = (bf16[6,256,256]{2,1,0:T(8,128)(2,1)}, bf16[6,256,256]{2,1,0:T(8,128)(2,1)S(1)}) custom-call(s32[6]{0:T(128)} %plan.9, f32[2048,256]{1,0:T(8,128)} %refs_6_.1), custom_call_target="tpu_custom_call" | custom-call | tf_op jit(solution)/shard_map/pick_targets/pallas_call | solution.py:238
  16.7 6.1 %collective-permute-done.2.recv = bf16[6,128,512]{2,1,0:T(8,128)(2,1)S(1)} collective-permute-done((bf16[6,128,512]{2,1,0:T(8,128)(2,1)}, bf16[6,128,512]{2,1,0:T(8,128)(2,1)S(1)}, u32[]{:S(2)}, u32[]{:S(2)}) %collective-permute-start.2) | collective-permute-done | bytes 786464 | tf_op jit(solution)/shard_map/ppermute | solution.py:37
  23.5 2.2 %collective-permute-start.4 = (bf16[6,64,512]{2,1,0:T(8,128)(2,1)S(1)}, bf16[6,64,512]{2,1,0:T(8,128)(2,1)S(1)}, u32[]{:S(2)}, u32[]{:S(2)}) collective-permute-start(bf16[6,64,512]{2,1,0:T(8,128)(2,1)S(1)} %get-tuple-element.49), channel_id=1, source_target_pairs={{0,2},{1,3},{2,0},{3,1},{4,6},{5,7},{6,4},{7,5},{8,9},{9,8},{10,11... | collective-permute-start | bytes 1179656 | tf_op jit(solution)/shard_map/ppermute | solution.py:37
  27.1 1.6 %collective-permute-start.3 = (bf16[6,128,256]{2,1,0:T(8,128)(2,1)S(1)}, bf16[6,128,256]{2,1,0:T(8,128)(2,1)S(1)}, u32[]{:S(2)}, u32[]{:S(2)}) collective-permute-start(bf16[6,128,256]{2,1,0:T(8,128)(2,1)S(1)} %get-tuple-element.50), channel_id=1, source_target_pairs={{0,1},{1,0},{2,3},{3,2},{4,5},{5,4},{6,7},{7,6},{8,24},{9,25},{10,... | collective-permute-start | bytes 1179656 | tf_op jit(solution)/shard_map/ppermute | solution.py:37
  28.7 2.6 %norms.1 = f32[2048,128]{1,0:T(8,128)} custom-call(bf16[2048,512]{1,0:T(8,128)(2,1)} %points.6), custom_call_target="tpu_custom_call" | custom-call | bytes 6291456 | tf_op jit(solution)/shard_map/norms/pallas_call | solution.py:264
  31.5 2.2 %collective-permute-start.6 = (bf16[6,32,512]{2,1,0:T(8,128)(2,1)S(1)}, bf16[6,32,512]{2,1,0:T(8,128)(2,1)S(1)}, u32[]{:S(2)}, u32[]{:S(2)}) collective-permute-start(bf16[6,32,512]{2,1,0:T(8,128)(2,1)S(1)} %dynamic-slice_select_fusion.2), channel_id=1, source_target_pairs={{0,16},{1,17},{2,18},{3,19},{4,20},{5,21},{6,22},{7,23},{8,10},{9,... | collective-permute-start | bytes 589832 | tf_op jit(solution)/shard_map/ppermute | solution.py:37
  37.6 3.0 %collective-permute-start.8 = (bf16[6,32,512]{2,1,0:T(8,128)(2,1)S(1)}, bf16[6,32,512]{2,1,0:T(8,128)(2,1)S(1)}, u32[]{:S(2)}, u32[]{:S(2)}) collective-permute-start(bf16[6,32,512]{2,1,0:T(8,128)(2,1)S(1)} %select_select_fusion), channel_id=1, source_target_pairs={{0,4},{1,5},{2,6},{3,7},{4,0},{5,1},{6,2},{7,3},{8,12},{9,13},{10,... | collective-permute-start | bytes 589832 | tf_op jit(solution)/shard_map/ppermute | solution.py:37
  40.5 4.5 %collective-permute-done.5 = bf16[6,64,256]{2,1,0:T(8,128)(2,1)S(1)} collective-permute-done((bf16[6,64,256]{2,1,0:T(8,128)(2,1)S(1)}, bf16[6,64,256]{2,1,0:T(8,128)(2,1)S(1)}, u32[]{:S(2)}, u32[]{:S(2)}) %collective-permute-start.5) | collective-permute-done | bytes 196640 | tf_op jit(solution)/shard_map/ppermute | solution.py:37
  45.1 2.9 %collective-permute-start.7 = (bf16[6,32,256]{2,1,0:T(8,128)(2,1)S(1)}, bf16[6,32,256]{2,1,0:T(8,128)(2,1)S(1)}, u32[]{:S(2)}, u32[]{:S(2)}) collective-permute-start(bf16[6,32,256]{2,1,0:T(8,128)(2,1)S(1)} %dynamic-slice_select_fusion.5), channel_id=1, source_target_pairs={{0,16},{1,17},{2,18},{3,19},{4,20},{5,21},{6,22},{7,23},{8,10},{9,... | collective-permute-start | bytes 294920 | tf_op jit(solution)/shard_map/ppermute | solution.py:37
  48.4 2.2 %collective-permute-done.7 = bf16[6,32,256]{2,1,0:T(8,128)(2,1)S(1)} collective-permute-done((bf16[6,32,256]{2,1,0:T(8,128)(2,1)S(1)}, bf16[6,32,256]{2,1,0:T(8,128)(2,1)S(1)}, u32[]{:S(2)}, u32[]{:S(2)}) %collective-permute-start.7) | collective-permute-done | bytes 98336 | tf_op jit(solution)/shard_map/ppermute | solution.py:37
  50.7 3.3 %collective-permute-done.10 = bf16[6,32,512]{2,1,0:T(8,128)(2,1)S(1)} collective-permute-done((bf16[6,32,512]{2,1,0:T(8,128)(2,1)S(1)}, bf16[6,32,512]{2,1,0:T(8,128)(2,1)S(1)}, u32[]{:S(2)}, u32[]{:S(2)}) %collective-permute-start.10) | collective-permute-done | bytes 196640 | tf_op jit(solution)/shard_map/ppermute | solution.py:37
  54.7 3.1 %collective-permute-start.9 = (bf16[6,32,256]{2,1,0:T(8,128)(2,1)S(1)}, bf16[6,32,256]{2,1,0:T(8,128)(2,1)S(1)}, u32[]{:S(2)}, u32[]{:S(2)}) collective-permute-start(bf16[6,32,256]{2,1,0:T(8,128)(2,1)S(1)} %select_select_fusion.1), channel_id=1, source_target_pairs={{0,4},{1,5},{2,6},{3,7},{4,0},{5,1},{6,2},{7,3},{8,12},{9,13},{10,... | collective-permute-start | bytes 294920 | tf_op jit(solution)/shard_map/ppermute | solution.py:37
  57.7 4.3 %collective-permute-done.9 = bf16[6,32,256]{2,1,0:T(8,128)(2,1)S(1)} collective-permute-done((bf16[6,32,256]{2,1,0:T(8,128)(2,1)S(1)}, bf16[6,32,256]{2,1,0:T(8,128)(2,1)S(1)}, u32[]{:S(2)}, u32[]{:S(2)}) %collective-permute-start.9) | collective-permute-done | bytes 98336 | tf_op jit(solution)/shard_map/ppermute | solution.py:37
  62.2 1.6 %collective-permute-done.12 = bf16[6,64,512]{2,1,0:T(8,128)(2,1)S(1)} collective-permute-done((bf16[6,64,512]{2,1,0:T(8,128)(2,1)S(1)}, bf16[6,64,512]{2,1,0:T(8,128)(2,1)S(1)}, u32[]{:S(2)}, u32[]{:S(2)}) %collective-permute-start.12) | collective-permute-done | bytes 393248 | tf_op jit(solution)/shard_map/ppermute | solution.py:37
  65.6 3.0 %collective-permute-done.11 = bf16[6,32,256]{2,1,0:T(8,128)(2,1)S(1)} collective-permute-done((bf16[6,32,256]{2,1,0:T(8,128)(2,1)S(1)}, bf16[6,32,256]{2,1,0:T(8,128)(2,1)S(1)}, u32[]{:S(2)}, u32[]{:S(2)}) %collective-permute-start.11) | collective-permute-done | bytes 98336 | tf_op jit(solution)/shard_map/ppermute | solution.py:37
  68.6 3.0 %collective-permute-start.13 = (bf16[6,64,256]{2,1,0:T(8,128)(2,1)S(1)}, bf16[6,64,256]{2,1,0:T(8,128)(2,1)S(1)}, u32[]{:S(2)}, u32[]{:S(2)}) collective-permute-start(bf16[6,64,256]{2,1,0:T(8,128)(2,1)S(1)} %pad_maximum_fusion.3), channel_id=1, source_target_pairs={{0,2},{1,3},{2,0},{3,1},{4,6},{5,7},{6,4},{7,5},{8,9},{9,8},{10,11... | collective-permute-start | bytes 589832 | tf_op jit(solution)/shard_map/ppermute | solution.py:37
  71.6 3.6 %collective-permute-done.13 = bf16[6,64,256]{2,1,0:T(8,128)(2,1)S(1)} collective-permute-done((bf16[6,64,256]{2,1,0:T(8,128)(2,1)S(1)}, bf16[6,64,256]{2,1,0:T(8,128)(2,1)S(1)}, u32[]{:S(2)}, u32[]{:S(2)}) %collective-permute-start.13) | collective-permute-done | bytes 196640 | tf_op jit(solution)/shard_map/ppermute | solution.py:37
  75.3 3.6 %tall.2.refs_7_ = bf16[6,2048,256]{2,1,0:T(8,128)(2,1)S(1)} custom-call(bf16[6,128,512]{2,1,0:T(8,128)(2,1)S(1)} %pad_maximum_fusion.mine.refs_0_, bf16[6,128,512]{2,1,0:T(8,128)(2,1)S(1)} %collective-permute-done.15.other.refs_2_, bf16[2048,512]{1,0:T(8,128)(2,1)S(1)} %copy-done.1, f32[2048,128]{1,0:T(8,128)S(1)} %copy-done.2), custom_call_target="tpu_custom_call" | custom-call | flops 3221225472 | bytes 12582912 | tf_op jit(solution)/shard_map/tall/pallas_call | solution.py:295
  81.3 3.6 %tall.3.refs_8_ = bf16[6,2048,256]{2,1,0:T(8,128)(2,1)S(1)} custom-call(bf16[6,128,512]{2,1,0:T(8,128)(2,1)S(1)} %collective-permute-done.14.mine.refs_1_, bf16[6,128,512]{2,1,0:T(8,128)(2,1)S(1)} %collective-permute-done.18.other.refs_3_, bf16[2048,512]{1,0:T(8,128)(2,1)S(1)} %copy-done.1, f32[2048,128]{1,0:T(8,128)S(1)} %copy-done.2), custom_call_target="tpu_custom_call" | custom-call | flops 3221225472 | bytes 12582912 | tf_op jit(solution)/shard_map/tall/pallas_call | solution.py:295
  84.9 2.0 %collective-permute-done.16.refs_1_ = bf16[6,128,256]{2,1,0:T(8,128)(2,1)S(1)} collective-permute-done((bf16[6,128,256]{2,1,0:T(8,128)(2,1)S(1)}, bf16[6,128,256]{2,1,0:T(8,128)(2,1)S(1)}, u32[]{:S(2)}, u32[]{:S(2)}) %collective-permute-start.16) | collective-permute-done | bytes 393248 | tf_op jit(solution)/shard_map/ppermute | solution.py:37
  86.9 6.0 %among.1.refs_5_ = bf16[15,512,512]{2,1,0:T(8,128)(2,1)S(1)} custom-call(bf16[6,128,512]{2,1,0:T(8,128)(2,1)S(1)} %pad_maximum_fusion.mine.refs_0_, bf16[6,128,512]{2,1,0:T(8,128)(2,1)S(1)} %collective-permute-done.14.mine.refs_1_, bf16[6,128,512]{2,1,0:T(8,128)(2,1)S(1)} %collective-permute-done.15.other.refs_2_, ...), custom_call_target="tpu_custom_call" | custom-call | flops 4026531840 | bytes 15728640 | tf_op jit(solution)/shard_map/among/pallas_call | solution.py:335
  93.0 14.1 %solve.1 = (f32[2048,256]{1,0:T(8,128)}, bf16[6,512,256]{2,1,0:T(8,128)(2,1)}, f32[6,128]{1,0:T(8,128)S(1)}) custom-call(s32[6]{0:T(128)S(1)} %copy-done.6, bf16[6,128,256]{2,1,0:T(8,128)(2,1)S(1)} %pad_maximum_fusion.2.refs_0_, bf16[6,128,256]{2,1,0:T(8,128)(2,1)S(1)} %collective-permute-done.16.refs_1_, ...), custom_call_target="tpu_custom_call" | custom-call | tf_op jit(solution)/shard_map/solve/pallas_call | solution.py:412
  109.6 2.4 %collective-permute-done.21 = f32[6,128]{1,0:T(8,128)S(1)} collective-permute-done((f32[6,128]{1,0:T(8,128)S(1)}, f32[6,128]{1,0:T(8,128)S(1)}, u32[]{:S(2)}, u32[]{:S(2)}) %collective-permute-start.21) | collective-permute-done | bytes 3104 | tf_op jit(solution)/shard_map/ppermute | solution.py:37
  112.0 2.3 %collective-permute-start.22 = (f32[6,128]{1,0:T(8,128)S(1)}, f32[6,128]{1,0:T(8,128)S(1)}, u32[]{:S(2)}, u32[]{:S(2)}) collective-permute-start(f32[6,128]{1,0:T(8,128)S(1)} %add.55), channel_id=1, source_target_pairs={{0,2},{1,3},{2,0},{3,1},{4,6},{5,7},{6,4},{7,5},{8,10},{9,11},{10,... | collective-permute-start | bytes 9224 | tf_op jit(solution)/shard_map/ppermute | solution.py:37
  114.3 1.6 %collective-permute-done.22 = f32[6,128]{1,0:T(8,128)S(1)} collective-permute-done((f32[6,128]{1,0:T(8,128)S(1)}, f32[6,128]{1,0:T(8,128)S(1)}, u32[]{:S(2)}, u32[]{:S(2)}) %collective-permute-start.22) | collective-permute-done | bytes 3104 | tf_op jit(solution)/shard_map/ppermute | solution.py:37
  117.1 2.5 %collective-permute-done.23 = f32[6,128]{1,0:T(8,128)S(1)} collective-permute-done((f32[6,128]{1,0:T(8,128)S(1)}, f32[6,128]{1,0:T(8,128)S(1)}, u32[]{:S(2)}, u32[]{:S(2)}) %collective-permute-start.23) | collective-permute-done | bytes 3104 | tf_op jit(solution)/shard_map/ppermute | solution.py:37
  119.5 2.2 %collective-permute-start.24 = (f32[6,128]{1,0:T(8,128)S(1)}, f32[6,128]{1,0:T(8,128)S(1)}, u32[]{:S(2)}, u32[]{:S(2)}) collective-permute-start(f32[6,128]{1,0:T(8,128)S(1)} %add.57), channel_id=1, source_target_pairs={{0,4},{1,5},{2,6},{3,7},{4,0},{5,1},{6,2},{7,3},{8,12},{9,13},{10,... | collective-permute-start | bytes 9224 | tf_op jit(solution)/shard_map/ppermute | solution.py:37
  121.7 2.3 %collective-permute-done.24 = f32[6,128]{1,0:T(8,128)S(1)} collective-permute-done((f32[6,128]{1,0:T(8,128)S(1)}, f32[6,128]{1,0:T(8,128)S(1)}, u32[]{:S(2)}, u32[]{:S(2)}) %collective-permute-start.24) | collective-permute-done | bytes 3104 | tf_op jit(solution)/shard_map/ppermute | solution.py:37
  (66 shorter events, 17.7 us)
Async XLA Ops:
  3.6 3.6 %collective-permute-start = (bf16[6,256,512]{2,1,0:T(8,128)(2,1)S(1)}, bf16[6,256,512]{2,1,0:T(8,128)(2,1)S(1)}, u32[]{:S(2)}, u32[]{:S(2)}) collective-permute-start(bf16[6,256,512]{2,1,0:T(8,128)(2,1)S(1)} %get-tuple-element.41), channel_id=1, source_target_pairs={{0,8},{1,9},{2,10},{3,11},{4,12},{5,13},{6,14},{7,15},{8,0},{9,1},... | collective-permute-start | bytes 4718600 | tf_op jit(solution)/shard_map/ppermute | solution.py:37
  9.7 6.9 %copy-start.6 = (s32[6]{0:T(128)S(1)}, s32[6]{0:T(128)}, u32[]{:S(2)}) copy-start(s32[6]{0:T(128)} %plan.9) | copy-start | bytes 76
  9.8 13.0 %copy-start.4 = (bf16[6,128,512]{2,1,0:T(8,128)(2,1)S(1)}, bf16[6,128,512]{2,1,0:T(8,128)(2,1)}, u32[]{:S(2)}) copy-start(bf16[6,128,512]{2,1,0:T(8,128)(2,1)} %copy-done.3) | copy-start | bytes 2359300
  9.8 13.0 %collective-permute-start.2 = (bf16[6,128,512]{2,1,0:T(8,128)(2,1)}, bf16[6,128,512]{2,1,0:T(8,128)(2,1)S(1)}, u32[]{:S(2)}, u32[]{:S(2)}) collective-permute-start(bf16[6,128,512]{2,1,0:T(8,128)(2,1)} %get-tuple-element.47), channel_id=1, source_target_pairs={{0,1},{1,0},{2,3},{3,2},{4,5},{5,4},{6,7},{7,6},{8,24},{9,25},{10,... | collective-permute-start | bytes 2359304 | tf_op jit(solution)/shard_map/ppermute | solution.py:37
  16.5 9.1 %collective-permute-start.1 = (bf16[6,256,256]{2,1,0:T(8,128)(2,1)}, bf16[6,256,256]{2,1,0:T(8,128)(2,1)}, u32[]{:S(2)}, u32[]{:S(2)}) collective-permute-start(bf16[6,256,256]{2,1,0:T(8,128)(2,1)} %get-tuple-element.45), channel_id=1, source_target_pairs={{0,8},{1,9},{2,10},{3,11},{4,12},{5,13},{6,14},{7,15},{8,0},{9,1},... | collective-permute-start | bytes 2359304 | tf_op jit(solution)/shard_map/ppermute | solution.py:37
  23.5 7.9 %collective-permute-start.4 = (bf16[6,64,512]{2,1,0:T(8,128)(2,1)S(1)}, bf16[6,64,512]{2,1,0:T(8,128)(2,1)S(1)}, u32[]{:S(2)}, u32[]{:S(2)}) collective-permute-start(bf16[6,64,512]{2,1,0:T(8,128)(2,1)S(1)} %get-tuple-element.49), channel_id=1, source_target_pairs={{0,2},{1,3},{2,0},{3,1},{4,6},{5,7},{6,4},{7,5},{8,9},{9,8},{10,11... | collective-permute-start | bytes 1179656 | tf_op jit(solution)/shard_map/ppermute | solution.py:37
  27.1 7.8 %collective-permute-start.3 = (bf16[6,128,256]{2,1,0:T(8,128)(2,1)S(1)}, bf16[6,128,256]{2,1,0:T(8,128)(2,1)S(1)}, u32[]{:S(2)}, u32[]{:S(2)}) collective-permute-start(bf16[6,128,256]{2,1,0:T(8,128)(2,1)S(1)} %get-tuple-element.50), channel_id=1, source_target_pairs={{0,1},{1,0},{2,3},{3,2},{4,5},{5,4},{6,7},{7,6},{8,24},{9,25},{10,... | collective-permute-start | bytes 1179656 | tf_op jit(solution)/shard_map/ppermute | solution.py:37
  31.5 5.9 %collective-permute-start.6 = (bf16[6,32,512]{2,1,0:T(8,128)(2,1)S(1)}, bf16[6,32,512]{2,1,0:T(8,128)(2,1)S(1)}, u32[]{:S(2)}, u32[]{:S(2)}) collective-permute-start(bf16[6,32,512]{2,1,0:T(8,128)(2,1)S(1)} %dynamic-slice_select_fusion.2), channel_id=1, source_target_pairs={{0,16},{1,17},{2,18},{3,19},{4,20},{5,21},{6,22},{7,23},{8,10},{9,... | collective-permute-start | bytes 589832 | tf_op jit(solution)/shard_map/ppermute | solution.py:37
  35.1 9.9 %collective-permute-start.5 = (bf16[6,64,256]{2,1,0:T(8,128)(2,1)S(1)}, bf16[6,64,256]{2,1,0:T(8,128)(2,1)S(1)}, u32[]{:S(2)}, u32[]{:S(2)}) collective-permute-start(bf16[6,64,256]{2,1,0:T(8,128)(2,1)S(1)} %get-tuple-element.55), channel_id=1, source_target_pairs={{0,2},{1,3},{2,0},{3,1},{4,6},{5,7},{6,4},{7,5},{8,9},{9,8},{10,11... | collective-permute-start | bytes 589832 | tf_op jit(solution)/shard_map/ppermute | solution.py:37
  37.6 10.7 %collective-permute-start.8 = (bf16[6,32,512]{2,1,0:T(8,128)(2,1)S(1)}, bf16[6,32,512]{2,1,0:T(8,128)(2,1)S(1)}, u32[]{:S(2)}, u32[]{:S(2)}) collective-permute-start(bf16[6,32,512]{2,1,0:T(8,128)(2,1)S(1)} %select_select_fusion), channel_id=1, source_target_pairs={{0,4},{1,5},{2,6},{3,7},{4,0},{5,1},{6,2},{7,3},{8,12},{9,13},{10,... | collective-permute-start | bytes 589832 | tf_op jit(solution)/shard_map/ppermute | solution.py:37
  45.1 5.5 %collective-permute-start.7 = (bf16[6,32,256]{2,1,0:T(8,128)(2,1)S(1)}, bf16[6,32,256]{2,1,0:T(8,128)(2,1)S(1)}, u32[]{:S(2)}, u32[]{:S(2)}) collective-permute-start(bf16[6,32,256]{2,1,0:T(8,128)(2,1)S(1)} %dynamic-slice_select_fusion.5), channel_id=1, source_target_pairs={{0,16},{1,17},{2,18},{3,19},{4,20},{5,21},{6,22},{7,23},{8,10},{9,... | collective-permute-start | bytes 294920 | tf_op jit(solution)/shard_map/ppermute | solution.py:37
  48.3 5.7 %collective-permute-start.10 = (bf16[6,32,512]{2,1,0:T(8,128)(2,1)S(1)}, bf16[6,32,512]{2,1,0:T(8,128)(2,1)S(1)}, u32[]{:S(2)}, u32[]{:S(2)}) collective-permute-start(bf16[6,32,512]{2,1,0:T(8,128)(2,1)S(1)} %broadcast_select_fusion), channel_id=1, source_target_pairs={{0,16},{1,17},{2,18},{3,19},{4,20},{5,21},{6,22},{7,23},{8,10},{9,... | collective-permute-start | bytes 589832 | tf_op jit(solution)/shard_map/ppermute | solution.py:37
  54.1 21.2 %copy-start.2 = (f32[2048,128]{1,0:T(8,128)S(1)}, f32[2048,128]{1,0:T(8,128)}, u32[]{:S(2)}) copy-start(f32[2048,128]{1,0:T(8,128)} %norms.1) | copy-start | bytes 3145732
  54.1 21.2 %copy-start.1 = (bf16[2048,512]{1,0:T(8,128)(2,1)S(1)}, bf16[2048,512]{1,0:T(8,128)(2,1)}, u32[]{:S(2)}) copy-start(bf16[2048,512]{1,0:T(8,128)(2,1)} %points.6) | copy-start | bytes 6291460
  54.1 9.7 %collective-permute-start.12 = (bf16[6,64,512]{2,1,0:T(8,128)(2,1)S(1)}, bf16[6,64,512]{2,1,0:T(8,128)(2,1)S(1)}, u32[]{:S(2)}, u32[]{:S(2)}) collective-permute-start(bf16[6,64,512]{2,1,0:T(8,128)(2,1)S(1)} %pad_maximum_fusion.1), channel_id=1, source_target_pairs={{0,2},{1,3},{2,0},{3,1},{4,6},{5,7},{6,4},{7,5},{8,9},{9,8},{10,11... | collective-permute-start | bytes 1179656 | tf_op jit(solution)/shard_map/ppermute | solution.py:37
  54.7 7.4 %collective-permute-start.9 = (bf16[6,32,256]{2,1,0:T(8,128)(2,1)S(1)}, bf16[6,32,256]{2,1,0:T(8,128)(2,1)S(1)}, u32[]{:S(2)}, u32[]{:S(2)}) collective-permute-start(bf16[6,32,256]{2,1,0:T(8,128)(2,1)S(1)} %select_select_fusion.1), channel_id=1, source_target_pairs={{0,4},{1,5},{2,6},{3,7},{4,0},{5,1},{6,2},{7,3},{8,12},{9,13},{10,... | collective-permute-start | bytes 294920 | tf_op jit(solution)/shard_map/ppermute | solution.py:37
  63.8 11.4 %collective-permute-start.15 = (bf16[6,128,512]{2,1,0:T(8,128)(2,1)S(1)}, bf16[6,128,512]{2,1,0:T(8,128)(2,1)S(1)}, u32[]{:S(2)}, u32[]{:S(2)}) collective-permute-start(bf16[6,128,512]{2,1,0:T(8,128)(2,1)S(1)} %pad_maximum_fusion.mine.refs_0_), channel_id=1, source_target_pairs={{0,8},{1,9},{2,10},{3,11},{4,12},{5,13},{6,14},{7,15},{8,0},{9,1},... | collective-permute-start | bytes 2359304 | tf_op jit(solution)/shard_map/ppermute | solution.py:37
  63.9 4.7 %collective-permute-start.11 = (bf16[6,32,256]{2,1,0:T(8,128)(2,1)S(1)}, bf16[6,32,256]{2,1,0:T(8,128)(2,1)S(1)}, u32[]{:S(2)}, u32[]{:S(2)}) collective-permute-start(bf16[6,32,256]{2,1,0:T(8,128)(2,1)S(1)} %broadcast_select_fusion.1), channel_id=1, source_target_pairs={{0,16},{1,17},{2,18},{3,19},{4,20},{5,21},{6,22},{7,23},{8,10},{9,... | collective-permute-start | bytes 294920 | tf_op jit(solution)/shard_map/ppermute | solution.py:37
  64.9 14.1 %collective-permute-start.14 = (bf16[6,128,512]{2,1,0:T(8,128)(2,1)S(1)}, bf16[6,128,512]{2,1,0:T(8,128)(2,1)S(1)}, u32[]{:S(2)}, u32[]{:S(2)}) collective-permute-start(bf16[6,128,512]{2,1,0:T(8,128)(2,1)S(1)} %pad_maximum_fusion.mine.refs_0_), channel_id=1, source_target_pairs={{0,1},{1,0},{2,3},{3,2},{4,5},{5,4},{6,7},{7,6},{8,24},{9,25},{10,... | collective-permute-start | bytes 2359304 | tf_op jit(solution)/shard_map/ppermute | solution.py:37
  68.6 6.6 %collective-permute-start.13 = (bf16[6,64,256]{2,1,0:T(8,128)(2,1)S(1)}, bf16[6,64,256]{2,1,0:T(8,128)(2,1)S(1)}, u32[]{:S(2)}, u32[]{:S(2)}) collective-permute-start(bf16[6,64,256]{2,1,0:T(8,128)(2,1)S(1)} %pad_maximum_fusion.3), channel_id=1, source_target_pairs={{0,2},{1,3},{2,0},{3,1},{4,6},{5,7},{6,4},{7,5},{8,9},{9,8},{10,11... | collective-permute-start | bytes 589832 | tf_op jit(solution)/shard_map/ppermute | solution.py:37
  79.0 2.3 %collective-permute-start.18 = (bf16[6,128,512]{2,1,0:T(8,128)(2,1)S(1)}, bf16[6,128,512]{2,1,0:T(8,128)(2,1)S(1)}, u32[]{:S(2)}, u32[]{:S(2)}) collective-permute-start(bf16[6,128,512]{2,1,0:T(8,128)(2,1)S(1)} %collective-permute-done.14.mine.refs_1_), channel_id=1, source_target_pairs={{0,8},{1,9},{2,10},{3,11},{4,12},{5,13},{6,14},{7,15},{8,0},{9,1},... | collective-permute-start | bytes 2359304 | tf_op jit(solution)/shard_map/ppermute | solution.py:37
  79.1 7.8 %collective-permute-start.16 = (bf16[6,128,256]{2,1,0:T(8,128)(2,1)S(1)}, bf16[6,128,256]{2,1,0:T(8,128)(2,1)S(1)}, u32[]{:S(2)}, u32[]{:S(2)}) collective-permute-start(bf16[6,128,256]{2,1,0:T(8,128)(2,1)S(1)} %pad_maximum_fusion.2.refs_0_), channel_id=1, source_target_pairs={{0,1},{1,0},{2,3},{3,2},{4,5},{5,4},{6,7},{7,6},{8,24},{9,25},{10,... | collective-permute-start | bytes 1179656 | tf_op jit(solution)/shard_map/ppermute | solution.py:37
  80.3 12.7 %collective-permute-start.17 = (bf16[6,128,256]{2,1,0:T(8,128)(2,1)S(1)}, bf16[6,128,256]{2,1,0:T(8,128)(2,1)S(1)}, u32[]{:S(2)}, u32[]{:S(2)}) collective-permute-start(bf16[6,128,256]{2,1,0:T(8,128)(2,1)S(1)} %pad_maximum_fusion.2.refs_0_), channel_id=1, source_target_pairs={{0,8},{1,9},{2,10},{3,11},{4,12},{5,13},{6,14},{7,15},{8,0},{9,1},... | collective-permute-start | bytes 1179656 | tf_op jit(solution)/shard_map/ppermute | solution.py:37
  81.3 11.6 %slice-start = ((s8[6291456]{0:T(1024)(128)(4,1)}), s8[4194304]{0:T(1024)(128)(4,1)S(1)}, s32[]{:S(2)}) async-start(s8[6291456]{0:T(1024)(128)(4,1)} %bitcast), calls=%async_computation | async-start | bytes 8388608
  84.9 8.1 %copy-start = (f32[2048,256]{1,0:T(8,128)S(1)}, f32[2048,256]{1,0:T(8,128)}, u32[]{:S(2)}) copy-start(f32[2048,256]{1,0:T(8,128)} %refs_6_.1) | copy-start | bytes 6291460
  84.9 8.1 %slice-start.1 = ((s8[6291456]{0:T(1024)(128)(4,1)}), s8[2097152]{0:T(1024)(128)(4,1)S(1)}, s32[]{:S(2)}) async-start(s8[6291456]{0:T(1024)(128)(4,1)} %bitcast), calls=%async_computation.1 | async-start | bytes 4194304
  86.9 6.1 %collective-permute-start.19 = (bf16[6,128,256]{2,1,0:T(8,128)(2,1)S(1)}, bf16[6,128,256]{2,1,0:T(8,128)(2,1)S(1)}, u32[]{:S(2)}, u32[]{:S(2)}) collective-permute-start(bf16[6,128,256]{2,1,0:T(8,128)(2,1)S(1)} %collective-permute-done.16.refs_1_), channel_id=1, source_target_pairs={{0,8},{1,9},{2,10},{3,11},{4,12},{5,13},{6,14},{7,15},{8,0},{9,1},... | collective-permute-start | bytes 1179656 | tf_op jit(solution)/shard_map/ppermute | solution.py:37
  107.1 1.3 %collective-permute-start.20 = (f32[6,128]{1,0:T(8,128)S(1)}, f32[6,128]{1,0:T(8,128)S(1)}, u32[]{:S(2)}, u32[]{:S(2)}) collective-permute-start(f32[6,128]{1,0:T(8,128)S(1)} %get-tuple-element.76), channel_id=1, source_target_pairs={{0,8},{1,9},{2,10},{3,11},{4,12},{5,13},{6,14},{7,15},{8,0},{9,1},... | collective-permute-start | bytes 9224 | tf_op jit(solution)/shard_map/ppermute | solution.py:37
  108.4 3.6 %collective-permute-start.21 = (f32[6,128]{1,0:T(8,128)S(1)}, f32[6,128]{1,0:T(8,128)S(1)}, u32[]{:S(2)}, u32[]{:S(2)}) collective-permute-start(f32[6,128]{1,0:T(8,128)S(1)} %add.54), channel_id=1, source_target_pairs={{0,1},{1,0},{2,3},{3,2},{4,5},{5,4},{6,7},{7,6},{8,9},{9,8},{10,11... | collective-permute-start | bytes 9224 | tf_op jit(solution)/shard_map/ppermute | solution.py:37
  112.0 3.9 %collective-permute-start.22 = (f32[6,128]{1,0:T(8,128)S(1)}, f32[6,128]{1,0:T(8,128)S(1)}, u32[]{:S(2)}, u32[]{:S(2)}) collective-permute-start(f32[6,128]{1,0:T(8,128)S(1)} %add.55), channel_id=1, source_target_pairs={{0,2},{1,3},{2,0},{3,1},{4,6},{5,7},{6,4},{7,5},{8,10},{9,11},{10,... | collective-permute-start | bytes 9224 | tf_op jit(solution)/shard_map/ppermute | solution.py:37
  115.9 3.6 %collective-permute-start.23 = (f32[6,128]{1,0:T(8,128)S(1)}, f32[6,128]{1,0:T(8,128)S(1)}, u32[]{:S(2)}, u32[]{:S(2)}) collective-permute-start(f32[6,128]{1,0:T(8,128)S(1)} %add.56), channel_id=1, source_target_pairs={{0,16},{1,17},{2,18},{3,19},{4,20},{5,21},{6,22},{7,23},{8,24},{9,... | collective-permute-start | bytes 9224 | tf_op jit(solution)/shard_map/ppermute | solution.py:37
  119.5 4.5 %collective-permute-start.24 = (f32[6,128]{1,0:T(8,128)S(1)}, f32[6,128]{1,0:T(8,128)S(1)}, u32[]{:S(2)}, u32[]{:S(2)}) collective-permute-start(f32[6,128]{1,0:T(8,128)S(1)} %add.57), channel_id=1, source_target_pairs={{0,4},{1,5},{2,6},{3,7},{4,0},{5,1},{6,2},{7,3},{8,12},{9,13},{10,... | collective-permute-start | bytes 9224 | tf_op jit(solution)/shard_map/ppermute | solution.py:37
  (2 other events, 7.5 us)
